TPU v7x, 32 devices: a whole 2x2x4 slice. The times are simulated.
32 devices in a mesh: groups: 2 (over y), ctx: 4 (over z), head: 4 (over x, core).
Axes of the slice: x: 2, y: 2, z: 4, core: 2. Of those that a mesh axis runs over, the one named last changes fastest.
Arguments:
- query_raw: bfloat16 [8192, 2048], P(('groups', 'ctx'), 'head'), parts along dimension 0, may hold values from -6 to 6
- key_raw: bfloat16 [8192, 2048], P(('groups', 'ctx'), 'head'), parts along dimension 0, may hold values from -6 to 6
- value_raw: bfloat16 [8192, 4096], P(('groups', 'ctx'), 'head'), parts along dimension 0, may hold values from -6 to 6
- conv_query: bfloat16 [4, 2048], P(None, 'head'), may hold values from -3 to 3
- conv_key: bfloat16 [4, 2048], P(None, 'head'), may hold values from -3 to 3
- conv_value: bfloat16 [4, 4096], P(None, 'head'), may hold values from -3 to 3
- gate_log: float32 [8192, 32], P(('groups', 'ctx'), 'head'), parts along dimension 0, may hold values from -0.8 to 0, as said below
- beta_logit: float32 [8192, 32], P(('groups', 'ctx'), 'head'), parts along dimension 0, may hold values from -8 to 2, as said below
- norm_gain: float32 [128], replicated, may hold values from 0.1 to 1.9
Outputs:
- attended: bfloat16 [8192, 4096], P(('groups', 'ctx'), 'head'), parts along dimension 0
There are 2 independent parts, one for each index of `groups`. A program takes and returns all parts, laid end to end along the dimension named above; an argument that names none is the same for every part. Nothing has to cross between parts.
Inputs may be any that keep to these rules, and one draw needn't show every extreme that they name: `gate_log`: decay logarithms are negative. `beta_logit`: write strengths are logits of numbers between 0 and 1.
All inputs are finite; a program needn't handle non-finite values.
Results may differ from a plain program's by a relative error of at most 0.012.
Values may be sent and summed in bfloat16 or wider, within the bound.
No kernel may reach another device: no remote copies, remote signals or barrier semaphores. Data moves between devices by JAX's collectives and lax.ppermute only.
A program may use at most 128 MiB of HBM per device.

v0:
```python
import jax
import jax.numpy as jnp
from jax import lax
from jax.sharding import PartitionSpec as P

DK = 128
DV = 128
KW = 4
SPAN = 64


EPSILON = 1e-06
EXACTNESS = lax.Precision.HIGHEST


def passed_along(value, axis, steps):
    count = lax.axis_size(axis)
    first, last = (max(0, -steps), min(count, count - steps))
    return lax.ppermute(value, axis, [(source, source + steps) for source in range(first, last)])


def conv_silu(values_in, prefix, kernel_function):
    padded = jnp.concatenate([prefix, values_in], axis=0)
    total = jnp.zeros(values_in.shape, jnp.float32)
    for start_offset in range(KW):
        total = total + padded[start_offset : start_offset + values_in.shape[0]].astype(
            jnp.float32
        ) * kernel_function[start_offset].astype(jnp.float32)
    return jax.nn.silu(total).astype(jnp.bfloat16)


def unit_rows(values):
    return values * lax.rsqrt(jnp.sum(values * values, axis=-1, keepdims=True) + EPSILON)


def lower_inverse(inner):
    power = -inner
    inverse = jnp.eye(SPAN, dtype=jnp.float32) + power
    for level in range(SPAN.bit_length() - 2):
        power = jnp.dot(power, power, precision=EXACTNESS)
        inverse = inverse + jnp.dot(inverse, power, precision=EXACTNESS)
    return inverse


def span_pieces(query, keys, values, gates, betas):
    cum_gate = jnp.cumsum(gates)
    row_ids = lax.broadcasted_iota(jnp.int32, (SPAN, SPAN), 0)
    col_ids = lax.broadcasted_iota(jnp.int32, (SPAN, SPAN), 1)
    lower = row_ids >= col_ids
    decays = jnp.where(
        lower, jnp.exp(jnp.where(lower, cum_gate[:, None] - cum_gate[None, :], 0.0)), 0.0
    )
    keys_wide = keys.astype(jnp.float32)
    query_wide = query.astype(jnp.float32)
    gram = jnp.dot(keys, keys.T, preferred_element_type=jnp.float32)
    inner = jnp.where(row_ids > col_ids, betas[:, None] * gram * decays, 0.0)
    key_beta = keys_wide * betas[:, None]
    right_side = jnp.concatenate(
        [key_beta * jnp.exp(cum_gate)[:, None], values * betas[:, None]], axis=1
    )
    solved = jnp.dot(lower_inverse(inner), right_side, precision=EXACTNESS)
    erase_rows = solved[:, : keys.shape[1]]
    write_rows = solved[:, keys.shape[1] :]
    scores = jnp.where(
        lower, jnp.dot(query, keys.T, preferred_element_type=jnp.float32) * decays, 0.0
    )
    query_dec = query_wide * jnp.exp(cum_gate)[:, None]
    key_dec = keys_wide * jnp.exp(cum_gate[-1] - cum_gate)[:, None]
    tail_decay = jnp.exp(cum_gate[-1])
    return (erase_rows, write_rows, scores, query_dec, key_dec, tail_decay)


def span_output(memory, pieces, gain):
    erase_rows, write_rows, scores, query_dec, key_dec, tail_decay = pieces
    corrected = write_rows - jnp.dot(erase_rows, memory, precision=EXACTNESS)
    output = jnp.dot(query_dec, memory, precision=EXACTNESS) + jnp.dot(
        scores, corrected, precision=EXACTNESS
    )
    memory = tail_decay * memory + jnp.dot(key_dec.T, corrected, precision=EXACTNESS)
    normed = output * lax.rsqrt(jnp.mean(output * output, axis=-1, keepdims=True) + EPSILON) * gain
    return (memory, normed.astype(jnp.bfloat16))


def matmul_heads(left, right):
    return jnp.einsum("hab,hbc->hac", left, right, precision=EXACTNESS)


def inner_heads(left, right):
    return jnp.einsum("hca,hcb->hab", left, right, precision=EXACTNESS)


def shards(
    query_raw, key_raw, value_raw, conv_query, conv_key, conv_value, gate_log, beta_logit, norm_gain
):
    tok_count = query_raw.shape[0]
    blocks = tok_count // SPAN
    kheads_dev = query_raw.shape[1] // DK
    vheads_dev = value_raw.shape[1] // DV
    ratio = vheads_dev // kheads_dev
    rim_start = tok_count - (KW - 1)
    rim_query, rim_key, rim_value = passed_along(
        (query_raw[rim_start:], key_raw[rim_start:], value_raw[rim_start:]), "ctx", 1
    )
    query_conv = conv_silu(query_raw, rim_query, conv_query)
    key_conv = conv_silu(key_raw, rim_key, conv_key)
    value_conv = conv_silu(value_raw, rim_value, conv_value)
    query_unit = (
        unit_rows(query_conv.astype(jnp.float32).reshape(tok_count, kheads_dev, DK)) * DK ** (-0.5)
    ).astype(jnp.bfloat16)
    key_unit = unit_rows(key_conv.astype(jnp.float32).reshape(tok_count, kheads_dev, DK)).astype(
        jnp.bfloat16
    )

    def by_block(values, heads, width, repeat):
        shaped = values.reshape(blocks, SPAN, heads, width)
        if repeat > 1:
            shaped = jnp.repeat(shaped, repeat, axis=2)
        return shaped.transpose(0, 2, 1, 3)

    inputs = (
        by_block(query_unit, kheads_dev, DK, ratio),
        by_block(key_unit, kheads_dev, DK, ratio),
        by_block(value_conv.astype(jnp.float32), vheads_dev, DV, 1),
        gate_log.reshape(blocks, SPAN, vheads_dev).transpose(0, 2, 1),
        jax.nn.sigmoid(beta_logit).reshape(blocks, SPAN, vheads_dev).transpose(0, 2, 1),
    )
    head_pieces = jax.vmap(span_pieces)
    source = jax.vmap(head_pieces)(inputs[0], inputs[1], inputs[2], inputs[3], inputs[4])
    identity = jnp.broadcast_to(jnp.eye(DK, dtype=jnp.float32), (vheads_dev, DK, DK))
    empty = jnp.zeros((vheads_dev, DK, DV), jnp.float32)

    def collect(carry, item):
        transit, memory = carry
        erase_rows, write_rows, scores, query_dec, key_dec, tail_decay = item
        corrected = write_rows - matmul_heads(erase_rows, memory)
        memory = tail_decay[:, None, None] * memory + inner_heads(key_dec, corrected)
        iteration_lookup = tail_decay[:, None, None] * identity - inner_heads(key_dec, erase_rows)
        transit = matmul_heads(iteration_lookup, transit)
        return ((transit, memory), None)

    transit, memory = lax.scan(collect, (identity, empty), source)[0]

    def relay_step(turn_index, incoming):
        outgoing_state = matmul_heads(transit, incoming) + memory
        return passed_along(outgoing_state, "ctx", 1)

    start = lax.fori_loop(0, lax.axis_size("ctx") - 1, relay_step, empty)
    per_head = jax.vmap(span_output, in_axes=(0, 0, None))

    def emit(carried, item):
        return per_head(carried, item, norm_gain)

    rows_out = lax.scan(emit, start, source)[1]
    return rows_out.transpose(0, 2, 1, 3).reshape(tok_count, vheads_dev * DV)


def solution(mesh):
    return jax.shard_map(
        shards,
        mesh=mesh,
        in_specs=(
            P(("groups", "ctx"), "head"),
            P(("groups", "ctx"), "head"),
            P(("groups", "ctx"), "head"),
            P(None, "head"),
            P(None, "head"),
            P(None, "head"),
            P(("groups", "ctx"), "head"),
            P(("groups", "ctx"), "head"),
            P(),
        ),
        out_specs=P(("groups", "ctx"), "head"),
        check_vma=False,
    )
```

profile of v0, /device:TPU:0, one launch (start us, length us, event | category | flops | bytes accessed | tf_op | source)
XLA Modules:
  0.0 427.0 jit_solution(5447946747590145646)
XLA Ops:
  0.7 4.9 %collective-permute-start.1 = (bf16[3,512]{1,0:T(4,128)(2,1)S(1)}, bf16[3,512]{1,0:T(4,128)(2,1)S(1)}, u32[]{:S(2)}, u32[]{:S(2)}) collective-permute-start(bf16[3,512]{1,0:T(4,128)(2,1)S(1)} %slice.83), channel_id=1, source_target_pairs={{0,4},{4,8},{8,12},{1,5},{5,9},{9,13},{2,6},{6,10},{10,14},{3,7},{... | collective-permute-start | bytes 9224 | tf_op jit(solution)/shard_map/ppermute | solution.py:19
  6.9 4.1 collective-permute-start.3
  12.3 2.9 collective-permute-start.2
  16.1 3.5 reduce_window_sum.11
  24.3 4.5 %fusion.74 = (f32[1024,512]{1,0:T(8,128)S(1)}, f32[1024,512]{1,0:T(8,128)}) fusion(f32[512]{0:T(512)S(1)} %bitcast.182, bf16[1024,512]{1,0:T(8,128)(2,1)} %param.16, f32[512]{0:T(512)S(1)} %bitcast.183, bf16[3,512]{1,0:T(4,128)(2,1)S(1)} %collective-permute-done.1, f32[512]{0:T(512)S(1)} %bitcast.181, f32[512]{0:T(512)S(1)} %bitcast.180), kind=kLoop, calls=%fused_computation.131 | loop fusion | flops 14155776 | bytes 5254144 | tf_op jit(solution)/shard_map/mul | solution.py:33
  30.5 2.8 reduce_sum.27
  38.9 8.4 %fusion.45 = f32[16,8,64,64]{3,2,1,0:T(8,128)S(1)} fusion(f32[16,8,64,64]{3,2,1,0:T(8,128)S(1)} %fusion.79, f32[16,8,64]{2,1,0:T(8,128)S(1)} %reduce_window_sum.11, f32[16,8,64]{2,1,0:T(8,128)S(1)} %bitcast.167, pred[64,64]{1,0:T(8,128)(4,1)S(1)} %copy-done.4, pred[64,64]{1,0:T(8,128)(4,1)S(1)} %copy-done.6), kind=kOutput, calls=%fused_computation.68 | convolution fusion | flops 406323200 | bytes 4268032 | tf_op jit(solution)/shard_map/vmap(vmap())/dot_general | solution.py:40
  47.3 5.0 %fusion.80 = f32[16,8,64,64]{3,2,1,0:T(8,128)S(1)} fusion(f32[16,8,64,64]{3,2,1,0:T(8,128)S(1)} %fusion.45), kind=kOutput, calls=%fused_computation.136 | convolution fusion | flops 402653184 | bytes 4194304 | tf_op jit(solution)/shard_map/vmap(vmap())/dot_general | solution.py:40
  52.4 7.7 %add_add_fusion = f32[16,8,64,64]{3,2,1,0:T(8,128)S(1)} fusion(f32[16,8,64,64]{3,2,1,0:T(8,128)S(1)} %fusion.45, f32[16,8,64,64]{3,2,1,0:T(8,128)S(1)} %fusion.79, f32[16,8,64]{2,1,0:T(8,128)S(1)} %reduce_window_sum.11, f32[16,8,64]{2,1,0:T(8,128)S(1)} %bitcast.168, f32[64,64]{1,0:T(8,128)S(1)} %fusion.68, pred[64,64]{1,0:T(8,128)(4,1)S(1)} %copy-done.4, ...), kind=kOutput, calls=%fused_computation.60 | convolution fusion | flops 411566080 | bytes 6381568 | tf_op jit(solution)/shard_map/vmap(vmap())/dot_general | solution.py:41
  60.0 5.1 %fusion.81 = f32[16,8,64,64]{3,2,1,0:T(8,128)S(1)} fusion(f32[16,8,64,64]{3,2,1,0:T(8,128)S(1)} %fusion.80), kind=kOutput, calls=%fused_computation.137 | convolution fusion | flops 402653184 | bytes 4194304 | tf_op jit(solution)/shard_map/vmap(vmap())/dot_general | solution.py:40
  65.1 4.8 %convolution_add_fusion.5 = f32[16,8,64,64]{3,2,1,0:T(8,128)S(1)} fusion(f32[16,8,64,64]{3,2,1,0:T(8,128)S(1)} %add_add_fusion, f32[16,8,64,64]{3,2,1,0:T(8,128)S(1)} %fusion.80), kind=kOutput, calls=%fused_computation.67 | convolution fusion | flops 403177472 | bytes 6291456 | tf_op jit(solution)/shard_map/vmap(vmap())/dot_general | solution.py:41
  70.0 4.9 %fusion.83 = f32[16,8,64,64]{3,2,1,0:T(8,128)S(1)} fusion(f32[16,8,64,64]{3,2,1,0:T(8,128)S(1)} %fusion.81), kind=kOutput, calls=%fused_computation.139 | convolution fusion | flops 402653184 | bytes 4194304 | tf_op jit(solution)/shard_map/vmap(vmap())/dot_general | solution.py:40
  74.8 4.7 %fusion.82 = f32[16,8,64,64]{3,2,1,0:T(8,128)S(1)} fusion(f32[16,8,64,64]{3,2,1,0:T(8,128)S(1)} %convolution_add_fusion.5, f32[16,8,64,64]{3,2,1,0:T(8,128)S(1)} %fusion.81), kind=kOutput, calls=%fused_computation.138 | convolution fusion | flops 402653184 | bytes 6291456 | tf_op jit(solution)/shard_map/vmap(vmap())/dot_general | solution.py:41
  79.6 6.0 %convolution_add_fusion.4 = f32[16,8,64,64]{3,2,1,0:T(8,128)} fusion(f32[16,8,64,64]{3,2,1,0:T(8,128)S(1)} %fusion.83, f32[16,8,64,64]{3,2,1,0:T(8,128)S(1)} %convolution_add_fusion.5, f32[16,8,64,64]{3,2,1,0:T(8,128)S(1)} %fusion.82), kind=kOutput, calls=%fused_computation.65 | convolution fusion | flops 403701760 | bytes 8388608 | tf_op jit(solution)/shard_map/vmap(vmap())/dot_general | solution.py:41
  85.6 5.7 %fusion.84 = f32[16,8,64,64]{3,2,1,0:T(8,128)} fusion(f32[16,8,64,64]{3,2,1,0:T(8,128)S(1)} %fusion.83), kind=kOutput, calls=%fused_computation.140 | convolution fusion | flops 402653184 | bytes 4194304 | tf_op jit(solution)/shard_map/vmap(vmap())/dot_general | solution.py:40
  91.2 3.5 fusion.72
  94.8 3.1 mul.365
  97.9 3.6 reduce_sum.28
  102.6 2.9 reshape.91
  105.5 2.6 multiply_convert_fusion.2
  108.4 7.4 %fusion.85 = f32[16,8,64,64]{3,2,1,0:T(8,128)} fusion(f32[16,8,64,64]{3,2,1,0:T(8,128)S(1)} %copy-done, f32[16,8,64,64]{3,2,1,0:T(8,128)} %fusion.84), kind=kOutput, calls=%fused_computation.141 | convolution fusion | flops 402653184 | bytes 6291456 | tf_op jit(solution)/shard_map/vmap(vmap())/dot_general | solution.py:41
  116.3 2.8 multiply_select_fusion
  119.1 2.8 convert_bitcast_fusion
  122.9 8.2 %fusion.38 = (f32[16,8,64,128]{3,2,1,0:T(8,128)}, f32[16,8,64,128]{3,2,1,0:T(8,128)}, f32[16,8,64,128]{3,2,1,0:T(8,128)}, f32[16,8,64,128]{3,2,1,0:T(8,128)}) fusion(bf16[16,8,64,128]{3,2,1,0:T(8,128)(2,1)S(1)} %bitcast.159, f32[16,8,64]{2,1,0:T(8,128)S(1)} %get-tuple-element.248, f32[16,8,64]{2,1,0:T(8,128)S(1)} %bitcast.169, ...), kind=kLoop, calls=%fused_computation.51 | loop fusion | flops 7340032 | bytes 25264128 | tf_op jit(solution)/shard_map/vmap(vmap())/mul | solution.py:59
  131.1 15.7 %fusion.34 = f32[16,8,64,256]{3,2,1,0:T(8,128)} fusion(f32[16,8,64,128]{3,2,1,0:T(8,128)} %get-tuple-element.247, f32[16,8,64,128]{3,2,1,0:T(8,128)} %get-tuple-element.244, f32[16,8,64,64]{3,2,1,0:T(8,128)S(1)} %copy-done, f32[16,8,64,64]{3,2,1,0:T(8,128)} %fusion.85), kind=kOutput, calls=%fused_computation.45 | convolution fusion | flops 1613234176 | bytes 20971520 | tf_op jit(solution)/shard_map/vmap(vmap())/dot_general | solution.py:61
  146.8 8.4 %fusion.76 = (f32[16,8,64,128]{3,2,1,0:T(8,128)}, f32[16,8,64,128]{3,2,1,0:T(8,128)}) fusion(f32[16,8,64,256]{3,2,1,0:T(8,128)} %fusion.34), kind=kLoop, calls=%fused_computation.132 | loop fusion | bytes 16777216 | tf_op jit(solution)/shard_map/vmap(vmap())/slice | solution.py:63
  155.2 104.0 %while.37 = (s32[]{:T(128)}, f32[8,128,128]{2,1,0:T(8,128)S(1)}, f32[8,128,128]{2,1,0:T(8,128)S(1)}, f32[16,8]{1,0:T(8,128)S(1)}, f32[16,8,64,128]{3,2,1,0:T(8,1...) while((s32[]{:T(128)}, f32[8,128,128]{2,1,0:T(8,128)S(1)}, ...), condition=%wide.region_3.4_spmd.clone, body=%wide.region_2.3_spmd.clone.sunk | while | flops 504168448 | bytes 6621940 | solution.py:141
  259.2 41.7 %while.35 = (s32[]{:T(128)}, f32[8,128,128]{2,1,0:T(8,128)S(1)}, f32[8,128,128]{2,1,0:T(8,128)S(1)}, f32[8,128,128]{2,1,0:T(8,128)S(1)}, s32[]{:T(128)}) while((s32[]{:T(128)}, f32[8,128,128]{2,1,0:T(8,128)S(1)}, f32[8,128,128]{2,1,0:T(8,128)S(1)}, f32[8,128,128]{2,1,0:T(8,128)S(1)}, s32[]{:T(128)}) %tuple.75), condition=%wide.region_5.6_spmd, body=%wide.region_4.5_spmd.sunk | while | flops 201457664 | bytes 4194405 | solution.py:147
  261.9 10.6 %collective-permute-done = f32[8,128,128]{2,1,0:T(8,128)S(1)} collective-permute-done((f32[8,128,128]{2,1,0:T(8,128)S(1)}, f32[8,128,128]{2,1,0:T(8,128)S(1)}, u32[]{:S(2)}, u32[]{:S(2)}) %collective-permute-start) | collective-permute-done | bytes 524320 | tf_op jit(solution)/shard_map/while/body/eval_jaxpr/ppermute | solution.py:19
  273.1 4.4 %collective-permute-start = (f32[8,128,128]{2,1,0:T(8,128)S(1)}, f32[8,128,128]{2,1,0:T(8,128)S(1)}, u32[]{:S(2)}, u32[]{:S(2)}) collective-permute-start(f32[8,128,128]{2,1,0:T(8,128)S(1)} %convolution_add_fusion.9), channel_id=1, source_target_pairs={{0,4},{4,8},{8,12},{1,5},{5,9},{9,13},{2,6},{6,10},{10,14},{3,7},{... | collective-permute-start | bytes 1572872 | tf_op jit(solution)/shard_map/while/body/eval_jaxpr/ppermute | solution.py:19
  277.5 9.6 %collective-permute-done = f32[8,128,128]{2,1,0:T(8,128)S(1)} collective-permute-done((f32[8,128,128]{2,1,0:T(8,128)S(1)}, f32[8,128,128]{2,1,0:T(8,128)S(1)}, u32[]{:S(2)}, u32[]{:S(2)}) %collective-permute-start) | collective-permute-done | bytes 524320 | tf_op jit(solution)/shard_map/while/body/eval_jaxpr/ppermute | solution.py:19
  287.8 4.4 %collective-permute-start = (f32[8,128,128]{2,1,0:T(8,128)S(1)}, f32[8,128,128]{2,1,0:T(8,128)S(1)}, u32[]{:S(2)}, u32[]{:S(2)}) collective-permute-start(f32[8,128,128]{2,1,0:T(8,128)S(1)} %convolution_add_fusion.9), channel_id=1, source_target_pairs={{0,4},{4,8},{8,12},{1,5},{5,9},{9,13},{2,6},{6,10},{10,14},{3,7},{... | collective-permute-start | bytes 1572872 | tf_op jit(solution)/shard_map/while/body/eval_jaxpr/ppermute | solution.py:19
  292.3 8.7 %collective-permute-done = f32[8,128,128]{2,1,0:T(8,128)S(1)} collective-permute-done((f32[8,128,128]{2,1,0:T(8,128)S(1)}, f32[8,128,128]{2,1,0:T(8,128)S(1)}, u32[]{:S(2)}, u32[]{:S(2)}) %collective-permute-start) | collective-permute-done | bytes 524320 | tf_op jit(solution)/shard_map/while/body/eval_jaxpr/ppermute | solution.py:19
  301.0 120.5 %while.36 = (s32[]{:T(128)}, f32[8,128,128]{2,1,0:T(8,128)S(1)}, bf16[16,8,64,128]{3,2,1,0:T(8,128)(2,1)}, f32[16,8]{1,0:T(8,128)S(1)}, f32[16,8,64,128]{3,2,1,0...) while((s32[]{:T(128)}, f32[8,128,128]{2,1,0:T(8,128)S(1)}, ...), condition=%wide.region_9.10_spmd, body=%wide.region_7.9_spmd.sunk | while | flops 353042944 | bytes 5385937 | solution.py:153
  306.4 2.1 convolution_add_fusion.10
  321.5 2.1 convolution_add_fusion.10
  329.0 2.1 convolution_add_fusion.10
  336.6 2.1 convolution_add_fusion.10
  351.6 2.1 convolution_add_fusion.10
  359.2 2.1 convolution_add_fusion.10
  366.7 2.1 convolution_add_fusion.10
  374.2 2.1 convolution_add_fusion.10
  381.8 2.1 convolution_add_fusion.10
  389.3 2.1 convolution_add_fusion.10
  396.8 2.1 convolution_add_fusion.10
  411.9 2.1 convolution_add_fusion.10
  419.4 2.1 convolution_add_fusion.10
  421.5 3.4 copy.28
  (252 shorter events, 220.8 us)
Async XLA Ops:
  0.7 23.6 %collective-permute-start.1 = (bf16[3,512]{1,0:T(4,128)(2,1)S(1)}, bf16[3,512]{1,0:T(4,128)(2,1)S(1)}, u32[]{:S(2)}, u32[]{:S(2)}) collective-permute-start(bf16[3,512]{1,0:T(4,128)(2,1)S(1)} %slice.83), channel_id=1, source_target_pairs={{0,4},{4,8},{8,12},{1,5},{5,9},{9,13},{2,6},{6,10},{10,14},{3,7},{... | collective-permute-start | bytes 9224 | tf_op jit(solution)/shard_map/ppermute | solution.py:19
  6.9 84.3 %collective-permute-start.3 = (bf16[3,512]{1,0:T(4,128)(2,1)}, bf16[3,512]{1,0:T(4,128)(2,1)}, u32[]{:S(2)}, u32[]{:S(2)}) collective-permute-start(bf16[3,512]{1,0:T(4,128)(2,1)} %slice.101), channel_id=1, source_target_pairs={{0,4},{4,8},{8,12},{1,5},{5,9},{9,13},{2,6},{6,10},{10,14},{3,7},{... | collective-permute-start | bytes 9224 | tf_op jit(solution)/shard_map/ppermute | solution.py:19
  12.3 106.8 %collective-permute-start.2 = (bf16[3,1024]{1,0:T(4,128)(2,1)}, bf16[3,1024]{1,0:T(4,128)(2,1)S(1)}, u32[]{:S(2)}, u32[]{:S(2)}) collective-permute-start(bf16[3,1024]{1,0:T(4,128)(2,1)} %slice.91), channel_id=1, source_target_pairs={{0,4},{4,8},{8,12},{1,5},{5,9},{9,13},{2,6},{6,10},{10,14},{3,7},{... | collective-permute-start | bytes 18440 | tf_op jit(solution)/shard_map/ppermute | solution.py:19
  37.7 1.2 copy-start.4
  37.7 1.2 copy-start.6
  85.6 5.7 %copy-start.2 = (bf16[1024,512]{1,0:T(8,128)(2,1)S(1)}, bf16[1024,512]{1,0:T(8,128)(2,1)}, u32[]{:S(2)}) copy-start(bf16[1024,512]{1,0:T(8,128)(2,1)} %param.15) | copy-start | bytes 3145732
  105.5 2.9 copy-start
  108.4 7.9 %copy-start.5 = (pred[64,64]{1,0:T(8,128)(4,1)S(1)}, pred[64,64]{1,0:T(8,128)(4,1)}, u32[]{:S(2)}) copy-start(pred[64,64]{1,0:T(8,128)(4,1)} %get-tuple-element.262) | copy-start | bytes 12292
  116.3 2.8 copy-start.1
  259.2 41.7 %copy-start.3 = (f32[128]{0:T(128)S(1)}, f32[128]{0:T(128)}, u32[]{:S(2)}) copy-start(f32[128]{0:T(128)} %param.23) | copy-start | bytes 1540
  259.9 12.5 %collective-permute-start = (f32[8,128,128]{2,1,0:T(8,128)S(1)}, f32[8,128,128]{2,1,0:T(8,128)S(1)}, u32[]{:S(2)}, u32[]{:S(2)}) collective-permute-start(f32[8,128,128]{2,1,0:T(8,128)S(1)} %convolution_add_fusion.9), channel_id=1, source_target_pairs={{0,4},{4,8},{8,12},{1,5},{5,9},{9,13},{2,6},{6,10},{10,14},{3,7},{... | collective-permute-start | bytes 1572872 | tf_op jit(solution)/shard_map/while/body/eval_jaxpr/ppermute | solution.py:19
  273.1 14.1 %collective-permute-start = (f32[8,128,128]{2,1,0:T(8,128)S(1)}, f32[8,128,128]{2,1,0:T(8,128)S(1)}, u32[]{:S(2)}, u32[]{:S(2)}) collective-permute-start(f32[8,128,128]{2,1,0:T(8,128)S(1)} %convolution_add_fusion.9), channel_id=1, source_target_pairs={{0,4},{4,8},{8,12},{1,5},{5,9},{9,13},{2,6},{6,10},{10,14},{3,7},{... | collective-permute-start | bytes 1572872 | tf_op jit(solution)/shard_map/while/body/eval_jaxpr/ppermute | solution.py:19
  287.8 13.2 %collective-permute-start = (f32[8,128,128]{2,1,0:T(8,128)S(1)}, f32[8,128,128]{2,1,0:T(8,128)S(1)}, u32[]{:S(2)}, u32[]{:S(2)}) collective-permute-start(f32[8,128,128]{2,1,0:T(8,128)S(1)} %convolution_add_fusion.9), channel_id=1, source_target_pairs={{0,4},{4,8},{8,12},{1,5},{5,9},{9,13},{2,6},{6,10},{10,14},{3,7},{... | collective-permute-start | bytes 1572872 | tf_op jit(solution)/shard_map/while/body/eval_jaxpr/ppermute | solution.py:19
where the time goes:
time: 434 us; the launch traced here: 427 us
  matrix products  290 us (67%)
  other arithmetic  51.1 us (12%)
  local copies, waits for them, and re-layouts  31.6 us (7%)
  waiting for transfers between devices  28.9 us (7%)
  starting transfers between devices  22.7 us (5%)
    dot_general x32, matrix products, inner_heads(): return jnp.einsum('hca,hcb->hab', left, right, precision=EXACTNESS)  65.5 us
    dot_general x35, matrix products, matmul_heads(): return jnp.einsum('hab,hbc->hac', left, right, precision=EXACTNESS)  38.5 us
    dot_general x16, matrix products, span_output(): jnp.dot(key_dec.T, corrected, precision=EXACTNESS)  32.8 us
    dot_general x5, matrix products, lower_inverse(): inverse = inverse + jnp.dot(inverse, power, precision=EXACTNESS)  30.6 us
    dot_general x5, matrix products, lower_inverse(): power = jnp.dot(power, power, precision=EXACTNESS)  29 us
    ppermute x6, waiting for transfers between devices, passed_along(): lax.ppermute(value, axis, [(source, source + steps) for source in range(f...  28.9 us
    dot_general x16, matrix products, span_output(): corrected = write_rows - jnp.dot(erase_rows, memory, precision=EXACTNESS)  26 us
    dot_general x16, matrix products, span_output(): jnp.dot(query_dec, memory, precision=EXACTNESS)  24.7 us
  transfers between devices with their start and end apart: 6, of which 3 were waited for; matrix products, arithmetic and copies ran while one was open for 25% of the time, Pallas kernels for 0%

commit v1 on v0

v1 whole, which is shorter than its diff:
```python
import jax
import jax.numpy as jnp
from jax import lax
from jax.experimental import pallas as pl
from jax.experimental.pallas import tpu as pltpu
from jax.sharding import PartitionSpec as P

DK = 128
DV = 128
KW = 4
CHUNK = 128
GROUP = 2
HALO = 8
RIM = 16
BASE = 16
EPSILON = 1e-06
F32 = jnp.float32
BF16 = jnp.bfloat16


def passed_along(value, axis):
    count = lax.axis_size(axis)
    return lax.ppermute(value, axis, [(source, source + 1) for source in range(count - 1)])


def dot(left, right):
    return jnp.dot(left, right, preferred_element_type=F32)


def diagonal_mask(size):
    rows = lax.broadcasted_iota(jnp.int32, (2 * CHUNK, 2 * CHUNK), 0)
    cols = lax.broadcasted_iota(jnp.int32, (2 * CHUNK, 2 * CHUNK), 1)
    return rows // size == cols // size


def odd_mask(size):
    rows = lax.broadcasted_iota(jnp.int32, (2 * CHUNK, 2 * CHUNK), 0)
    cols = lax.broadcasted_iota(jnp.int32, (2 * CHUNK, 2 * CHUNK), 1)
    return (rows // (2 * size) == cols // (2 * size)) & ((rows // size) % 2 == 1)


def levels():
    sizes = []
    size = BASE
    while size < CHUNK:
        sizes.append(size)
        size *= 2
    return sizes


def spread(strip, mask):
    count = 2 * CHUNK // strip.shape[0]
    return jnp.concatenate([strip] * count, axis=0) * mask


def inverses(negs, diag_ref, odd_ref):
    sizes = levels()
    lanes = lax.broadcasted_iota(jnp.int32, (1, 2 * CHUNK), 1) % CHUNK

    def strips(neg, size, step, first):
        out = neg[first : first + size]
        for turn in range(1, CHUNK // step):
            start = turn * step + first
            out = jnp.where(lanes // step == turn, neg[start : start + size], out)
        return out

    rows = lax.broadcasted_iota(jnp.int32, (BASE, 2 * CHUNK), 0)
    cols = lax.broadcasted_iota(jnp.int32, (BASE, 2 * CHUNK), 1)
    unit = (rows == cols % BASE).astype(F32)
    powers = [strips(neg, BASE, BASE, 0) for neg in negs]
    found = [unit + power for power in powers]
    shorts = [power.astype(BF16) for power in powers]
    weights = [spread(short, diag_ref[0]) for short in shorts]
    shorts = [dot(short, weight).astype(BF16) for short, weight in zip(shorts, weights)]
    reach = 2
    while reach < BASE:
        weights = [spread(short, diag_ref[0]) for short in shorts]
        last = 2 * reach >= BASE
        if last:
            found = [f + dot(f.astype(BF16), w) for f, w in zip(found, weights)]
        else:
            both = [
                dot(jnp.concatenate([s, f.astype(BF16)], axis=0), w)
                for s, f, w in zip(shorts, found, weights)
            ]
            shorts = [b[:BASE].astype(BF16) for b in both]
            found = [f + b[BASE:] for f, b in zip(found, both)]
        reach *= 2
    for place, size in enumerate(sizes):
        even = (lanes // size) % 2 == 0
        shorts = [f.astype(BF16) for f in found]
        lowers = [
            jnp.where(even, strips(neg, size, 2 * size, size), 0.0).astype(BF16) for neg in negs
        ]
        weights = [spread(short, diag_ref[place]) for short in shorts]
        halves = [dot(low, w).astype(BF16) for low, w in zip(lowers, weights)]
        weights = [spread(half, odd_ref[place]) for half in halves]
        corners = [dot(short, w) for short, w in zip(shorts, weights)]
        found = [
            jnp.concatenate([jnp.where(even, f, 0.0), jnp.where(even, corner, f)], axis=0)
            for f, corner in zip(found, corners)
        ]
    return found


def local_kernel(
    kheads,
    vheads,
    query_ref,
    key_ref,
    value_ref,
    rim_ref,
    taps_ref,
    gate_ref,
    logit_ref,
    rows_ref,
    local_ref,
    transit_ref,
    memory_ref,
    wide,
    state,
    diag_ref,
    odd_ref,
):
    step = pl.program_id(0)
    ratio = vheads // kheads
    span = GROUP * CHUNK
    tiles = 2 * kheads + vheads
    sizes = levels()

    @pl.when(step == 0)
    def _():
        for place, size in enumerate(sizes):
            diag_ref[place] = diagonal_mask(size).astype(BF16)
            odd_ref[place] = odd_mask(size).astype(BF16)
        rows = lax.broadcasted_iota(jnp.int32, (DK, DK + DV), 0)
        cols = lax.broadcasted_iota(jnp.int32, (DK, DK + DV), 1)
        for head in range(vheads):
            state[head] = (rows == cols).astype(F32)
        rim = rim_ref[...].astype(F32)
        for tile in range(tiles):
            wide[tile, 0:HALO] = rim[RIM - HALO :, tile * 128 : (tile + 1) * 128]

    @pl.when(step > 0)
    def _():
        for tile in range(tiles):
            wide[tile, 0:HALO] = wide[tile, span : span + HALO]

    taps = taps_ref[...].astype(F32) * 0.5

    def conv(tile):
        if tile < kheads:
            raw = query_ref[:, tile * 128 : (tile + 1) * 128]
        elif tile < 2 * kheads:
            raw = key_ref[:, (tile - kheads) * 128 : (tile - kheads + 1) * 128]
        else:
            raw = value_ref[:, (tile - 2 * kheads) * 128 : (tile - 2 * kheads + 1) * 128]
        raw = raw.astype(F32)
        wide[tile, HALO : HALO + span] = raw
        tap = taps[:, tile * 128 : (tile + 1) * 128]
        total = raw * tap[KW - 1 : KW]
        for back in range(1, KW):
            total += wide[tile, HALO - back : HALO - back + span] * tap[KW - 1 - back : KW - back]
        return (total + total * jnp.tanh(total)).astype(BF16)

    def unit(values, factor):
        values = values.astype(F32)
        scale = lax.rsqrt(jnp.sum(values * values, axis=-1, keepdims=True) + EPSILON)
        if factor != 1.0:
            scale = scale * factor
        return (values * scale).astype(BF16)

    queries = [unit(conv(tile), DK**-0.5) for tile in range(kheads)]
    keys = [unit(conv(kheads + tile), 1.0) for tile in range(kheads)]
    values = [conv(2 * kheads + tile) for tile in range(vheads)]

    rows = lax.broadcasted_iota(jnp.int32, (CHUNK, CHUNK), 0)
    cols = lax.broadcasted_iota(jnp.int32, (CHUNK, CHUNK), 1)
    lower = rows >= cols
    strict = rows > cols
    triangle = lower.astype(F32)

    items = []
    for part in range(GROUP):
        here = slice(part * CHUNK, (part + 1) * CHUNK)
        cum = jnp.dot(
            triangle,
            gate_ref[here],
            precision=lax.Precision.HIGHEST,
            preferred_element_type=F32,
        )
        cum_flat = cum.T
        beta_flat = jax.nn.sigmoid(logit_ref[here]).T
        for khead in range(kheads):
            query = queries[khead][here]
            key = keys[khead][here]
            key_flat = key.T
            grams = dot(jnp.concatenate([key, query], axis=0), key_flat)
            for which in range(ratio):
                head = khead * ratio + which
                cum_col = cum[:, head : head + 1]
                cum_row = cum_flat[head : head + 1]
                beta_row = beta_flat[head : head + 1]
                last = cum_row[:, CHUNK - 1 :]
                decays = jnp.exp(jnp.where(lower, cum_col - cum_row, -jnp.inf)) * beta_row
                growth = jnp.exp(cum_col)
                items.append(
                    dict(
                        part=part,
                        head=head,
                        neg=jnp.where(strict, -grams[:CHUNK] * decays, 0.0),
                        scores=(grams[CHUNK:] * decays).astype(BF16),
                        tail_keys=(
                            key_flat.astype(F32) * (jnp.exp(last - cum_row) * beta_row)
                        ).astype(BF16),
                        grown_keys=(key.astype(F32) * growth).astype(BF16),
                        grown_query=query.astype(F32) * growth,
                        tail=jnp.exp(last),
                    )
                )
    negs = [
        jnp.concatenate([items[i]["neg"], items[i + 1]["neg"]], axis=1)
        for i in range(0, len(items), 2)
    ]
    found = inverses(negs, diag_ref, odd_ref)
    for place, item in enumerate(items):
        side = place % 2
        part, head = item["part"], item["head"]
        here = slice(part * CHUNK, (part + 1) * CHUNK)
        inverse = found[place // 2][:, side * CHUNK : (side + 1) * CHUNK].astype(BF16)
        right = jnp.concatenate([item["grown_keys"], values[head][here]], axis=1)
        solved = dot(inverse, right).astype(BF16)
        product = dot(jnp.concatenate([item["tail_keys"], item["scores"]], axis=0), solved)
        item["erase"] = product[:CHUNK, :DK].astype(BF16)
        item["write"] = product[:CHUNK, DK:]
        item["meet"] = (item["grown_query"] - product[CHUNK:, :DK]).astype(BF16)
        item["own"] = product[CHUNK:, DK:]
    for item in items:
        part, head = item["part"], item["head"]
        here = slice(part * CHUNK, (part + 1) * CHUNK)
        there = slice(head * DV, (head + 1) * DV)
        now = state[head]
        product = dot(jnp.concatenate([item["erase"], item["meet"]], axis=0), now.astype(BF16))
        after = item["tail"] * now - product[:CHUNK]
        state[head, :, :DK] = after[:, :DK]
        state[head, :, DK:] = after[:, DK:] + item["write"]
        rows_ref[here, there] = product[CHUNK:, :DK].astype(BF16)
        local_ref[here, there] = (product[CHUNK:, DK:] + item["own"]).astype(local_ref.dtype)

    @pl.when(step == pl.num_programs(0) - 1)
    def _():
        for head in range(vheads):
            transit_ref[head] = state[head, :, :DK].astype(BF16)
            memory_ref[head] = state[head, :, DK:]


def local_pass(query_raw, key_raw, value_raw, rim, taps, gate_log, beta_logit):
    tok_count = query_raw.shape[0]
    kheads = query_raw.shape[1] // DK
    vheads = value_raw.shape[1] // DV
    tiles = 2 * kheads + vheads
    span = GROUP * CHUNK
    count = len(levels())

    def along(width):
        return pl.BlockSpec((span, width), lambda i: (i, 0))

    def whole(*shape):
        return pl.BlockSpec(shape, lambda i: (0,) * len(shape))

    def kernel(*refs):
        local_kernel(kheads, vheads, *refs)

    return pl.pallas_call(
        kernel,
        grid=(tok_count // span,),
        in_specs=[
            along(kheads * DK),
            along(kheads * DK),
            along(vheads * DV),
            whole(RIM, tiles * 128),
            whole(KW, tiles * 128),
            along(vheads),
            along(vheads),
        ],
        out_specs=[
            along(vheads * DV),
            along(vheads * DV),
            whole(vheads, DK, DK),
            whole(vheads, DK, DV),
        ],
        out_shape=[
            jax.ShapeDtypeStruct((tok_count, vheads * DV), BF16),
            jax.ShapeDtypeStruct((tok_count, vheads * DV), BF16),
            jax.ShapeDtypeStruct((vheads, DK, DK), BF16),
            jax.ShapeDtypeStruct((vheads, DK, DV), F32),
        ],
        scratch_shapes=[
            pltpu.VMEM((tiles, span + HALO, 128), F32),
            pltpu.VMEM((vheads, DK, DK + DV), F32),
            pltpu.VMEM((count, 2 * CHUNK, 2 * CHUNK), BF16),
            pltpu.VMEM((count, 2 * CHUNK, 2 * CHUNK), BF16),
        ],
        compiler_params=pltpu.CompilerParams(vmem_limit_bytes=48 * 1024 * 1024),
        name="local_pass",
    )(query_raw, key_raw, value_raw, rim, taps, gate_log, beta_logit)


def final_kernel(vheads, rows_ref, local_ref, start_ref, gain_ref, out_ref):
    gain = gain_ref[...]
    for head in range(vheads):
        there = slice(head * DV, (head + 1) * DV)
        output = dot(rows_ref[:, there], start_ref[head]) + local_ref[:, there].astype(F32)
        mean = jnp.mean(output * output, axis=-1, keepdims=True)
        out_ref[:, there] = (output * lax.rsqrt(mean + EPSILON) * gain).astype(BF16)


def final_pass(rows, local, start, gain):
    tok_count = rows.shape[0]
    vheads = start.shape[0]
    span = 256

    def along(width):
        return pl.BlockSpec((span, width), lambda i: (i, 0))

    def kernel(*refs):
        final_kernel(vheads, *refs)

    return pl.pallas_call(
        kernel,
        grid=(tok_count // span,),
        in_specs=[
            along(vheads * DV),
            along(vheads * DV),
            pl.BlockSpec((vheads, DK, DV), lambda i: (0, 0, 0)),
            pl.BlockSpec((1, DV), lambda i: (0, 0)),
        ],
        out_specs=along(vheads * DV),
        out_shape=jax.ShapeDtypeStruct((tok_count, vheads * DV), BF16),
        compiler_params=pltpu.CompilerParams(vmem_limit_bytes=32 * 1024 * 1024),
        name="final_pass",
    )(rows, local, start, gain)


def shards(
    query_raw, key_raw, value_raw, conv_query, conv_key, conv_value, gate_log, beta_logit, norm_gain
):
    rim_start = query_raw.shape[0] - RIM
    rim = passed_along(
        jnp.concatenate([query_raw[rim_start:], key_raw[rim_start:], value_raw[rim_start:]], axis=1),
        "ctx",
    )
    taps = jnp.concatenate([conv_query, conv_key, conv_value], axis=1)
    rows, local, transit, memory = local_pass(
        query_raw, key_raw, value_raw, rim, taps, gate_log, beta_logit
    )
    start = passed_along(memory.astype(BF16), "ctx")
    for _ in range(lax.axis_size("ctx") - 2):
        moved = jnp.einsum("hab,hbc->hac", transit, start, preferred_element_type=F32) + memory
        start = passed_along(moved.astype(BF16), "ctx")
    return final_pass(rows, local, start, norm_gain.reshape(1, DV))


def solution(mesh):
    return jax.shard_map(
        shards,
        mesh=mesh,
        in_specs=(
            P(("groups", "ctx"), "head"),
            P(("groups", "ctx"), "head"),
            P(("groups", "ctx"), "head"),
            P(None, "head"),
            P(None, "head"),
            P(None, "head"),
            P(("groups", "ctx"), "head"),
            P(("groups", "ctx"), "head"),
            P(),
        ),
        out_specs=P(("groups", "ctx"), "head"),
        check_vma=False,
    )
```

time: 434 us -> 65.5 us (0.15); the launches traced: 427 us -> 64.9 us
  matrix products: 290 us -> 0.43 us
  other arithmetic: 51.1 us -> 0.78 us
  Pallas kernels: 0 us -> 27.4 us
  local copies, waits for them, and re-layouts: 31.6 us -> 5.43 us
  waiting for transfers between devices: 28.9 us -> 13.4 us
  starting transfers between devices: 22.7 us -> 17.4 us
    dot_general x144 -> x2, matrix products: 290 us -> 0.43 us  [shards(): jnp.einsum('hab,hbc->hac', transit, start, preferred_element_type=F32)]
    pallas_call x0 -> x2, Pallas kernels: none -> 27.4 us  [the longest x1 24.2 us: local_pass(): pl.pallas_call(kernel, grid=(tok_count // span,), in_specs=[along(kheads...]
    mul x6 -> x0, other arithmetic: 18.8 us -> none  [the longest x1 8.16 us: span_pieces(): key_beta * jnp.exp(cum_gate)[:, None]]
    ppermute x6 -> x4, waiting for transfers between devices: 28.9 us -> 13.4 us  [passed_along(): lax.ppermute(value, axis, [(source, source + 1) for source in range(count...]
    dynamic_update_slice x16 -> x0, other arithmetic: 12.7 us -> none  [shards(): rows_out = lax.scan(emit, start, source)[1]]
    slice x3 -> x0, local copies, waits for them, and re-layouts: 8.61 us -> none  [the longest x1 8.4 us: span_pieces(): write_rows = solved[:, keys.shape[1]:]]
    reduce_sum x2 -> x0, other arithmetic: 6.35 us -> none  [unit_rows(): jnp.sum(values * values, axis=-1, keepdims=True) + EPSILON]
    reshape x6 -> x0, local copies, waits for them, and re-layouts: 5.79 us -> none  [the longest x1 2.89 us: shards(): query_conv.astype(jnp.float32).reshape(tok_count, kheads_dev, DK)]
  transfers between devices with their start and end apart: 6 -> 4, of which waited for: 3 -> 3; matrix products, arithmetic and copies ran while one was open for 25% -> 4% of each run, Pallas kernels for 0% -> 0%
where the time goes in v1:
time: 65.5 us; the launch traced here: 64.9 us
  Pallas kernels  27.4 us (42%)
  starting transfers between devices  17.4 us (27%)
  waiting for transfers between devices  13.4 us (20%)
  local copies, waits for them, and re-layouts  5.43 us (8%)
  other arithmetic  0.78 us (1%)
    pallas_call x1, Pallas kernels, local_pass(): pl.pallas_call(kernel, grid=(tok_count // span,), in_specs=[along(kheads...  24.2 us
    ppermute x4, starting transfers between devices, passed_along(): lax.ppermute(value, axis, [(source, source + 1) for source in range(count...  17.4 us
    ppermute x4, waiting for transfers between devices, passed_along(): lax.ppermute(value, axis, [(source, source + 1) for source in range(count...  13.4 us
    pallas_call x1, Pallas kernels, final_pass(): pl.pallas_call(kernel, grid=(tok_count // span,), in_specs=[along(vheads...  3.15 us
    unnamed x10, local copies, waits for them, and re-layouts  3.14 us
  transfers between devices with their start and end apart: 4, of which 3 were waited for; matrix products, arithmetic and copies ran while one was open for 4% of the time, Pallas kernels for 0%

profile of v1, /device:TPU:0, one launch (start us, length us, event | category | flops | bytes accessed | tf_op | source)
XLA Modules:
  0.0 64.9 jit_solution(15373562326634015474)
XLA Ops:
  0.0 0.0 copy-start.1
  0.0 0.8 %slice.9 = bf16[16,512]{1,0:T(8,128)(2,1)S(1)} slice(bf16[1024,512]{1,0:T(8,128)(2,1)} %refs_0_.1), slice={[1008:1024], [0:512]} | slice | bytes 32768 | tf_op jit(solution)/shard_map/slice | solution.py:350
  0.8 0.7 %slice.10 = bf16[16,512]{1,0:T(8,128)(2,1)S(1)} slice(bf16[1024,512]{1,0:T(8,128)(2,1)} %refs_1_.1), slice={[1008:1024], [0:512]} | slice | bytes 32768 | tf_op jit(solution)/shard_map/slice | solution.py:350
  1.5 0.8 %slice.11 = bf16[16,1024]{1,0:T(8,128)(2,1)S(1)} slice(bf16[1024,1024]{1,0:T(8,128)(2,1)} %refs_2_.1), slice={[1008:1024], [0:1024]} | slice | bytes 65536 | tf_op jit(solution)/shard_map/slice | solution.py:350
  2.3 4.9 %collective-permute-start = (bf16[16,2048]{1,0:T(8,128)(2,1)S(1)}, bf16[16,2048]{1,0:T(8,128)(2,1)S(1)}, u32[]{:S(2)}, u32[]{:S(2)}) collective-permute-start(bf16[16,2048]{1,0:T(8,128)(2,1)S(1)} %pad_maximum_fusion), channel_id=1, source_target_pairs={{0,4},{4,8},{8,12},{1,5},{5,9},{9,13},{2,6},{6,10},{10,14},{3,7},{... | collective-permute-start | bytes 196616 | tf_op jit(solution)/shard_map/ppermute | solution.py:23
  7.2 0.7 %pad_maximum_fusion.1.refs_4_ = bf16[4,2048]{1,0:T(4,128)(2,1)S(1)} fusion(bf16[4,1024]{1,0:T(4,128)(2,1)} %param.14, bf16[4,512]{1,0:T(4,128)(2,1)} %param.13, bf16[4,512]{1,0:T(4,128)(2,1)} %param.12), kind=kLoop, calls=%fused_computation.5 | loop fusion | flops 49152 | bytes 32768 | tf_op jit(solution)/shard_map/concatenate | solution.py:353
  8.0 1.0 %copy.10.refs_5_ = f32[1024,8]{1,0:T(8,128)S(1)} copy(f32[1024,8]{0,1:T(8,128)} %param.15) | data formatting | bytes 65536 | tf_op args[6]
  8.9 1.0 %copy.11.refs_6_ = f32[1024,8]{1,0:T(8,128)S(1)} copy(f32[1024,8]{0,1:T(8,128)} %param.16) | data formatting | bytes 65536 | tf_op args[7]
  9.9 0.0 collective-permute-done.refs_3_
  9.9 0.0 copy-done.1
  9.9 0.0 copy-start.2
  9.9 1.2 %copy-done.2 = bf16[1024,512]{1,0:T(8,128)(2,1)S(1)} copy-done((bf16[1024,512]{1,0:T(8,128)(2,1)S(1)}, bf16[1024,512]{1,0:T(8,128)(2,1)}, u32[]{:S(2)}) %copy-start.2) | copy-done | bytes 1048600
  11.1 24.2 %local_pass.1 = (bf16[1024,1024]{1,0:T(8,128)(2,1)S(1)}, bf16[1024,1024]{1,0:T(8,128)(2,1)}, bf16[8,128,128]{2,1,0:T(8,128)(2,1)S(1)}, f32[8,128,128]{2,1,0:T(8,128)S(1)}) custom-call(bf16[1024,512]{1,0:T(8,128)(2,1)S(1)} %copy-done.1, bf16[1024,512]{1,0:T(8,128)(2,1)S(1)} %copy-done.2, bf16[1024,1024]{1,0:T(8,128)(2,1)} %refs_2_.1, ...), custom_call_target="tpu_custom_call" | custom-call | tf_op jit(solution)/shard_map/local_pass/pallas_call | solution.py:274
  35.4 0.0 copy-start
  35.4 0.0 copy-start.3
  35.4 3.6 %collective-permute-start.1 = (bf16[8,128,128]{2,1,0:T(8,128)(2,1)S(1)}, bf16[8,128,128]{2,1,0:T(8,128)(2,1)S(1)}, u32[]{:S(2)}, u32[]{:S(2)}) collective-permute-start(bf16[8,128,128]{2,1,0:T(8,128)(2,1)S(1)} %convert_element_type.9), channel_id=1, source_target_pairs={{0,4},{4,8},{8,12},{1,5},{5,9},{9,13},{2,6},{6,10},{10,14},{3,7},{... | collective-permute-start | bytes 786440 | tf_op jit(solution)/shard_map/ppermute | solution.py:23
  39.1 5.2 %collective-permute-done.1 = bf16[8,128,128]{2,1,0:T(8,128)(2,1)S(1)} collective-permute-done((bf16[8,128,128]{2,1,0:T(8,128)(2,1)S(1)}, bf16[8,128,128]{2,1,0:T(8,128)(2,1)S(1)}, u32[]{:S(2)}, u32[]{:S(2)}) %collective-permute-start.1) | collective-permute-done | bytes 262176 | tf_op jit(solution)/shard_map/ppermute | solution.py:23
  44.3 0.2 fusion
  44.5 4.4 %collective-permute-start.2 = (bf16[8,128,128]{2,1,0:T(8,128)(2,1)S(1)}, bf16[8,128,128]{2,1,0:T(8,128)(2,1)S(1)}, u32[]{:S(2)}, u32[]{:S(2)}) collective-permute-start(bf16[8,128,128]{2,1,0:T(8,128)(2,1)S(1)} %fusion), channel_id=1, source_target_pairs={{0,4},{4,8},{8,12},{1,5},{5,9},{9,13},{2,6},{6,10},{10,14},{3,7},{... | collective-permute-start | bytes 786440 | tf_op jit(solution)/shard_map/ppermute | solution.py:23
  49.0 4.3 %collective-permute-done.2 = bf16[8,128,128]{2,1,0:T(8,128)(2,1)S(1)} collective-permute-done((bf16[8,128,128]{2,1,0:T(8,128)(2,1)S(1)}, bf16[8,128,128]{2,1,0:T(8,128)(2,1)S(1)}, u32[]{:S(2)}, u32[]{:S(2)}) %collective-permute-start.2) | collective-permute-done | bytes 262176 | tf_op jit(solution)/shard_map/ppermute | solution.py:23
  53.3 0.2 fusion.1
  53.5 4.4 %collective-permute-start.3 = (bf16[8,128,128]{2,1,0:T(8,128)(2,1)S(1)}, bf16[8,128,128]{2,1,0:T(8,128)(2,1)S(1)}, u32[]{:S(2)}, u32[]{:S(2)}) collective-permute-start(bf16[8,128,128]{2,1,0:T(8,128)(2,1)S(1)} %fusion.1), channel_id=1, source_target_pairs={{0,4},{4,8},{8,12},{1,5},{5,9},{9,13},{2,6},{6,10},{10,14},{3,7},{... | collective-permute-start | bytes 786440 | tf_op jit(solution)/shard_map/ppermute | solution.py:23
  57.9 3.9 %collective-permute-done.3.refs_2_ = bf16[8,128,128]{2,1,0:T(8,128)(2,1)S(1)} collective-permute-done((bf16[8,128,128]{2,1,0:T(8,128)(2,1)S(1)}, bf16[8,128,128]{2,1,0:T(8,128)(2,1)S(1)}, u32[]{:S(2)}, u32[]{:S(2)}) %collective-permute-start.3) | collective-permute-done | bytes 262176 | tf_op jit(solution)/shard_map/ppermute | solution.py:23
  61.8 0.0 copy-done
  61.8 0.0 copy-done.3
  61.8 3.1 %final_pass.1 = bf16[1024,1024]{1,0:T(8,128)(2,1)} custom-call(bf16[1024,1024]{1,0:T(8,128)(2,1)S(1)} %get-tuple-element.9.refs_0_, bf16[1024,1024]{1,0:T(8,128)(2,1)S(1)} %copy-done, bf16[8,128,128]{2,1,0:T(8,128)(2,1)S(1)} %collective-permute-done.3.refs_2_, f32[1,128]{1,0:T(1,128)S(1)} %bitcast.5), custom_call_target="tpu_custom_call" | custom-call | tf_op jit(solution)/shard_map/final_pass/pallas_call | solution.py:329
  (2 shorter events, 0.0 us)
Async XLA Ops:
  0.0 9.9 %copy-start.1 = (bf16[1024,512]{1,0:T(8,128)(2,1)S(1)}, bf16[1024,512]{1,0:T(8,128)(2,1)}, u32[]{:S(2)}) copy-start(bf16[1024,512]{1,0:T(8,128)(2,1)} %refs_0_.1) | copy-start | bytes 3145732
  2.3 7.6 %collective-permute-start = (bf16[16,2048]{1,0:T(8,128)(2,1)S(1)}, bf16[16,2048]{1,0:T(8,128)(2,1)S(1)}, u32[]{:S(2)}, u32[]{:S(2)}) collective-permute-start(bf16[16,2048]{1,0:T(8,128)(2,1)S(1)} %pad_maximum_fusion), channel_id=1, source_target_pairs={{0,4},{4,8},{8,12},{1,5},{5,9},{9,13},{2,6},{6,10},{10,14},{3,7},{... | collective-permute-start | bytes 196616 | tf_op jit(solution)/shard_map/ppermute | solution.py:23
  9.9 1.2 %copy-start.2 = (bf16[1024,512]{1,0:T(8,128)(2,1)S(1)}, bf16[1024,512]{1,0:T(8,128)(2,1)}, u32[]{:S(2)}) copy-start(bf16[1024,512]{1,0:T(8,128)(2,1)} %refs_1_.1) | copy-start | bytes 3145732
  35.4 26.4 %copy-start = (bf16[1024,1024]{1,0:T(8,128)(2,1)S(1)}, bf16[1024,1024]{1,0:T(8,128)(2,1)}, u32[]{:S(2)}) copy-start(bf16[1024,1024]{1,0:T(8,128)(2,1)} %get-tuple-element.10.refs_1_) | copy-start | bytes 6291460
  35.4 26.4 %copy-start.3 = (f32[128]{0:T(128)S(1)}, f32[128]{0:T(128)}, u32[]{:S(2)}) copy-start(f32[128]{0:T(128)} %param.17) | copy-start | bytes 1540
  35.4 8.9 %collective-permute-start.1 = (bf16[8,128,128]{2,1,0:T(8,128)(2,1)S(1)}, bf16[8,128,128]{2,1,0:T(8,128)(2,1)S(1)}, u32[]{:S(2)}, u32[]{:S(2)}) collective-permute-start(bf16[8,128,128]{2,1,0:T(8,128)(2,1)S(1)} %convert_element_type.9), channel_id=1, source_target_pairs={{0,4},{4,8},{8,12},{1,5},{5,9},{9,13},{2,6},{6,10},{10,14},{3,7},{... | collective-permute-start | bytes 786440 | tf_op jit(solution)/shard_map/ppermute | solution.py:23
  44.5 8.7 %collective-permute-start.2 = (bf16[8,128,128]{2,1,0:T(8,128)(2,1)S(1)}, bf16[8,128,128]{2,1,0:T(8,128)(2,1)S(1)}, u32[]{:S(2)}, u32[]{:S(2)}) collective-permute-start(bf16[8,128,128]{2,1,0:T(8,128)(2,1)S(1)} %fusion), channel_id=1, source_target_pairs={{0,4},{4,8},{8,12},{1,5},{5,9},{9,13},{2,6},{6,10},{10,14},{3,7},{... | collective-permute-start | bytes 786440 | tf_op jit(solution)/shard_map/ppermute | solution.py:23
  53.5 8.3 %collective-permute-start.3 = (bf16[8,128,128]{2,1,0:T(8,128)(2,1)S(1)}, bf16[8,128,128]{2,1,0:T(8,128)(2,1)S(1)}, u32[]{:S(2)}, u32[]{:S(2)}) collective-permute-start(bf16[8,128,128]{2,1,0:T(8,128)(2,1)S(1)} %fusion.1), channel_id=1, source_target_pairs={{0,4},{4,8},{8,12},{1,5},{5,9},{9,13},{2,6},{6,10},{10,14},{3,7},{... | collective-permute-start | bytes 786440 | tf_op jit(solution)/shard_map/ppermute | solution.py:23

commit v2 on v1

v2 whole, which is shorter than its diff:
```python
import jax
import jax.numpy as jnp
from jax import lax
from jax.experimental import pallas as pl
from jax.experimental.pallas import tpu as pltpu
from jax.sharding import PartitionSpec as P

DK = 128
DV = 128
KW = 4
CHUNK = 128
HALF = 64
BASE = 16
HALO = 8
RIM = 16
PARTS = 2
SPAN_X = 512
SPAN_Y = 512
EPSILON = 1e-06
F32 = jnp.float32
BF16 = jnp.bfloat16
WIDE = DK + DV


def dot(left, right):
    return jnp.dot(left, right, preferred_element_type=F32)


def levels():
    sizes = []
    size = BASE
    while size < HALF:
        sizes.append(size)
        size *= 2
    return sizes


def iotas(shape):
    return lax.broadcasted_iota(jnp.int32, shape, 0), lax.broadcasted_iota(jnp.int32, shape, 1)


def fill_masks(diag_ref, odd_ref):
    rows, cols = iotas((CHUNK, CHUNK))
    for place, size in enumerate(levels()):
        diag_ref[place] = (rows // size == cols // size).astype(BF16)
        pair = rows // (2 * size) == cols // (2 * size)
        odd_ref[place] = (pair & ((rows // size) % 2 == 1)).astype(BF16)


def spread(strip, mask):
    count = CHUNK // strip.shape[0]
    return jnp.concatenate([strip] * count, axis=0) * mask


def half_inverses(negs, diag_ref, odd_ref):
    lanes = lax.broadcasted_iota(jnp.int32, (1, CHUNK), 1)

    def strips(neg, size, step, first):
        out = neg[first : first + size]
        for turn in range(1, CHUNK // step):
            start = turn * step + first
            out = jnp.where(lanes // step == turn, neg[start : start + size], out)
        return out

    rows, cols = iotas((BASE, CHUNK))
    unit = (rows == cols % BASE).astype(F32)
    powers = [strips(neg, BASE, BASE, 0) for neg in negs]
    found = [unit + power for power in powers]
    shorts = [power.astype(BF16) for power in powers]
    weights = [spread(short, diag_ref[0]) for short in shorts]
    shorts = [dot(short, weight).astype(BF16) for short, weight in zip(shorts, weights)]
    reach = 2
    while reach < BASE:
        weights = [spread(short, diag_ref[0]) for short in shorts]
        if 2 * reach >= BASE:
            found = [f + dot(f.astype(BF16), w) for f, w in zip(found, weights)]
        else:
            both = [
                dot(jnp.concatenate([s, f.astype(BF16)], axis=0), w)
                for s, f, w in zip(shorts, found, weights)
            ]
            shorts = [b[:BASE].astype(BF16) for b in both]
            found = [f + b[BASE:] for f, b in zip(found, both)]
        reach *= 2
    for place, size in enumerate(levels()):
        even = (lanes // size) % 2 == 0
        shorts = [f.astype(BF16) for f in found]
        lowers = [
            jnp.where(even, strips(neg, size, 2 * size, size), 0.0).astype(BF16) for neg in negs
        ]
        weights = [spread(short, diag_ref[place]) for short in shorts]
        middles = [dot(low, w).astype(BF16) for low, w in zip(lowers, weights)]
        weights = [spread(middle, odd_ref[place]) for middle in middles]
        corners = [dot(short, w) for short, w in zip(shorts, weights)]
        found = [
            jnp.concatenate([jnp.where(even, f, 0.0), jnp.where(even, corner, f)], axis=0)
            for f, corner in zip(found, corners)
        ]
    return [f.astype(BF16) for f in found]


def conv(raw, wide, tile, tap):
    span = raw.shape[0]
    raw = raw.astype(F32)
    wide[tile, HALO : HALO + span] = raw
    total = raw * tap[KW - 1 : KW]
    for back in range(1, KW):
        total += wide[tile, HALO - back : HALO - back + span] * tap[KW - 1 - back : KW - back]
    return (total + total * jnp.tanh(total)).astype(BF16)


def unit(values, factor):
    values = values.astype(F32)
    scale = lax.rsqrt(jnp.sum(values * values, axis=-1, keepdims=True) + EPSILON)
    if factor != 1.0:
        scale = scale * factor
    return (values * scale).astype(BF16)


def sums(gates, span):
    rows, cols = iotas((CHUNK, CHUNK))
    stacked = jnp.concatenate(
        [gates[:, at : at + CHUNK] for at in range(0, span, CHUNK)], axis=0
    )
    total = jnp.dot(
        stacked,
        (rows <= cols).astype(F32),
        precision=lax.Precision.HIGHEST,
        preferred_element_type=F32,
    )
    heads = gates.shape[0]
    return [total[at * heads : (at + 1) * heads] for at in range(span // CHUNK)]


def rim_kernel(query_ref, key_ref, value_ref, out_ref):
    first, second = query_ref.shape[1], key_ref.shape[1]
    out_ref[:, :first] = query_ref[...]
    out_ref[:, first : first + second] = key_ref[...]
    out_ref[:, first + second :] = value_ref[...]


def pack_rim(query_raw, key_raw, value_raw):
    last = query_raw.shape[0] // RIM - 1
    widths = [array.shape[1] for array in (query_raw, key_raw, value_raw)]
    return pl.pallas_call(
        rim_kernel,
        grid=(1,),
        in_specs=[pl.BlockSpec((RIM, width), lambda i: (last, 0)) for width in widths],
        out_specs=pl.BlockSpec((RIM, sum(widths)), lambda i: (0, 0)),
        out_shape=jax.ShapeDtypeStruct((RIM, sum(widths)), BF16),
        name="pack_rim",
    )(query_raw, key_raw, value_raw)


def memory_kernel(
    kheads,
    vheads,
    first_head,
    key_ref,
    value_ref,
    rim_key_ref,
    rim_value_ref,
    tap_key_ref,
    tap_value_ref,
    gate_ref,
    logit_ref,
    unit_ref,
    solved_ref,
    before_ref,
    transit_ref,
    memory_ref,
    wide,
    state,
    diag_ref,
    odd_ref,
):
    step = pl.program_id(0)
    ratio = vheads // kheads
    span = key_ref.shape[0]
    tiles = kheads + vheads

    @pl.when(step == 0)
    def _():
        fill_masks(diag_ref, odd_ref)
        rows, cols = iotas((DK, WIDE))
        for head in range(vheads):
            state[head] = (rows == cols).astype(F32)
        for tile in range(tiles):
            ref, at = (rim_key_ref, tile) if tile < kheads else (rim_value_ref, tile - kheads)
            wide[tile, 0:HALO] = ref[:, at * 128 : (at + 1) * 128].astype(F32)[RIM - HALO :]

    @pl.when(step > 0)
    def _():
        for tile in range(tiles):
            wide[tile, 0:HALO] = wide[tile, span : span + HALO]

    tap_key = tap_key_ref[...].astype(F32) * 0.5
    tap_value = tap_value_ref[...].astype(F32) * 0.5
    keys = []
    for tile in range(kheads):
        at = slice(tile * DK, (tile + 1) * DK)
        keys.append(unit(conv(key_ref[:, at], wide, tile, tap_key[:, at]), 1.0))
        unit_ref[:, at] = keys[tile]
    values = []
    for tile in range(vheads):
        at = slice(tile * DV, (tile + 1) * DV)
        values.append(conv(value_ref[:, at], wide, kheads + tile, tap_value[:, at]))

    rows, cols = iotas((CHUNK, CHUNK))
    strict = rows > cols
    cums = sums(gate_ref[...], span)
    betas = jax.nn.sigmoid(logit_ref[...])

    items = []
    for part in range(span // CHUNK):
        here = slice(part * CHUNK, (part + 1) * CHUNK)
        cum_flat = cums[part]
        cum = cum_flat.T
        for khead in range(kheads):
            key = keys[khead][here]
            key_flat = key.T
            gram = dot(key, key_flat)
            for which in range(ratio):
                head = khead * ratio + which
                place = first_head + head
                cum_col = cum[:, place : place + 1]
                cum_row = cum_flat[place : place + 1]
                beta_row = betas[place : place + 1, here]
                last = cum_row[:, CHUNK - 1 :]
                decays = jnp.exp(jnp.where(strict, cum_col - cum_row, -jnp.inf))
                items.append(
                    dict(
                        part=part,
                        head=head,
                        neg=(gram * decays) * -beta_row,
                        tail_keys=(
                            key_flat.astype(F32) * (jnp.exp(last - cum_row) * beta_row)
                        ).astype(BF16),
                        right=jnp.concatenate(
                            [
                                (key.astype(F32) * jnp.exp(cum_col)).astype(BF16),
                                values[head][here],
                            ],
                            axis=1,
                        ),
                        tail=jnp.exp(last),
                    )
                )
    found = half_inverses([item["neg"] for item in items], diag_ref, odd_ref)
    tops = [dot(f[:, :HALF], item["right"][:HALF]).astype(BF16) for f, item in zip(found, items)]
    rests = [
        (item["right"][HALF:].astype(F32) + dot(item["neg"][HALF:, :HALF].astype(BF16), top)).astype(
            BF16
        )
        for item, top in zip(items, tops)
    ]
    lows = [dot(f[:, HALF:], rest).astype(BF16) for f, rest in zip(found, rests)]
    for item, top, low in zip(items, tops, lows):
        start = item["part"] * CHUNK
        there = slice(item["head"] * WIDE, (item["head"] + 1) * WIDE)
        solved = jnp.concatenate([top, low], axis=0)
        solved_ref[start : start + CHUNK, there] = solved
        product = dot(item["tail_keys"], solved)
        item["erase"] = product[:, :DK].astype(BF16)
        item["write"] = product[:, DK:]
    for item in items:
        part, head = item["part"], item["head"]
        now = state[head]
        short = now.astype(BF16)
        before_ref[part, head] = short
        after = item["tail"] * now - dot(item["erase"], short)
        state[head, :, :DK] = after[:, :DK]
        state[head, :, DK:] = after[:, DK:] + item["write"]

    @pl.when(step == pl.num_programs(0) - 1)
    def _():
        for head in range(vheads):
            transit_ref[head] = state[head, :, :DK].astype(BF16)
            memory_ref[head] = state[head, :, DK:]


def memory_pass(part, key_raw, value_raw, rim, conv_key, conv_value, gate_flat, logit_flat):
    tok_count = key_raw.shape[0]
    all_kheads = key_raw.shape[1] // DK
    all_vheads = value_raw.shape[1] // DV
    kheads, vheads = all_kheads // PARTS, all_vheads // PARTS
    tiles = kheads + vheads
    span = min(SPAN_X, tok_count)
    chunks = tok_count // CHUNK
    count = len(levels())
    rim_key = PARTS + part
    rim_value = (2 * all_kheads) // vheads + part

    def along(width, column):
        return pl.BlockSpec((span, width), lambda i: (i, column))

    def fixed(shape, *place):
        return pl.BlockSpec(shape, lambda i: place)

    def kernel(*refs):
        memory_kernel(kheads, vheads, part * vheads, *refs)

    return pl.pallas_call(
        kernel,
        grid=(tok_count // span,),
        in_specs=[
            along(kheads * DK, part),
            along(vheads * DV, part),
            fixed((RIM, kheads * DK), 0, rim_key),
            fixed((RIM, vheads * DV), 0, rim_value),
            fixed((KW, kheads * DK), 0, part),
            fixed((KW, vheads * DV), 0, part),
            pl.BlockSpec((all_vheads, span), lambda i: (0, i)),
            pl.BlockSpec((all_vheads, span), lambda i: (0, i)),
        ],
        out_specs=[
            along(kheads * DK, 0),
            along(vheads * WIDE, 0),
            pl.BlockSpec((span // CHUNK, vheads, DK, WIDE), lambda i: (i, 0, 0, 0)),
            fixed((vheads, DK, DK), 0, 0, 0),
            fixed((vheads, DK, DV), 0, 0, 0),
        ],
        out_shape=[
            jax.ShapeDtypeStruct((tok_count, kheads * DK), BF16),
            jax.ShapeDtypeStruct((tok_count, vheads * WIDE), BF16),
            jax.ShapeDtypeStruct((chunks, vheads, DK, WIDE), BF16),
            jax.ShapeDtypeStruct((vheads, DK, DK), BF16),
            jax.ShapeDtypeStruct((vheads, DK, DV), F32),
        ],
        scratch_shapes=[
            pltpu.VMEM((tiles, span + HALO, 128), F32),
            pltpu.VMEM((vheads, DK, WIDE), F32),
            pltpu.VMEM((count, CHUNK, CHUNK), BF16),
            pltpu.VMEM((count, CHUNK, CHUNK), BF16),
        ],
        compiler_params=pltpu.CompilerParams(vmem_limit_bytes=40 * 1024 * 1024),
        cost_estimate=pl.CostEstimate(
            flops=2 * tok_count * vheads * 1000 * 1000, bytes_accessed=1 << 23, transcendentals=0
        ),
        name="memory_pass",
    )(key_raw, value_raw, rim, rim, conv_key, conv_value, gate_flat, logit_flat)


def rows_kernel(
    kheads,
    vheads,
    first_head,
    query_ref,
    rim_ref,
    tap_ref,
    key_ref,
    gate_ref,
    logit_ref,
    solved_ref,
    before_ref,
    rows_ref,
    local_ref,
    wide,
):
    step = pl.program_id(0)
    ratio = vheads // kheads
    span = query_ref.shape[0]

    @pl.when(step == 0)
    def _():
        for tile in range(kheads):
            wide[tile, 0:HALO] = rim_ref[:, tile * DK : (tile + 1) * DK].astype(F32)[RIM - HALO :]

    @pl.when(step > 0)
    def _():
        for tile in range(kheads):
            wide[tile, 0:HALO] = wide[tile, span : span + HALO]

    taps = tap_ref[...].astype(F32) * 0.5
    queries = []
    for tile in range(kheads):
        at = slice(tile * DK, (tile + 1) * DK)
        queries.append(unit(conv(query_ref[:, at], wide, tile, taps[:, at]), DK**-0.5))

    rows, cols = iotas((CHUNK, CHUNK))
    lower = rows >= cols
    cums = sums(gate_ref[...], span)
    betas = jax.nn.sigmoid(logit_ref[...])
    for part in range(span // CHUNK):
        here = slice(part * CHUNK, (part + 1) * CHUNK)
        cum_flat = cums[part]
        cum = cum_flat.T
        for khead in range(kheads):
            query = queries[khead][here]
            gram = lax.dot_general(
                query,
                key_ref[here, khead * DK : (khead + 1) * DK],
                (((1,), (1,)), ((), ())),
                preferred_element_type=F32,
            )
            for which in range(ratio):
                head = khead * ratio + which
                place = first_head + head
                there = slice(head * DV, (head + 1) * DV)
                cum_col = cum[:, place : place + 1]
                cum_row = cum_flat[place : place + 1]
                decays = jnp.exp(jnp.where(lower, cum_col - cum_row, -jnp.inf))
                scores = (gram * decays * betas[place : place + 1, here]).astype(BF16)
                product = dot(scores, solved_ref[here, head * WIDE : (head + 1) * WIDE])
                meet = query.astype(F32) * jnp.exp(cum_col) - product[:, :DK]
                final = dot(meet.astype(BF16), before_ref[part, head])
                rows_ref[here, there] = final[:, :DK].astype(BF16)
                local_ref[here, there] = (final[:, DK:] + product[:, DK:]).astype(BF16)


def rows_pass(part, query_raw, rim, conv_query, keys, gate_flat, logit_flat, solved, before):
    tok_count = query_raw.shape[0]
    kheads = query_raw.shape[1] // DK // PARTS
    all_vheads = gate_flat.shape[0]
    vheads = all_vheads // PARTS
    span = min(SPAN_Y, tok_count)

    def along(width, column):
        return pl.BlockSpec((span, width), lambda i: (i, column))

    def kernel(*refs):
        rows_kernel(kheads, vheads, part * vheads, *refs)

    return pl.pallas_call(
        kernel,
        grid=(tok_count // span,),
        in_specs=[
            along(kheads * DK, part),
            pl.BlockSpec((RIM, kheads * DK), lambda i: (0, part)),
            pl.BlockSpec((KW, kheads * DK), lambda i: (0, part)),
            along(kheads * DK, 0),
            pl.BlockSpec((all_vheads, span), lambda i: (0, i)),
            pl.BlockSpec((all_vheads, span), lambda i: (0, i)),
            along(vheads * WIDE, 0),
            pl.BlockSpec((span // CHUNK, vheads, DK, WIDE), lambda i: (i, 0, 0, 0)),
        ],
        out_specs=[along(vheads * DV, 0), along(vheads * DV, 0)],
        out_shape=[
            jax.ShapeDtypeStruct((tok_count, vheads * DV), BF16),
            jax.ShapeDtypeStruct((tok_count, vheads * DV), BF16),
        ],
        scratch_shapes=[pltpu.VMEM((kheads, span + HALO, 128), F32)],
        compiler_params=pltpu.CompilerParams(vmem_limit_bytes=32 * 1024 * 1024),
        cost_estimate=pl.CostEstimate(
            flops=2 * tok_count * vheads * 1000 * 500, bytes_accessed=1 << 23, transcendentals=0
        ),
        name="rows_pass",
    )(query_raw, rim, conv_query, keys, gate_flat, logit_flat, solved, before)


def final_kernel(vheads, rows_ref, local_ref, early_ref, late_ref, gain_ref, *rest):
    out_ref = rest[-1]
    gain = gain_ref[...]
    for head in range(vheads):
        there = slice(head * DV, (head + 1) * DV)
        start = early_ref[head] + late_ref[head]
        output = dot(rows_ref[:, there], start) + local_ref[:, there].astype(F32)
        mean = jnp.mean(output * output, axis=-1, keepdims=True)
        out_ref[:, there] = (output * lax.rsqrt(mean + EPSILON) * gain).astype(BF16)


def final_pass(part, rows, local, early, late, gain, earlier):
    tok_count = rows.shape[0]
    vheads = early.shape[0]
    span = min(256, tok_count)

    def along(width, column):
        return pl.BlockSpec((span, width), lambda i: (i, column))

    def kernel(*refs):
        final_kernel(vheads, *refs)

    whole = pl.BlockSpec((vheads, DK, DV), lambda i: (0, 0, 0))
    arrays = [rows, local, early, late, gain]
    specs = [
        along(vheads * DV, 0),
        along(vheads * DV, 0),
        whole,
        whole,
        pl.BlockSpec((1, DV), lambda i: (0, 0)),
    ]
    if earlier is not None:
        arrays.append(earlier)
        specs.append(pl.BlockSpec(memory_space=pl.ANY))
    return pl.pallas_call(
        kernel,
        grid=(tok_count // span,),
        in_specs=specs,
        out_specs=along(vheads * DV, part),
        out_shape=jax.ShapeDtypeStruct((tok_count, PARTS * vheads * DV), BF16),
        input_output_aliases={} if earlier is None else {5: 0},
        compiler_params=pltpu.CompilerParams(vmem_limit_bytes=32 * 1024 * 1024),
        name="final_pass",
    )(*arrays)


def shards(
    query_raw, key_raw, value_raw, conv_query, conv_key, conv_value, gate_log, beta_logit, norm_gain
):
    count = lax.axis_size("ctx")
    rim = lax.ppermute(
        pack_rim(query_raw, key_raw, value_raw), "ctx", [(at, at + 1) for at in range(count - 1)]
    )
    gate_flat, logit_flat = gate_log.T, beta_logit.T
    gain = norm_gain.reshape(1, DV)
    first = [
        memory_pass(part, key_raw, value_raw, rim, conv_key, conv_value, gate_flat, logit_flat)
        for part in range(PARTS)
    ]
    second, early, late = [], [], []
    for part in range(PARTS):
        keys, solved, before, transit, memory = first[part]
        second.append(
            rows_pass(
                part, query_raw, rim, conv_query, keys, gate_flat, logit_flat, solved, before
            )
        )
        got = lax.ppermute(memory.astype(BF16), "ctx", [(0, 1)])
        total = jnp.zeros_like(got)
        for source in range(1, count - 1):
            total = total + got
            moved = jnp.einsum("hab,hbc->hac", transit, got, preferred_element_type=F32) + memory
            got = lax.ppermute(moved.astype(BF16), "ctx", [(source, source + 1)])
        early.append(total)
        late.append(got)
    out = None
    for part in range(PARTS):
        rows, local = second[part]
        out = final_pass(part, rows, local, early[part], late[part], gain, out)
    return out


def solution(mesh):
    return jax.shard_map(
        shards,
        mesh=mesh,
        in_specs=(
            P(("groups", "ctx"), "head"),
            P(("groups", "ctx"), "head"),
            P(("groups", "ctx"), "head"),
            P(None, "head"),
            P(None, "head"),
            P(None, "head"),
            P(("groups", "ctx"), "head"),
            P(("groups", "ctx"), "head"),
            P(),
        ),
        out_specs=P(("groups", "ctx"), "head"),
        check_vma=False,
    )
```

time: 65.5 us -> 51.3 us (0.78)
  the two profiles are of different devices: /device:TPU:0 before, /device:TPU:18 now
where the time goes in v2:
time: 51.3 us; the launch traced here: 51.1 us
  Pallas kernels  32 us (62%)
  starting transfers between devices  10.3 us (20%)
  waiting for transfers between devices  7.58 us (15%)
  matrix products  0.7 us (1%)
    pallas_call x2, Pallas kernels, memory_pass(): pl.pallas_call(kernel, grid=(tok_count // span,), in_specs=[along(kheads...  16.5 us
    pallas_call x2, Pallas kernels, rows_pass(): pl.pallas_call(kernel, grid=(tok_count // span,), in_specs=[along(kheads...  8.87 us
    ppermute x4, starting transfers between devices, shards(): got = lax.ppermute(moved.astype(BF16), 'ctx', [(source, source + 1)])  5.36 us
    pallas_call x2, Pallas kernels, final_pass(): pl.pallas_call(kernel, grid=(tok_count // span,), in_specs=specs, out_spe...  5.13 us
    ppermute x4, waiting for transfers between devices, shards(): got = lax.ppermute(moved.astype(BF16), 'ctx', [(source, source + 1)])  4.7 us
    ppermute x1, starting transfers between devices, shards(): lax.ppermute(pack_rim(query_raw, key_raw, value_raw), 'ctx', [(at, at + 1...  3.47 us
    ppermute x1, waiting for transfers between devices, shards(): lax.ppermute(pack_rim(query_raw, key_raw, value_raw), 'ctx', [(at, at + 1...  2.88 us
    pallas_call x1, Pallas kernels, pack_rim(): pl.pallas_call(rim_kernel, grid=(1,), in_specs=[pl.BlockSpec((RIM, width)...  1.58 us
  transfers between devices with their start and end apart: 7, of which 2 were waited for; matrix products, arithmetic and copies ran while one was open for 2% of the time, Pallas kernels for 39%

profile of v2, /device:TPU:18, one launch (start us, length us, event | category | flops | bytes accessed | tf_op | source)
XLA Modules:
  0.0 51.1 jit_solution(8634912545823387232)
XLA Ops:
  0.0 0.0 copy-start.1
  0.0 0.0 copy-start
  0.0 0.0 copy-start.4
  0.0 0.0 copy-start.5
  0.0 0.0 copy-start.7
  0.0 0.0 copy-start.6
  0.0 1.6 %pack_rim.1 = bf16[16,2048]{1,0:T(8,128)(2,1)} custom-call(bf16[1024,512]{1,0:T(8,128)(2,1)} %refs_0_.7, bf16[1024,512]{1,0:T(8,128)(2,1)} %refs_0_.6, bf16[1024,1024]{1,0:T(8,128)(2,1)} %refs_1_.3), custom_call_target="tpu_custom_call" | custom-call | tf_op jit(solution)/shard_map/pack_rim/pallas_call | solution.py:145
  1.6 3.5 %collective-permute-start = (bf16[16,2048]{1,0:T(8,128)(2,1)}, bf16[16,2048]{1,0:T(8,128)(2,1)S(1)}, u32[]{:S(2)}, u32[]{:S(2)}) collective-permute-start(bf16[16,2048]{1,0:T(8,128)(2,1)} %pack_rim.1), channel_id=1, source_target_pairs={{0,4},{4,8},{8,12},{1,5},{5,9},{9,13},{2,6},{6,10},{10,14},{3,7},{... | collective-permute-start | bytes 196616 | tf_op jit(solution)/shard_map/ppermute | solution.py:501
  5.1 2.9 %collective-permute-done.refs_2_.refs_3_.refs_1_ = bf16[16,2048]{1,0:T(8,128)(2,1)S(1)} collective-permute-done((bf16[16,2048]{1,0:T(8,128)(2,1)}, bf16[16,2048]{1,0:T(8,128)(2,1)S(1)}, u32[]{:S(2)}, u32[]{:S(2)}) %collective-permute-start) | collective-permute-done | bytes 65568 | tf_op jit(solution)/shard_map/ppermute | solution.py:501
  8.0 0.0 copy-done.1
  8.0 0.0 copy-done
  8.0 0.0 copy-done.4
  8.0 0.0 copy-done.5
  8.0 0.0 copy-done.7
  8.0 0.0 copy-done.6
  8.0 8.2 %memory_pass.3 = (bf16[1024,256]{1,0:T(8,128)(2,1)S(1)}, bf16[1024,1024]{1,0:T(8,128)(2,1)S(1)}, bf16[8,4,128,256]{3,2,1,0:T(8,128)(2,1)S(1)}, bf16[4,128,128]{2,1,0:T(8,128)(2,1)S(1)}, f32[4,128,128]{2,1,0:T(8,128)S(1)}) custom-call(bf16[1024,512]{1,0:T(8,128)(2,1)S(1)} %copy-done.1, bf16[1024,1024]{1,0:T(8,128)(2,1)S(1)} %copy-done, ...), custom_call_target="tpu_custom_call" | custom-call | flops 8192000000 | bytes 8388608 | tf_op jit(solution)/shard_map/memory_pass/pallas_call | solution.py:303
  16.3 0.0 copy-start.2
  16.3 0.0 copy-start.8
  16.3 0.8 %collective-permute-start.4 = (bf16[4,128,128]{2,1,0:T(8,128)(2,1)S(1)}, bf16[4,128,128]{2,1,0:T(8,128)(2,1)S(1)}, u32[]{:S(2)}, u32[]{:S(2)}) collective-permute-start(bf16[4,128,128]{2,1,0:T(8,128)(2,1)S(1)} %convert_element_type.21), channel_id=1, source_target_pairs={{0,4},{1,5},{2,6},{3,7},{16,20},{17,21},{18,22},{19,23}} | collective-permute-start | bytes 393224 | tf_op jit(solution)/shard_map/ppermute | solution.py:518
  17.1 8.2 %memory_pass.2 = (bf16[1024,256]{1,0:T(8,128)(2,1)S(1)}, bf16[1024,1024]{1,0:T(8,128)(2,1)S(1)}, bf16[8,4,128,256]{3,2,1,0:T(8,128)(2,1)S(1)}, bf16[4,128,128]{2,1,0:T(8,128)(2,1)S(1)}, f32[4,128,128]{2,1,0:T(8,128)S(1)}) custom-call(bf16[1024,512]{1,0:T(8,128)(2,1)S(1)} %copy-done.1, bf16[1024,1024]{1,0:T(8,128)(2,1)S(1)} %copy-done, ...), custom_call_target="tpu_custom_call" | custom-call | flops 8192000000 | bytes 8388608 | tf_op jit(solution)/shard_map/memory_pass/pallas_call | solution.py:303
  25.4 0.7 %collective-permute-start.1 = (bf16[4,128,128]{2,1,0:T(8,128)(2,1)S(1)}, bf16[4,128,128]{2,1,0:T(8,128)(2,1)S(1)}, u32[]{:S(2)}, u32[]{:S(2)}) collective-permute-start(bf16[4,128,128]{2,1,0:T(8,128)(2,1)S(1)} %convert_element_type.18), channel_id=1, source_target_pairs={{0,4},{1,5},{2,6},{3,7},{16,20},{17,21},{18,22},{19,23}} | collective-permute-start | bytes 393224 | tf_op jit(solution)/shard_map/ppermute | solution.py:518
  26.0 0.0 copy-done.2
  26.1 0.0 copy-done.8
  26.1 4.4 %rows_pass.3 = (bf16[1024,512]{1,0:T(8,128)(2,1)S(1)}, bf16[1024,512]{1,0:T(8,128)(2,1)S(1)}) custom-call(bf16[1024,512]{1,0:T(8,128)(2,1)S(1)} %copy-done.2, bf16[16,2048]{1,0:T(8,128)(2,1)S(1)} %collective-permute-done.refs_2_.refs_3_.refs_1_, bf16[4,512]{1,0:T(4,128)(2,1)S(1)} %copy-done.8, bf16[1024,256]{1,0:T(8,128)(2,1)S(1)} %get-tuple-element.26.refs_3_, ...), custom_call_target="tpu_custom_call" | custom-call | flops 4096000000 | bytes 8388608 | tf_op jit(solution)/shard_map/rows_pass/pallas_call | solution.py:424
  30.5 0.0 collective-permute-done.4
  30.5 0.2 fusion.2
  30.7 1.3 %collective-permute-start.5 = (bf16[4,128,128]{2,1,0:T(8,128)(2,1)S(1)}, bf16[4,128,128]{2,1,0:T(8,128)(2,1)S(1)}, u32[]{:S(2)}, u32[]{:S(2)}) collective-permute-start(bf16[4,128,128]{2,1,0:T(8,128)(2,1)S(1)} %fusion.2), channel_id=1, source_target_pairs={{4,8},{5,9},{6,10},{7,11},{20,24},{21,25},{22,26},{23,27}} | collective-permute-start | bytes 393224 | tf_op jit(solution)/shard_map/ppermute | solution.py:523
  32.0 0.0 collective-permute-done.1
  32.0 0.2 fusion
  32.2 1.3 %collective-permute-start.2 = (bf16[4,128,128]{2,1,0:T(8,128)(2,1)S(1)}, bf16[4,128,128]{2,1,0:T(8,128)(2,1)S(1)}, u32[]{:S(2)}, u32[]{:S(2)}) collective-permute-start(bf16[4,128,128]{2,1,0:T(8,128)(2,1)S(1)} %fusion), channel_id=1, source_target_pairs={{4,8},{5,9},{6,10},{7,11},{20,24},{21,25},{22,26},{23,27}} | collective-permute-start | bytes 393224 | tf_op jit(solution)/shard_map/ppermute | solution.py:523
  33.5 4.7 %collective-permute-done.5 = bf16[4,128,128]{2,1,0:T(8,128)(2,1)S(1)} collective-permute-done((bf16[4,128,128]{2,1,0:T(8,128)(2,1)S(1)}, bf16[4,128,128]{2,1,0:T(8,128)(2,1)S(1)}, u32[]{:S(2)}, u32[]{:S(2)}) %collective-permute-start.5) | collective-permute-done | bytes 131104 | tf_op jit(solution)/shard_map/ppermute | solution.py:523
  38.2 0.2 fusion.3
  38.4 1.3 %collective-permute-start.6 = (bf16[4,128,128]{2,1,0:T(8,128)(2,1)S(1)}, bf16[4,128,128]{2,1,0:T(8,128)(2,1)S(1)}, u32[]{:S(2)}, u32[]{:S(2)}) collective-permute-start(bf16[4,128,128]{2,1,0:T(8,128)(2,1)S(1)} %fusion.3), channel_id=1, source_target_pairs={{8,12},{9,13},{10,14},{11,15},{24,28},{25,29},{26,30},{27,31}} | collective-permute-start | bytes 393224 | tf_op jit(solution)/shard_map/ppermute | solution.py:523
  39.7 0.0 collective-permute-done.2
  39.7 0.2 fusion.1
  39.9 1.5 %collective-permute-start.3 = (bf16[4,128,128]{2,1,0:T(8,128)(2,1)S(1)}, bf16[4,128,128]{2,1,0:T(8,128)(2,1)S(1)}, u32[]{:S(2)}, u32[]{:S(2)}) collective-permute-start(bf16[4,128,128]{2,1,0:T(8,128)(2,1)S(1)} %fusion.1), channel_id=1, source_target_pairs={{8,12},{9,13},{10,14},{11,15},{24,28},{25,29},{26,30},{27,31}} | collective-permute-start | bytes 393224 | tf_op jit(solution)/shard_map/ppermute | solution.py:523
  41.4 0.0 copy-start.3
  41.4 4.4 %rows_pass.2 = (bf16[1024,512]{1,0:T(8,128)(2,1)S(1)}, bf16[1024,512]{1,0:T(8,128)(2,1)S(1)}) custom-call(bf16[1024,512]{1,0:T(8,128)(2,1)S(1)} %copy-done.2, bf16[16,2048]{1,0:T(8,128)(2,1)S(1)} %collective-permute-done.refs_2_.refs_3_.refs_1_, bf16[4,512]{1,0:T(4,128)(2,1)S(1)} %copy-done.8, bf16[1024,256]{1,0:T(8,128)(2,1)S(1)} %get-tuple-element.19.refs_3_, ...), custom_call_target="tpu_custom_call" | custom-call | flops 4096000000 | bytes 8388608 | tf_op jit(solution)/shard_map/rows_pass/pallas_call | solution.py:424
  45.9 0.0 collective-permute-done.6.refs_3_
  45.9 0.0 copy-done.3
  45.9 2.6 %final_pass.2.refs_5_ = bf16[1024,1024]{1,0:T(8,128)(2,1)} custom-call(bf16[1024,512]{1,0:T(8,128)(2,1)S(1)} %get-tuple-element.29.refs_0_, bf16[1024,512]{1,0:T(8,128)(2,1)S(1)} %get-tuple-element.30.refs_1_, bf16[4,128,128]{2,1,0:T(8,128)(2,1)S(1)} %add.22.refs_2_, bf16[4,128,128]{2,1,0:T(8,128)(2,1)S(1)} %collective-permute-done.6.refs_3_, ...), custom_call_target="tpu_custom_call" | custom-call | tf_op jit(solution)/shard_map/final_pass/pallas_call | solution.py:485
  48.5 0.0 collective-permute-done.3.refs_3_
  48.5 2.5 %final_pass.3 = bf16[1024,1024]{1,0:T(8,128)(2,1)} custom-call(bf16[1024,512]{1,0:T(8,128)(2,1)S(1)} %get-tuple-element.22.refs_0_, bf16[1024,512]{1,0:T(8,128)(2,1)S(1)} %get-tuple-element.23.refs_1_, bf16[4,128,128]{2,1,0:T(8,128)(2,1)S(1)} %add.19.refs_2_, ...), custom_call_target="tpu_custom_call", output_to_operand_aliasing={{}: (5, {})} | custom-call | tf_op jit(solution)/shard_map/final_pass/pallas_call | solution.py:485
  (4 shorter events, 0.1 us)
Async XLA Ops:
  0.0 8.0 %copy-start.1 = (bf16[1024,512]{1,0:T(8,128)(2,1)S(1)}, bf16[1024,512]{1,0:T(8,128)(2,1)}, u32[]{:S(2)}) copy-start(bf16[1024,512]{1,0:T(8,128)(2,1)} %refs_0_.6) | copy-start | bytes 3145732
  0.0 8.0 %copy-start = (bf16[1024,1024]{1,0:T(8,128)(2,1)S(1)}, bf16[1024,1024]{1,0:T(8,128)(2,1)}, u32[]{:S(2)}) copy-start(bf16[1024,1024]{1,0:T(8,128)(2,1)} %refs_1_.3) | copy-start | bytes 6291460
  0.0 8.0 %copy-start.4 = (f32[1024,8]{0,1:T(8,128)S(1)}, f32[1024,8]{0,1:T(8,128)}, u32[]{:S(2)}) copy-start(f32[1024,8]{0,1:T(8,128)} %param.15) | copy-start | bytes 98308
  0.0 8.0 %copy-start.5 = (f32[1024,8]{0,1:T(8,128)S(1)}, f32[1024,8]{0,1:T(8,128)}, u32[]{:S(2)}) copy-start(f32[1024,8]{0,1:T(8,128)} %param.16) | copy-start | bytes 98308
  0.0 8.0 %copy-start.7 = (bf16[4,512]{1,0:T(4,128)(2,1)S(1)}, bf16[4,512]{1,0:T(4,128)(2,1)}, u32[]{:S(2)}) copy-start(bf16[4,512]{1,0:T(4,128)(2,1)} %refs_4_.3) | copy-start | bytes 12292
  0.0 8.0 %copy-start.6 = (bf16[4,1024]{1,0:T(4,128)(2,1)S(1)}, bf16[4,1024]{1,0:T(4,128)(2,1)}, u32[]{:S(2)}) copy-start(bf16[4,1024]{1,0:T(4,128)(2,1)} %refs_5_.3) | copy-start | bytes 24580
  1.6 6.4 %collective-permute-start = (bf16[16,2048]{1,0:T(8,128)(2,1)}, bf16[16,2048]{1,0:T(8,128)(2,1)S(1)}, u32[]{:S(2)}, u32[]{:S(2)}) collective-permute-start(bf16[16,2048]{1,0:T(8,128)(2,1)} %pack_rim.1), channel_id=1, source_target_pairs={{0,4},{4,8},{8,12},{1,5},{5,9},{9,13},{2,6},{6,10},{10,14},{3,7},{... | collective-permute-start | bytes 196616 | tf_op jit(solution)/shard_map/ppermute | solution.py:501
  16.3 9.8 %copy-start.2 = (bf16[1024,512]{1,0:T(8,128)(2,1)S(1)}, bf16[1024,512]{1,0:T(8,128)(2,1)}, u32[]{:S(2)}) copy-start(bf16[1024,512]{1,0:T(8,128)(2,1)} %refs_0_.7) | copy-start | bytes 3145732
  16.3 9.8 %copy-start.8 = (bf16[4,512]{1,0:T(4,128)(2,1)S(1)}, bf16[4,512]{1,0:T(4,128)(2,1)}, u32[]{:S(2)}) copy-start(bf16[4,512]{1,0:T(4,128)(2,1)} %refs_2_.3) | copy-start | bytes 12292
  16.3 14.2 %collective-permute-start.4 = (bf16[4,128,128]{2,1,0:T(8,128)(2,1)S(1)}, bf16[4,128,128]{2,1,0:T(8,128)(2,1)S(1)}, u32[]{:S(2)}, u32[]{:S(2)}) collective-permute-start(bf16[4,128,128]{2,1,0:T(8,128)(2,1)S(1)} %convert_element_type.21), channel_id=1, source_target_pairs={{0,4},{1,5},{2,6},{3,7},{16,20},{17,21},{18,22},{19,23}} | collective-permute-start | bytes 393224 | tf_op jit(solution)/shard_map/ppermute | solution.py:518
  25.4 6.6 %collective-permute-start.1 = (bf16[4,128,128]{2,1,0:T(8,128)(2,1)S(1)}, bf16[4,128,128]{2,1,0:T(8,128)(2,1)S(1)}, u32[]{:S(2)}, u32[]{:S(2)}) collective-permute-start(bf16[4,128,128]{2,1,0:T(8,128)(2,1)S(1)} %convert_element_type.18), channel_id=1, source_target_pairs={{0,4},{1,5},{2,6},{3,7},{16,20},{17,21},{18,22},{19,23}} | collective-permute-start | bytes 393224 | tf_op jit(solution)/shard_map/ppermute | solution.py:518
  30.7 7.5 %collective-permute-start.5 = (bf16[4,128,128]{2,1,0:T(8,128)(2,1)S(1)}, bf16[4,128,128]{2,1,0:T(8,128)(2,1)S(1)}, u32[]{:S(2)}, u32[]{:S(2)}) collective-permute-start(bf16[4,128,128]{2,1,0:T(8,128)(2,1)S(1)} %fusion.2), channel_id=1, source_target_pairs={{4,8},{5,9},{6,10},{7,11},{20,24},{21,25},{22,26},{23,27}} | collective-permute-start | bytes 393224 | tf_op jit(solution)/shard_map/ppermute | solution.py:523
  32.2 7.5 %collective-permute-start.2 = (bf16[4,128,128]{2,1,0:T(8,128)(2,1)S(1)}, bf16[4,128,128]{2,1,0:T(8,128)(2,1)S(1)}, u32[]{:S(2)}, u32[]{:S(2)}) collective-permute-start(bf16[4,128,128]{2,1,0:T(8,128)(2,1)S(1)} %fusion), channel_id=1, source_target_pairs={{4,8},{5,9},{6,10},{7,11},{20,24},{21,25},{22,26},{23,27}} | collective-permute-start | bytes 393224 | tf_op jit(solution)/shard_map/ppermute | solution.py:523
  38.4 7.5 %collective-permute-start.6 = (bf16[4,128,128]{2,1,0:T(8,128)(2,1)S(1)}, bf16[4,128,128]{2,1,0:T(8,128)(2,1)S(1)}, u32[]{:S(2)}, u32[]{:S(2)}) collective-permute-start(bf16[4,128,128]{2,1,0:T(8,128)(2,1)S(1)} %fusion.3), channel_id=1, source_target_pairs={{8,12},{9,13},{10,14},{11,15},{24,28},{25,29},{26,30},{27,31}} | collective-permute-start | bytes 393224 | tf_op jit(solution)/shard_map/ppermute | solution.py:523
  39.9 8.6 %collective-permute-start.3 = (bf16[4,128,128]{2,1,0:T(8,128)(2,1)S(1)}, bf16[4,128,128]{2,1,0:T(8,128)(2,1)S(1)}, u32[]{:S(2)}, u32[]{:S(2)}) collective-permute-start(bf16[4,128,128]{2,1,0:T(8,128)(2,1)S(1)} %fusion.1), channel_id=1, source_target_pairs={{8,12},{9,13},{10,14},{11,15},{24,28},{25,29},{26,30},{27,31}} | collective-permute-start | bytes 393224 | tf_op jit(solution)/shard_map/ppermute | solution.py:523
  41.4 4.6 %copy-start.3 = (f32[128]{0:T(128)S(1)}, f32[128]{0:T(128)}, u32[]{:S(2)}) copy-start(f32[128]{0:T(128)} %param.17) | copy-start | bytes 1540

commit v3 on v2

v3 whole, which is shorter than its diff:
```python
import jax
import jax.numpy as jnp
from jax import lax
from jax.experimental import pallas as pl
from jax.experimental.pallas import tpu as pltpu
from jax.sharding import PartitionSpec as P

DK = 128
DV = 128
KW = 4
CHUNK = 128
HALF = 64
BASE = 8
HALO = 8
RIM = 16
PARTS = 2
SPAN_X = 512
SPAN_Y = 512
EPSILON = 1e-06
LOG2E = 1.4426950408889634
F32 = jnp.float32
BF16 = jnp.bfloat16
WIDE = DK + DV


def dot(left, right):
    return jnp.dot(left, right, preferred_element_type=F32)


def levels():
    sizes = []
    size = BASE
    while size < HALF:
        sizes.append(size)
        size *= 2
    return sizes


def iotas(shape):
    return lax.broadcasted_iota(jnp.int32, shape, 0), lax.broadcasted_iota(jnp.int32, shape, 1)


def fill_masks(diag_ref):
    rows, cols = iotas((CHUNK, CHUNK))
    for place, size in enumerate(levels()):
        diag_ref[place] = (rows // size == cols // size).astype(BF16)


def packed(strip):
    if strip.shape[0] < 16:
        strip = jnp.concatenate([strip] * (16 // strip.shape[0]), axis=0)
    return strip.astype(BF16)


def spread(strip, mask):
    count = CHUNK // strip.shape[0]
    return jnp.concatenate([strip] * count, axis=0) * mask


def strips(neg, size, step, first):
    lanes = lax.broadcasted_iota(jnp.int32, (1, CHUNK), 1)
    out = neg[first : first + size]
    for turn in range(1, CHUNK // step):
        start = turn * step + first
        out = jnp.where(lanes // step == turn, neg[start : start + size], out)
    return out


def substitute(strip):
    rows, cols = iotas((8, CHUNK))
    halves = [strip[at : at + 8] for at in range(0, BASE, 8)]
    found = [(rows + at == cols % BASE).astype(F32) for at in range(0, BASE, 8)]
    for row in range(BASE - 1):
        at = cols // BASE * BASE + row
        solved = found[row // 8][row % 8 : row % 8 + 1]
        for half in range((row + 1) // 8, BASE // 8):
            column = jnp.take_along_axis(halves[half], at, axis=1)
            found[half] = found[half] + column * solved
    return jnp.concatenate(found, axis=0)


def half_inverses(negs, diag_ref):
    lanes = lax.broadcasted_iota(jnp.int32, (1, CHUNK), 1)
    found = [substitute(strips(neg, BASE, BASE, 0)) for neg in negs]
    pairs = range(0, len(negs), 2)
    for place, size in enumerate(levels()):
        even = (lanes // size) % 2 == 0

        def up(value):
            return pltpu.roll(value, size, 1)

        def down(value):
            return pltpu.roll(value, CHUNK - size, 1)

        lowers = [strips(neg, size, 2 * size, size) for neg in negs]
        evens = [packed(jnp.where(even, found[i], up(found[i + 1]))) for i in pairs]
        odds = [packed(jnp.where(even, down(found[i]), found[i + 1])) for i in pairs]
        both = [packed(jnp.where(even, lowers[i], up(lowers[i + 1]))) for i in pairs]
        weights = [spread(value, diag_ref[place]) for value in evens]
        middles = [dot(value, weight).astype(BF16) for value, weight in zip(both, weights)]
        weights = [spread(value, diag_ref[place]) for value in middles]
        corners = [dot(value, weight)[:size] for value, weight in zip(odds, weights)]
        wider = []
        for i, f in enumerate(found):
            corner = corners[i // 2] if i % 2 == 0 else down(corners[i // 2])
            wider.append(
                jnp.concatenate([jnp.where(even, f, 0.0), jnp.where(even, corner, f)], axis=0)
            )
        found = wider
    return [f.astype(BF16) for f in found]


def conv(raw, wide, tile, tap):
    span = raw.shape[0]
    raw = raw.astype(F32)
    wide[tile, HALO : HALO + span] = raw
    total = raw * tap[KW - 1 : KW]
    for back in range(1, KW):
        total += wide[tile, HALO - back : HALO - back + span] * tap[KW - 1 - back : KW - back]
    return (total + total * jnp.tanh(total)).astype(BF16)


def row_sums(values):
    return dot(values.astype(BF16), jnp.ones((values.shape[1], values.shape[1]), BF16))


def unit(values, factor):
    values = values.astype(F32)
    scale = lax.rsqrt(jnp.sum(values * values, axis=-1, keepdims=True) + EPSILON)
    if factor != 1.0:
        scale = scale * factor
    return (values * scale).astype(BF16)


def sums(gates, span):
    rows, cols = iotas((CHUNK, CHUNK))
    stacked = jnp.concatenate(
        [gates[:, at : at + CHUNK] for at in range(0, span, CHUNK)], axis=0
    )
    total = jnp.dot(
        stacked,
        (rows <= cols).astype(F32),
        precision=lax.Precision.HIGHEST,
        preferred_element_type=F32,
    )
    heads = gates.shape[0]
    return [total[at * heads : (at + 1) * heads] for at in range(span // CHUNK)]


def rim_kernel(query_ref, key_ref, value_ref, out_ref):
    first, second = query_ref.shape[1], key_ref.shape[1]
    out_ref[:, :first] = query_ref[...]
    out_ref[:, first : first + second] = key_ref[...]
    out_ref[:, first + second :] = value_ref[...]


def pack_rim(query_raw, key_raw, value_raw):
    last = query_raw.shape[0] // RIM - 1
    widths = [array.shape[1] for array in (query_raw, key_raw, value_raw)]
    return pl.pallas_call(
        rim_kernel,
        grid=(1,),
        in_specs=[pl.BlockSpec((RIM, width), lambda i: (last, 0)) for width in widths],
        out_specs=pl.BlockSpec((RIM, sum(widths)), lambda i: (0, 0)),
        out_shape=jax.ShapeDtypeStruct((RIM, sum(widths)), BF16),
        name="pack_rim",
    )(query_raw, key_raw, value_raw)


def log_weights(logit):
    return (jnp.minimum(logit, 0.0) - jnp.log(1.0 + jnp.exp(-jnp.abs(logit)))) * LOG2E


def memory_kernel(
    kheads,
    vheads,
    first_head,
    key_ref,
    value_ref,
    rim_key_ref,
    rim_value_ref,
    tap_key_ref,
    tap_value_ref,
    gate_ref,
    logit_ref,
    unit_ref,
    solved_ref,
    before_ref,
    transit_ref,
    memory_ref,
    wide,
    state,
    diag_ref,
    neg_ref,
    tail_ref,
    right_ref,
    sum_ref,
):
    step = pl.program_id(0)
    last_step = pl.num_programs(0) - 1
    ratio = vheads // kheads
    span = key_ref.shape[0]
    tiles = kheads + vheads
    parts = span // CHUNK
    places = [(part, head) for part in range(parts) for head in range(vheads)]

    def set_up():
        fill_masks(diag_ref)
        rows, cols = iotas((DK, WIDE))
        for head in range(vheads):
            state[head] = (rows == cols).astype(F32)
        for tile in range(tiles):
            ref, at = (rim_key_ref, tile) if tile < kheads else (rim_value_ref, tile - kheads)
            wide[tile, 0:HALO] = ref[:, at * 128 : (at + 1) * 128].astype(F32)[RIM - HALO :]

    def prepare():
        tap_key = tap_key_ref[...].astype(F32) * 0.5
        tap_value = tap_value_ref[...].astype(F32) * 0.5
        keys = []
        for tile in range(kheads):
            at = slice(tile * DK, (tile + 1) * DK)
            keys.append(unit(conv(key_ref[:, at], wide, tile, tap_key[:, at]), 1.0))
            unit_ref[:, at] = keys[tile]
        for tile in range(vheads):
            at = slice(tile * DV, (tile + 1) * DV)
            value = conv(value_ref[:, at], wide, kheads + tile, tap_value[:, at])
            for part in range(parts):
                right_ref[part * vheads + tile, :, DK:] = value[
                    part * CHUNK : (part + 1) * CHUNK
                ]
        for tile in range(tiles):
            wide[tile, 0:HALO] = wide[tile, span : span + HALO]
        rows, cols = iotas((CHUNK, CHUNK))
        strict = rows > cols
        cums = sums(gate_ref[...] * LOG2E, span)
        strengths = log_weights(logit_ref[...])
        for part in range(parts):
            here = slice(part * CHUNK, (part + 1) * CHUNK)
            cum_flat = cums[part]
            cum = cum_flat.T
            lift = strengths[:, here] - cum_flat
            last = cum_flat[:, CHUNK - 1 :]
            ends = jnp.exp2(last + lift)
            sum_ref[part] = jnp.broadcast_to(jnp.exp2(last), cum_flat.shape)
            for khead in range(kheads):
                key = keys[khead][here]
                flat = (-key).T
                gram = dot(key, flat)
                for which in range(ratio):
                    head = khead * ratio + which
                    item = part * vheads + head
                    place = first_head + head
                    cum_col = jnp.broadcast_to(cum[:, place : place + 1], (CHUNK, CHUNK))
                    powers = cum_col + lift[place : place + 1]
                    decays = jnp.exp2(jnp.where(strict, powers, -jnp.inf))
                    neg_ref[item] = gram * decays
                    tail_ref[item] = flat * ends[place : place + 1].astype(BF16)
                    right_ref[item, :, :DK] = key * jnp.exp2(cum_col).astype(BF16)

    def finish():
        negs = [neg_ref[item] for item in range(len(places))]
        found = half_inverses(negs, diag_ref)
        tops = [
            dot(f[:, :HALF], right_ref[item, :HALF]).astype(BF16)
            for item, f in enumerate(found)
        ]
        rests = [
            (
                right_ref[item, HALF:].astype(F32)
                + dot(neg_ref[item, HALF:, :HALF].astype(BF16), top)
            ).astype(BF16)
            for item, top in enumerate(tops)
        ]
        lows = [dot(f[:, HALF:], rest).astype(BF16) for f, rest in zip(found, rests)]
        erases, writes = [], []
        for item, (part, head) in enumerate(places):
            there = slice(head * WIDE, (head + 1) * WIDE)
            solved = jnp.concatenate([tops[item], lows[item]], axis=0)
            solved_ref[part * CHUNK : (part + 1) * CHUNK, there] = solved
            product = dot(tail_ref[item], solved)
            erases.append(product[:, :DK].astype(BF16))
            writes.append(product[:, DK:])
        for item, (part, head) in enumerate(places):
            now = state[head]
            short = now.astype(BF16)
            before_ref[part, head] = short
            tail = sum_ref[part, first_head + head : first_head + head + 1]
            change = dot(erases[item], short)
            state[head, :, :DK] = now[:, :DK] * tail + change[:, :DK]
            state[head, :, DK:] = now[:, DK:] * tail + (change[:, DK:] - writes[item])

    @pl.when(step == 0)
    def _():
        set_up()

    prepare()
    finish()

    @pl.when(step == last_step)
    def _():
        for head in range(vheads):
            transit_ref[head] = state[head, :, :DK].astype(BF16)
            memory_ref[head] = state[head, :, DK:]


def memory_pass(part, key_raw, value_raw, rim, conv_key, conv_value, gate_flat, logit_flat):
    tok_count = key_raw.shape[0]
    all_kheads = key_raw.shape[1] // DK
    all_vheads = value_raw.shape[1] // DV
    kheads, vheads = all_kheads // PARTS, all_vheads // PARTS
    tiles = kheads + vheads
    span = min(SPAN_X, tok_count)
    chunks = tok_count // CHUNK
    items = span // CHUNK * vheads
    blocks = tok_count // span
    count = len(levels())
    rim_key = PARTS + part
    rim_value = (2 * all_kheads) // vheads + part

    def ahead(width, column):
        return pl.BlockSpec((span, width), lambda i: (i, column))

    def fixed(shape, *place):
        return pl.BlockSpec(shape, lambda i: place)

    flat = pl.BlockSpec((all_vheads, span), lambda i: (0, i))

    def kernel(*refs):
        memory_kernel(kheads, vheads, part * vheads, *refs)

    return pl.pallas_call(
        kernel,
        grid=(blocks,),
        in_specs=[
            ahead(kheads * DK, part),
            ahead(vheads * DV, part),
            fixed((RIM, kheads * DK), 0, rim_key),
            fixed((RIM, vheads * DV), 0, rim_value),
            fixed((KW, kheads * DK), 0, part),
            fixed((KW, vheads * DV), 0, part),
            flat,
            flat,
        ],
        out_specs=[
            ahead(kheads * DK, 0),
            pl.BlockSpec((span, vheads * WIDE), lambda i: (i, 0)),
            pl.BlockSpec(
                (span // CHUNK, vheads, DK, WIDE), lambda i: (i, 0, 0, 0)
            ),
            fixed((vheads, DK, DK), 0, 0, 0),
            fixed((vheads, DK, DV), 0, 0, 0),
        ],
        out_shape=[
            jax.ShapeDtypeStruct((tok_count, kheads * DK), BF16),
            jax.ShapeDtypeStruct((tok_count, vheads * WIDE), BF16),
            jax.ShapeDtypeStruct((chunks, vheads, DK, WIDE), BF16),
            jax.ShapeDtypeStruct((vheads, DK, DK), BF16),
            jax.ShapeDtypeStruct((vheads, DK, DV), F32),
        ],
        scratch_shapes=[
            pltpu.VMEM((tiles, span + HALO, 128), F32),
            pltpu.VMEM((vheads, DK, WIDE), F32),
            pltpu.VMEM((count, CHUNK, CHUNK), BF16),
            pltpu.VMEM((items, CHUNK, CHUNK), F32),
            pltpu.VMEM((items, CHUNK, CHUNK), BF16),
            pltpu.VMEM((items, CHUNK, WIDE), BF16),
            pltpu.VMEM((span // CHUNK, all_vheads, CHUNK), F32),
        ],
        compiler_params=pltpu.CompilerParams(vmem_limit_bytes=40 * 1024 * 1024),
        cost_estimate=pl.CostEstimate(
            flops=2 * tok_count * vheads * 1000 * 1000, bytes_accessed=1 << 23, transcendentals=0
        ),
        name="memory_pass",
    )(key_raw, value_raw, rim, rim, conv_key, conv_value, gate_flat, logit_flat)


def rows_kernel(
    kheads,
    vheads,
    first_head,
    query_ref,
    rim_ref,
    tap_ref,
    key_ref,
    gate_ref,
    logit_ref,
    solved_ref,
    before_ref,
    rows_ref,
    local_ref,
    wide,
):
    step = pl.program_id(0)
    ratio = vheads // kheads
    span = query_ref.shape[0]

    @pl.when(step == 0)
    def _():
        for tile in range(kheads):
            wide[tile, 0:HALO] = rim_ref[:, tile * DK : (tile + 1) * DK].astype(F32)[RIM - HALO :]

    @pl.when(step > 0)
    def _():
        for tile in range(kheads):
            wide[tile, 0:HALO] = wide[tile, span : span + HALO]

    taps = tap_ref[...].astype(F32) * 0.5
    queries = []
    for tile in range(kheads):
        at = slice(tile * DK, (tile + 1) * DK)
        queries.append(unit(conv(query_ref[:, at], wide, tile, taps[:, at]), DK**-0.5))

    rows, cols = iotas((CHUNK, CHUNK))
    lower = rows >= cols
    cums = sums(gate_ref[...] * LOG2E, span)
    strengths = log_weights(logit_ref[...])
    for part in range(span // CHUNK):
        here = slice(part * CHUNK, (part + 1) * CHUNK)
        cum_flat = cums[part]
        cum = cum_flat.T
        lift = strengths[:, here] - cum_flat
        for khead in range(kheads):
            query = queries[khead][here]
            gram = lax.dot_general(
                query,
                key_ref[here, khead * DK : (khead + 1) * DK],
                (((1,), (1,)), ((), ())),
                preferred_element_type=F32,
            )
            for which in range(ratio):
                head = khead * ratio + which
                place = first_head + head
                there = slice(head * DV, (head + 1) * DV)
                cum_col = jnp.broadcast_to(cum[:, place : place + 1], (CHUNK, CHUNK))
                powers = cum_col + lift[place : place + 1]
                scores = (gram * jnp.exp2(jnp.where(lower, powers, -jnp.inf))).astype(BF16)
                product = dot(scores, solved_ref[here, head * WIDE : (head + 1) * WIDE])
                meet = query.astype(F32) * jnp.exp2(cum_col) - product[:, :DK]
                final = dot(meet.astype(BF16), before_ref[part, head])
                rows_ref[here, there] = final[:, :DK].astype(BF16)
                local_ref[here, there] = (final[:, DK:] + product[:, DK:]).astype(BF16)


def rows_pass(part, query_raw, rim, conv_query, keys, gate_flat, logit_flat, solved, before):
    tok_count = query_raw.shape[0]
    kheads = query_raw.shape[1] // DK // PARTS
    all_vheads = gate_flat.shape[0]
    vheads = all_vheads // PARTS
    span = min(SPAN_Y, tok_count)

    def along(width, column):
        return pl.BlockSpec((span, width), lambda i: (i, column))

    def kernel(*refs):
        rows_kernel(kheads, vheads, part * vheads, *refs)

    return pl.pallas_call(
        kernel,
        grid=(tok_count // span,),
        in_specs=[
            along(kheads * DK, part),
            pl.BlockSpec((RIM, kheads * DK), lambda i: (0, part)),
            pl.BlockSpec((KW, kheads * DK), lambda i: (0, part)),
            along(kheads * DK, 0),
            pl.BlockSpec((all_vheads, span), lambda i: (0, i)),
            pl.BlockSpec((all_vheads, span), lambda i: (0, i)),
            along(vheads * WIDE, 0),
            pl.BlockSpec((span // CHUNK, vheads, DK, WIDE), lambda i: (i, 0, 0, 0)),
        ],
        out_specs=[along(vheads * DV, 0), along(vheads * DV, 0)],
        out_shape=[
            jax.ShapeDtypeStruct((tok_count, vheads * DV), BF16),
            jax.ShapeDtypeStruct((tok_count, vheads * DV), BF16),
        ],
        scratch_shapes=[pltpu.VMEM((kheads, span + HALO, 128), F32)],
        compiler_params=pltpu.CompilerParams(vmem_limit_bytes=32 * 1024 * 1024),
        cost_estimate=pl.CostEstimate(
            flops=2 * tok_count * vheads * 1000 * 500, bytes_accessed=1 << 23, transcendentals=0
        ),
        name="rows_pass",
    )(query_raw, rim, conv_query, keys, gate_flat, logit_flat, solved, before)


def final_kernel(vheads, rows_ref, local_ref, early_ref, late_ref, gain_ref, *rest):
    out_ref = rest[-1]
    gain = gain_ref[...]
    for head in range(vheads):
        there = slice(head * DV, (head + 1) * DV)
        start = early_ref[head] + late_ref[head]
        output = dot(rows_ref[:, there], start) + local_ref[:, there].astype(F32)
        square = output * output
        if head % 2:
            total = row_sums(square)
        else:
            total = jnp.sum(square, axis=-1, keepdims=True)
        mean = total * (1.0 / DV)
        out_ref[:, there] = (output * lax.rsqrt(mean + EPSILON) * gain).astype(BF16)


def final_pass(part, rows, local, early, late, gain, earlier):
    tok_count = rows.shape[0]
    vheads = early.shape[0]
    span = min(512, tok_count)

    def along(width, column):
        return pl.BlockSpec((span, width), lambda i: (i, column))

    def kernel(*refs):
        final_kernel(vheads, *refs)

    whole = pl.BlockSpec((vheads, DK, DV), lambda i: (0, 0, 0))
    arrays = [rows, local, early, late, gain]
    specs = [
        along(vheads * DV, 0),
        along(vheads * DV, 0),
        whole,
        whole,
        pl.BlockSpec((1, DV), lambda i: (0, 0)),
    ]
    if earlier is not None:
        arrays.append(earlier)
        specs.append(pl.BlockSpec(memory_space=pl.ANY))
    return pl.pallas_call(
        kernel,
        grid=(tok_count // span,),
        in_specs=specs,
        out_specs=along(vheads * DV, part),
        out_shape=jax.ShapeDtypeStruct((tok_count, PARTS * vheads * DV), BF16),
        input_output_aliases={} if earlier is None else {5: 0},
        compiler_params=pltpu.CompilerParams(vmem_limit_bytes=32 * 1024 * 1024),
        name="final_pass",
    )(*arrays)


def shards(
    query_raw, key_raw, value_raw, conv_query, conv_key, conv_value, gate_log, beta_logit, norm_gain
):
    count = lax.axis_size("ctx")
    rim = lax.ppermute(
        pack_rim(query_raw, key_raw, value_raw), "ctx", [(at, at + 1) for at in range(count - 1)]
    )
    gate_flat, logit_flat = gate_log.T, beta_logit.T
    gain = norm_gain.reshape(1, DV)
    first = [
        memory_pass(part, key_raw, value_raw, rim, conv_key, conv_value, gate_flat, logit_flat)
        for part in range(PARTS)
    ]
    def after(value, *others):
        return lax.optimization_barrier((value, *others))[0]

    moved = [[found[4].astype(BF16)] for found in first]
    got = [[] for _ in first]
    second = [None] * PARTS

    def send(part):
        source = len(got[part])
        got[part].append(lax.ppermute(moved[part][source], "ctx", [(source, source + 1)]))

    def carry(part, *others):
        transit, memory = first[part][3:]
        arrived = after(got[part][-1], *others)
        ahead = jnp.einsum("hab,hbc->hac", transit, arrived, preferred_element_type=F32)
        moved[part].append((ahead + memory).astype(BF16))

    def rows_of(part, *others):
        keys, solved, before = first[part][:3]
        second[part] = rows_pass(
            part,
            query_raw,
            rim,
            conv_query,
            keys,
            gate_flat,
            logit_flat,
            after(solved, *others),
            before,
        )

    for turn in range(count - 1):
        for part in range(PARTS):
            send(part)
            if turn + 1 < count - 1:
                waits = [] if part == 0 or turn >= PARTS else [second[turn][1]]
                carry(part, *waits)
            if part == 0 and turn < PARTS:
                ready = [moved[part][-1] for part in range(PARTS)]
                rows_of(turn, *ready)
    out = None
    for part in range(PARTS):
        rows, local = second[part]
        early = sum(got[part][:-1], jnp.zeros_like(got[part][-1]))
        late = got[part][-1]
        if part + 1 < PARTS:
            late = after(late, moved[part + 1][-1])
        out = final_pass(part, rows, local, early, late, gain, out)
    return out


def solution(mesh):
    return jax.shard_map(
        shards,
        mesh=mesh,
        in_specs=(
            P(("groups", "ctx"), "head"),
            P(("groups", "ctx"), "head"),
            P(("groups", "ctx"), "head"),
            P(None, "head"),
            P(None, "head"),
            P(None, "head"),
            P(("groups", "ctx"), "head"),
            P(("groups", "ctx"), "head"),
            P(),
        ),
        out_specs=P(("groups", "ctx"), "head"),
        check_vma=False,
    )
```

time: 51.3 us -> 48.5 us (0.945)
  the two profiles are of different devices: /device:TPU:18 before, /device:TPU:0 now
where the time goes in v3:
time: 48.5 us; the launch traced here: 48.3 us
  Pallas kernels  31.5 us (65%)
  starting transfers between devices  13.4 us (28%)
  waiting for transfers between devices  2.22 us (5%)
  matrix products  0.71 us (1%)
    pallas_call x2, Pallas kernels, memory_pass(): pl.pallas_call(kernel, grid=(blocks,), in_specs=[ahead(kheads * DK, part)...  17 us
    pallas_call x2, Pallas kernels, rows_pass(): pl.pallas_call(kernel, grid=(tok_count // span,), in_specs=[along(kheads...  9.09 us
    ppermute x6, starting transfers between devices, send(): lax.ppermute(moved[part][source], 'ctx', [(source, source + 1)])  8.46 us
    ppermute x1, starting transfers between devices, shards(): lax.ppermute(pack_rim(query_raw, key_raw, value_raw), 'ctx', [(at, at + 1...  4.93 us
    pallas_call x2, Pallas kernels, final_pass(): pl.pallas_call(kernel, grid=(tok_count // span,), in_specs=specs, out_spe...  3.88 us
    ppermute x1, waiting for transfers between devices, shards(): lax.ppermute(pack_rim(query_raw, key_raw, value_raw), 'ctx', [(at, at + 1...  2.2 us
    pallas_call x1, Pallas kernels, pack_rim(): pl.pallas_call(rim_kernel, grid=(1,), in_specs=[pl.BlockSpec((RIM, width)...  1.58 us
  transfers between devices with their start and end apart: 7, of which 1 were waited for; matrix products, arithmetic and copies ran while one was open for 2% of the time, Pallas kernels for 40%

profile of v3, /device:TPU:0, one launch (start us, length us, event | category | flops | bytes accessed | tf_op | source)
XLA Modules:
  0.0 48.3 jit_solution(14743319674015714026)
XLA Ops:
  0.0 0.0 copy-start
  0.0 0.0 copy-start.1
  0.0 0.0 copy-start.6
  0.0 0.0 copy-start.7
  0.0 0.0 copy-start.5
  0.0 0.0 copy-start.4
  0.0 1.6 %pack_rim.1 = bf16[16,2048]{1,0:T(8,128)(2,1)} custom-call(bf16[1024,512]{1,0:T(8,128)(2,1)} %refs_0_.7, bf16[1024,512]{1,0:T(8,128)(2,1)} %refs_0_.5, bf16[1024,1024]{1,0:T(8,128)(2,1)} %refs_1_.3), custom_call_target="tpu_custom_call" | custom-call | tf_op jit(solution)/shard_map/pack_rim/pallas_call | solution.py:160
  1.6 4.9 %collective-permute-start = (bf16[16,2048]{1,0:T(8,128)(2,1)}, bf16[16,2048]{1,0:T(8,128)(2,1)S(1)}, u32[]{:S(2)}, u32[]{:S(2)}) collective-permute-start(bf16[16,2048]{1,0:T(8,128)(2,1)} %pack_rim.1), channel_id=1, source_target_pairs={{0,4},{4,8},{8,12},{1,5},{5,9},{9,13},{2,6},{6,10},{10,14},{3,7},{... | collective-permute-start | bytes 196616 | tf_op jit(solution)/shard_map/ppermute | solution.py:539
  6.5 2.2 %collective-permute-done.refs_2_.refs_3_.refs_1_ = bf16[16,2048]{1,0:T(8,128)(2,1)S(1)} collective-permute-done((bf16[16,2048]{1,0:T(8,128)(2,1)}, bf16[16,2048]{1,0:T(8,128)(2,1)S(1)}, u32[]{:S(2)}, u32[]{:S(2)}) %collective-permute-start) | collective-permute-done | bytes 65568 | tf_op jit(solution)/shard_map/ppermute | solution.py:539
  8.7 0.0 copy-done
  8.7 0.0 copy-done.1
  8.7 0.0 copy-done.6
  8.8 0.0 copy-done.7
  8.8 0.0 copy-done.5
  8.8 0.0 copy-done.4
  8.8 8.5 %memory_pass.3 = (bf16[1024,256]{1,0:T(8,128)(2,1)S(1)}, bf16[1024,1024]{1,0:T(8,128)(2,1)S(1)}, bf16[8,4,128,256]{3,2,1,0:T(8,128)(2,1)S(1)}, bf16[4,128,128]{2,1,0:T(8,128)(2,1)S(1)}, f32[4,128,128]{2,1,0:T(8,128)S(1)}) custom-call(bf16[1024,512]{1,0:T(8,128)(2,1)S(1)} %copy-done.1, bf16[1024,1024]{1,0:T(8,128)(2,1)S(1)} %copy-done, ...), custom_call_target="tpu_custom_call" | custom-call | flops 8192000000 | bytes 8388608 | tf_op jit(solution)/shard_map/memory_pass/pallas_call | solution.py:331
  17.3 0.0 copy-start.2
  17.3 0.0 copy-start.8
  17.3 4.3 %collective-permute-start.1 = (bf16[4,128,128]{2,1,0:T(8,128)(2,1)S(1)}, bf16[4,128,128]{2,1,0:T(8,128)(2,1)S(1)}, u32[]{:S(2)}, u32[]{:S(2)}) collective-permute-start(bf16[4,128,128]{2,1,0:T(8,128)(2,1)S(1)} %convert_element_type.18), channel_id=1, source_target_pairs={{0,4},{1,5},{2,6},{3,7},{16,20},{17,21},{18,22},{19,23}} | collective-permute-start | bytes 393224 | tf_op jit(solution)/shard_map/ppermute | solution.py:557
  21.6 8.5 %memory_pass.2 = (bf16[1024,256]{1,0:T(8,128)(2,1)S(1)}, bf16[1024,1024]{1,0:T(8,128)(2,1)S(1)}, bf16[8,4,128,256]{3,2,1,0:T(8,128)(2,1)S(1)}, bf16[4,128,128]{2,1,0:T(8,128)(2,1)S(1)}, f32[4,128,128]{2,1,0:T(8,128)S(1)}) custom-call(bf16[1024,512]{1,0:T(8,128)(2,1)S(1)} %copy-done.1, bf16[1024,1024]{1,0:T(8,128)(2,1)S(1)} %copy-done, ...), custom_call_target="tpu_custom_call" | custom-call | flops 8192000000 | bytes 8388608 | tf_op jit(solution)/shard_map/memory_pass/pallas_call | solution.py:331
  30.2 1.3 %collective-permute-start.3 = (bf16[4,128,128]{2,1,0:T(8,128)(2,1)S(1)}, bf16[4,128,128]{2,1,0:T(8,128)(2,1)S(1)}, u32[]{:S(2)}, u32[]{:S(2)}) collective-permute-start(bf16[4,128,128]{2,1,0:T(8,128)(2,1)S(1)} %convert_element_type.21), channel_id=1, source_target_pairs={{0,4},{1,5},{2,6},{3,7},{16,20},{17,21},{18,22},{19,23}} | collective-permute-start | bytes 393224 | tf_op jit(solution)/shard_map/ppermute | solution.py:557
  31.5 0.0 collective-permute-done.1
  31.5 0.2 fusion
  31.7 0.7 %collective-permute-start.2 = (bf16[4,128,128]{2,1,0:T(8,128)(2,1)S(1)}, bf16[4,128,128]{2,1,0:T(8,128)(2,1)S(1)}, u32[]{:S(2)}, u32[]{:S(2)}) collective-permute-start(bf16[4,128,128]{2,1,0:T(8,128)(2,1)S(1)} %fusion), channel_id=1, source_target_pairs={{4,8},{5,9},{6,10},{7,11},{20,24},{21,25},{22,26},{23,27}} | collective-permute-start | bytes 393224 | tf_op jit(solution)/shard_map/ppermute | solution.py:557
  32.3 0.0 copy-done.2
  32.4 0.0 copy-done.8
  32.4 4.5 %rows_pass.2 = (bf16[1024,512]{1,0:T(8,128)(2,1)S(1)}, bf16[1024,512]{1,0:T(8,128)(2,1)S(1)}) custom-call(bf16[1024,512]{1,0:T(8,128)(2,1)S(1)} %copy-done.2, bf16[16,2048]{1,0:T(8,128)(2,1)S(1)} %collective-permute-done.refs_2_.refs_3_.refs_1_, bf16[4,512]{1,0:T(4,128)(2,1)S(1)} %copy-done.8, bf16[1024,256]{1,0:T(8,128)(2,1)S(1)} %get-tuple-element.30.refs_3_, ...), custom_call_target="tpu_custom_call" | custom-call | flops 4096000000 | bytes 8388608 | tf_op jit(solution)/shard_map/rows_pass/pallas_call | solution.py:457
  36.9 0.0 collective-permute-done.3
  36.9 0.2 fusion.2
  37.1 0.7 %collective-permute-start.4 = (bf16[4,128,128]{2,1,0:T(8,128)(2,1)S(1)}, bf16[4,128,128]{2,1,0:T(8,128)(2,1)S(1)}, u32[]{:S(2)}, u32[]{:S(2)}) collective-permute-start(bf16[4,128,128]{2,1,0:T(8,128)(2,1)S(1)} %fusion.2), channel_id=1, source_target_pairs={{4,8},{5,9},{6,10},{7,11},{20,24},{21,25},{22,26},{23,27}} | collective-permute-start | bytes 393224 | tf_op jit(solution)/shard_map/ppermute | solution.py:557
  37.8 0.0 collective-permute-done.2
  37.8 0.2 fusion.1
  38.0 0.8 %collective-permute-start.6 = (bf16[4,128,128]{2,1,0:T(8,128)(2,1)S(1)}, bf16[4,128,128]{2,1,0:T(8,128)(2,1)S(1)}, u32[]{:S(2)}, u32[]{:S(2)}) collective-permute-start(bf16[4,128,128]{2,1,0:T(8,128)(2,1)S(1)} %fusion.1), channel_id=1, source_target_pairs={{8,12},{9,13},{10,14},{11,15},{24,28},{25,29},{26,30},{27,31}} | collective-permute-start | bytes 393224 | tf_op jit(solution)/shard_map/ppermute | solution.py:557
  38.8 0.0 copy-start.3
  38.9 4.5 %rows_pass.3 = (bf16[1024,512]{1,0:T(8,128)(2,1)S(1)}, bf16[1024,512]{1,0:T(8,128)(2,1)S(1)}) custom-call(bf16[1024,512]{1,0:T(8,128)(2,1)S(1)} %copy-done.2, bf16[16,2048]{1,0:T(8,128)(2,1)S(1)} %collective-permute-done.refs_2_.refs_3_.refs_1_, bf16[4,512]{1,0:T(4,128)(2,1)S(1)} %copy-done.8, bf16[1024,256]{1,0:T(8,128)(2,1)S(1)} %get-tuple-element.24.refs_3_, ...), custom_call_target="tpu_custom_call" | custom-call | flops 4096000000 | bytes 8388608 | tf_op jit(solution)/shard_map/rows_pass/pallas_call | solution.py:457
  43.4 0.0 collective-permute-done.4
  43.4 0.2 fusion.3
  43.6 0.7 %collective-permute-start.5 = (bf16[4,128,128]{2,1,0:T(8,128)(2,1)S(1)}, bf16[4,128,128]{2,1,0:T(8,128)(2,1)S(1)}, u32[]{:S(2)}, u32[]{:S(2)}) collective-permute-start(bf16[4,128,128]{2,1,0:T(8,128)(2,1)S(1)} %fusion.3), channel_id=1, source_target_pairs={{8,12},{9,13},{10,14},{11,15},{24,28},{25,29},{26,30},{27,31}} | collective-permute-start | bytes 393224 | tf_op jit(solution)/shard_map/ppermute | solution.py:557
  44.4 0.0 collective-permute-done.6.refs_3_
  44.4 0.0 copy-done.3
  44.4 1.9 %final_pass.2.refs_5_ = bf16[1024,1024]{1,0:T(8,128)(2,1)} custom-call(bf16[1024,512]{1,0:T(8,128)(2,1)S(1)} %get-tuple-element.41.refs_0_, bf16[1024,512]{1,0:T(8,128)(2,1)S(1)} %get-tuple-element.34.refs_1_, bf16[4,128,128]{2,1,0:T(8,128)(2,1)S(1)} %add.23.refs_2_, bf16[4,128,128]{2,1,0:T(8,128)(2,1)S(1)} %collective-permute-done.6.refs_3_, ...), custom_call_target="tpu_custom_call" | custom-call | tf_op jit(solution)/shard_map/final_pass/pallas_call | solution.py:523
  46.3 0.0 collective-permute-done.5.refs_3_
  46.3 1.9 %final_pass.3 = bf16[1024,1024]{1,0:T(8,128)(2,1)} custom-call(bf16[1024,512]{1,0:T(8,128)(2,1)S(1)} %get-tuple-element.38.refs_0_, bf16[1024,512]{1,0:T(8,128)(2,1)S(1)} %get-tuple-element.39.refs_1_, bf16[4,128,128]{2,1,0:T(8,128)(2,1)S(1)} %add.21.refs_2_, ...), custom_call_target="tpu_custom_call", output_to_operand_aliasing={{}: (5, {})} | custom-call | tf_op jit(solution)/shard_map/final_pass/pallas_call | solution.py:523
  (4 shorter events, 0.1 us)
Async XLA Ops:
  0.0 8.7 %copy-start = (bf16[1024,1024]{1,0:T(8,128)(2,1)S(1)}, bf16[1024,1024]{1,0:T(8,128)(2,1)}, u32[]{:S(2)}) copy-start(bf16[1024,1024]{1,0:T(8,128)(2,1)} %refs_1_.3) | copy-start | bytes 6291460
  0.0 8.7 %copy-start.1 = (bf16[1024,512]{1,0:T(8,128)(2,1)S(1)}, bf16[1024,512]{1,0:T(8,128)(2,1)}, u32[]{:S(2)}) copy-start(bf16[1024,512]{1,0:T(8,128)(2,1)} %refs_0_.5) | copy-start | bytes 3145732
  0.0 8.7 %copy-start.6 = (bf16[4,1024]{1,0:T(4,128)(2,1)S(1)}, bf16[4,1024]{1,0:T(4,128)(2,1)}, u32[]{:S(2)}) copy-start(bf16[4,1024]{1,0:T(4,128)(2,1)} %refs_5_.3) | copy-start | bytes 24580
  0.0 8.7 %copy-start.7 = (bf16[4,512]{1,0:T(4,128)(2,1)S(1)}, bf16[4,512]{1,0:T(4,128)(2,1)}, u32[]{:S(2)}) copy-start(bf16[4,512]{1,0:T(4,128)(2,1)} %refs_4_.3) | copy-start | bytes 12292
  0.0 8.8 %copy-start.5 = (f32[1024,8]{0,1:T(8,128)S(1)}, f32[1024,8]{0,1:T(8,128)}, u32[]{:S(2)}) copy-start(f32[1024,8]{0,1:T(8,128)} %param.16) | copy-start | bytes 98308
  0.0 8.8 %copy-start.4 = (f32[1024,8]{0,1:T(8,128)S(1)}, f32[1024,8]{0,1:T(8,128)}, u32[]{:S(2)}) copy-start(f32[1024,8]{0,1:T(8,128)} %param.15) | copy-start | bytes 98308
  1.6 7.1 %collective-permute-start = (bf16[16,2048]{1,0:T(8,128)(2,1)}, bf16[16,2048]{1,0:T(8,128)(2,1)S(1)}, u32[]{:S(2)}, u32[]{:S(2)}) collective-permute-start(bf16[16,2048]{1,0:T(8,128)(2,1)} %pack_rim.1), channel_id=1, source_target_pairs={{0,4},{4,8},{8,12},{1,5},{5,9},{9,13},{2,6},{6,10},{10,14},{3,7},{... | collective-permute-start | bytes 196616 | tf_op jit(solution)/shard_map/ppermute | solution.py:539
  17.3 15.0 %copy-start.2 = (bf16[1024,512]{1,0:T(8,128)(2,1)S(1)}, bf16[1024,512]{1,0:T(8,128)(2,1)}, u32[]{:S(2)}) copy-start(bf16[1024,512]{1,0:T(8,128)(2,1)} %refs_0_.7) | copy-start | bytes 3145732
  17.3 15.0 %copy-start.8 = (bf16[4,512]{1,0:T(4,128)(2,1)S(1)}, bf16[4,512]{1,0:T(4,128)(2,1)}, u32[]{:S(2)}) copy-start(bf16[4,512]{1,0:T(4,128)(2,1)} %refs_2_.3) | copy-start | bytes 12292
  17.3 14.1 %collective-permute-start.1 = (bf16[4,128,128]{2,1,0:T(8,128)(2,1)S(1)}, bf16[4,128,128]{2,1,0:T(8,128)(2,1)S(1)}, u32[]{:S(2)}, u32[]{:S(2)}) collective-permute-start(bf16[4,128,128]{2,1,0:T(8,128)(2,1)S(1)} %convert_element_type.18), channel_id=1, source_target_pairs={{0,4},{1,5},{2,6},{3,7},{16,20},{17,21},{18,22},{19,23}} | collective-permute-start | bytes 393224 | tf_op jit(solution)/shard_map/ppermute | solution.py:557
  30.2 6.8 %collective-permute-start.3 = (bf16[4,128,128]{2,1,0:T(8,128)(2,1)S(1)}, bf16[4,128,128]{2,1,0:T(8,128)(2,1)S(1)}, u32[]{:S(2)}, u32[]{:S(2)}) collective-permute-start(bf16[4,128,128]{2,1,0:T(8,128)(2,1)S(1)} %convert_element_type.21), channel_id=1, source_target_pairs={{0,4},{1,5},{2,6},{3,7},{16,20},{17,21},{18,22},{19,23}} | collective-permute-start | bytes 393224 | tf_op jit(solution)/shard_map/ppermute | solution.py:557
  31.7 6.1 %collective-permute-start.2 = (bf16[4,128,128]{2,1,0:T(8,128)(2,1)S(1)}, bf16[4,128,128]{2,1,0:T(8,128)(2,1)S(1)}, u32[]{:S(2)}, u32[]{:S(2)}) collective-permute-start(bf16[4,128,128]{2,1,0:T(8,128)(2,1)S(1)} %fusion), channel_id=1, source_target_pairs={{4,8},{5,9},{6,10},{7,11},{20,24},{21,25},{22,26},{23,27}} | collective-permute-start | bytes 393224 | tf_op jit(solution)/shard_map/ppermute | solution.py:557
  37.1 6.3 %collective-permute-start.4 = (bf16[4,128,128]{2,1,0:T(8,128)(2,1)S(1)}, bf16[4,128,128]{2,1,0:T(8,128)(2,1)S(1)}, u32[]{:S(2)}, u32[]{:S(2)}) collective-permute-start(bf16[4,128,128]{2,1,0:T(8,128)(2,1)S(1)} %fusion.2), channel_id=1, source_target_pairs={{4,8},{5,9},{6,10},{7,11},{20,24},{21,25},{22,26},{23,27}} | collective-permute-start | bytes 393224 | tf_op jit(solution)/shard_map/ppermute | solution.py:557
  38.0 6.4 %collective-permute-start.6 = (bf16[4,128,128]{2,1,0:T(8,128)(2,1)S(1)}, bf16[4,128,128]{2,1,0:T(8,128)(2,1)S(1)}, u32[]{:S(2)}, u32[]{:S(2)}) collective-permute-start(bf16[4,128,128]{2,1,0:T(8,128)(2,1)S(1)} %fusion.1), channel_id=1, source_target_pairs={{8,12},{9,13},{10,14},{11,15},{24,28},{25,29},{26,30},{27,31}} | collective-permute-start | bytes 393224 | tf_op jit(solution)/shard_map/ppermute | solution.py:557
  38.8 5.5 %copy-start.3 = (f32[128]{0:T(128)S(1)}, f32[128]{0:T(128)}, u32[]{:S(2)}) copy-start(f32[128]{0:T(128)} %param.17) | copy-start | bytes 1540
  43.6 2.7 %collective-permute-start.5 = (bf16[4,128,128]{2,1,0:T(8,128)(2,1)S(1)}, bf16[4,128,128]{2,1,0:T(8,128)(2,1)S(1)}, u32[]{:S(2)}, u32[]{:S(2)}) collective-permute-start(bf16[4,128,128]{2,1,0:T(8,128)(2,1)S(1)} %fusion.3), channel_id=1, source_target_pairs={{8,12},{9,13},{10,14},{11,15},{24,28},{25,29},{26,30},{27,31}} | collective-permute-start | bytes 393224 | tf_op jit(solution)/shard_map/ppermute | solution.py:557

commit v4 on v3

--- a/solution.py
+++ b/solution.py
@@ -21,6 +21,7 @@
 F32 = jnp.float32
 BF16 = jnp.bfloat16
 WIDE = DK + DV
+VMEM = pl.BlockSpec(memory_space=pltpu.VMEM)
 
 
 def dot(left, right):
@@ -174,11 +175,11 @@
 def memory_kernel(
     kheads,
     vheads,
-    first_head,
+    part,
+    span,
     key_ref,
     value_ref,
-    rim_key_ref,
-    rim_value_ref,
+    rim_ref,
     tap_key_ref,
     tap_value_ref,
     gate_ref,
@@ -199,10 +200,15 @@
     step = pl.program_id(0)
     last_step = pl.num_programs(0) - 1
     ratio = vheads // kheads
-    span = key_ref.shape[0]
     tiles = kheads + vheads
     parts = span // CHUNK
-    places = [(part, head) for part in range(parts) for head in range(vheads)]
+    first_head = part * vheads
+    base = pl.multiple_of(step * span, span)
+    now_rows = pl.ds(base, span)
+    key_from = part * kheads * DK
+    value_from = part * vheads * DV
+    rim_from = (key_ref.shape[1] + key_from, 2 * key_ref.shape[1] + value_from)
+    places = [(chunk, head) for chunk in range(parts) for head in range(vheads)]
 
     def set_up():
         fill_masks(diag_ref)
@@ -210,8 +216,8 @@
         for head in range(vheads):
             state[head] = (rows == cols).astype(F32)
         for tile in range(tiles):
-            ref, at = (rim_key_ref, tile) if tile < kheads else (rim_value_ref, tile - kheads)
-            wide[tile, 0:HALO] = ref[:, at * 128 : (at + 1) * 128].astype(F32)[RIM - HALO :]
+            at = rim_from[0] + tile * DK if tile < kheads else rim_from[1] + (tile - kheads) * DV
+            wide[tile, 0:HALO] = rim_ref[:, at : at + 128].astype(F32)[RIM - HALO :]
 
     def prepare():
         tap_key = tap_key_ref[...].astype(F32) * 0.5
@@ -219,36 +225,37 @@
         keys = []
         for tile in range(kheads):
             at = slice(tile * DK, (tile + 1) * DK)
-            keys.append(unit(conv(key_ref[:, at], wide, tile, tap_key[:, at]), 1.0))
-            unit_ref[:, at] = keys[tile]
+            place = slice(key_from + tile * DK, key_from + (tile + 1) * DK)
+            keys.append(unit(conv(key_ref[now_rows, place], wide, tile, tap_key[:, place]), 1.0))
+            unit_ref[now_rows, at] = keys[tile]
         for tile in range(vheads):
-            at = slice(tile * DV, (tile + 1) * DV)
-            value = conv(value_ref[:, at], wide, kheads + tile, tap_value[:, at])
-            for part in range(parts):
-                right_ref[part * vheads + tile, :, DK:] = value[
-                    part * CHUNK : (part + 1) * CHUNK
+            place = slice(value_from + tile * DV, value_from + (tile + 1) * DV)
+            value = conv(value_ref[now_rows, place], wide, kheads + tile, tap_value[:, place])
+            for chunk in range(parts):
+                right_ref[chunk * vheads + tile, :, DK:] = value[
+                    chunk * CHUNK : (chunk + 1) * CHUNK
                 ]
         for tile in range(tiles):
             wide[tile, 0:HALO] = wide[tile, span : span + HALO]
         rows, cols = iotas((CHUNK, CHUNK))
         strict = rows > cols
-        cums = sums(gate_ref[...] * LOG2E, span)
-        strengths = log_weights(logit_ref[...])
-        for part in range(parts):
-            here = slice(part * CHUNK, (part + 1) * CHUNK)
-            cum_flat = cums[part]
+        cums = sums(gate_ref[:, now_rows] * LOG2E, span)
+        strengths = log_weights(logit_ref[:, now_rows])
+        for chunk in range(parts):
+            here = slice(chunk * CHUNK, (chunk + 1) * CHUNK)
+            cum_flat = cums[chunk]
             cum = cum_flat.T
             lift = strengths[:, here] - cum_flat
             last = cum_flat[:, CHUNK - 1 :]
             ends = jnp.exp2(last + lift)
-            sum_ref[part] = jnp.broadcast_to(jnp.exp2(last), cum_flat.shape)
+            sum_ref[chunk] = jnp.broadcast_to(jnp.exp2(last), cum_flat.shape)
             for khead in range(kheads):
                 key = keys[khead][here]
                 flat = (-key).T
                 gram = dot(key, flat)
                 for which in range(ratio):
                     head = khead * ratio + which
-                    item = part * vheads + head
+                    item = chunk * vheads + head
                     place = first_head + head
                     cum_col = jnp.broadcast_to(cum[:, place : place + 1], (CHUNK, CHUNK))
                     powers = cum_col + lift[place : place + 1]
@@ -273,18 +280,18 @@
         ]
         lows = [dot(f[:, HALF:], rest).astype(BF16) for f, rest in zip(found, rests)]
         erases, writes = [], []
-        for item, (part, head) in enumerate(places):
+        for item, (chunk, head) in enumerate(places):
             there = slice(head * WIDE, (head + 1) * WIDE)
             solved = jnp.concatenate([tops[item], lows[item]], axis=0)
-            solved_ref[part * CHUNK : (part + 1) * CHUNK, there] = solved
+            solved_ref[pl.ds(base + chunk * CHUNK, CHUNK), there] = solved
             product = dot(tail_ref[item], solved)
             erases.append(product[:, :DK].astype(BF16))
             writes.append(product[:, DK:])
-        for item, (part, head) in enumerate(places):
+        for item, (chunk, head) in enumerate(places):
             now = state[head]
             short = now.astype(BF16)
-            before_ref[part, head] = short
-            tail = sum_ref[part, first_head + head : first_head + head + 1]
+            before_ref[step * parts + chunk, head] = short
+            tail = sum_ref[chunk, first_head + head : first_head + head + 1]
             change = dot(erases[item], short)
             state[head, :, :DK] = now[:, :DK] * tail + change[:, :DK]
             state[head, :, DK:] = now[:, DK:] * tail + (change[:, DK:] - writes[item])
@@ -314,42 +321,15 @@
     items = span // CHUNK * vheads
     blocks = tok_count // span
     count = len(levels())
-    rim_key = PARTS + part
-    rim_value = (2 * all_kheads) // vheads + part
-
-    def ahead(width, column):
-        return pl.BlockSpec((span, width), lambda i: (i, column))
-
-    def fixed(shape, *place):
-        return pl.BlockSpec(shape, lambda i: place)
-
-    flat = pl.BlockSpec((all_vheads, span), lambda i: (0, i))
 
     def kernel(*refs):
-        memory_kernel(kheads, vheads, part * vheads, *refs)
+        memory_kernel(kheads, vheads, part, span, *refs)
 
     return pl.pallas_call(
         kernel,
         grid=(blocks,),
-        in_specs=[
-            ahead(kheads * DK, part),
-            ahead(vheads * DV, part),
-            fixed((RIM, kheads * DK), 0, rim_key),
-            fixed((RIM, vheads * DV), 0, rim_value),
-            fixed((KW, kheads * DK), 0, part),
-            fixed((KW, vheads * DV), 0, part),
-            flat,
-            flat,
-        ],
-        out_specs=[
-            ahead(kheads * DK, 0),
-            pl.BlockSpec((span, vheads * WIDE), lambda i: (i, 0)),
-            pl.BlockSpec(
-                (span // CHUNK, vheads, DK, WIDE), lambda i: (i, 0, 0, 0)
-            ),
-            fixed((vheads, DK, DK), 0, 0, 0),
-            fixed((vheads, DK, DV), 0, 0, 0),
-        ],
+        in_specs=[VMEM] * 7,
+        out_specs=[VMEM] * 5,
         out_shape=[
             jax.ShapeDtypeStruct((tok_count, kheads * DK), BF16),
             jax.ShapeDtypeStruct((tok_count, vheads * WIDE), BF16),
@@ -366,18 +346,19 @@
             pltpu.VMEM((items, CHUNK, WIDE), BF16),
             pltpu.VMEM((span // CHUNK, all_vheads, CHUNK), F32),
         ],
-        compiler_params=pltpu.CompilerParams(vmem_limit_bytes=40 * 1024 * 1024),
+        compiler_params=pltpu.CompilerParams(vmem_limit_bytes=20 * 1024 * 1024),
         cost_estimate=pl.CostEstimate(
             flops=2 * tok_count * vheads * 1000 * 1000, bytes_accessed=1 << 23, transcendentals=0
         ),
         name="memory_pass",
-    )(key_raw, value_raw, rim, rim, conv_key, conv_value, gate_flat, logit_flat)
+    )(key_raw, value_raw, rim, conv_key, conv_value, gate_flat, logit_flat)
 
 
 def rows_kernel(
     kheads,
     vheads,
-    first_head,
+    group,
+    span,
     query_ref,
     rim_ref,
     tap_ref,
@@ -392,12 +373,16 @@
 ):
     step = pl.program_id(0)
     ratio = vheads // kheads
-    span = query_ref.shape[0]
+    first_head = group * vheads
+    base = pl.multiple_of(step * span, span)
+    now_rows = pl.ds(base, span)
+    query_from = group * kheads * DK
 
     @pl.when(step == 0)
     def _():
         for tile in range(kheads):
-            wide[tile, 0:HALO] = rim_ref[:, tile * DK : (tile + 1) * DK].astype(F32)[RIM - HALO :]
+            at = slice(query_from + tile * DK, query_from + (tile + 1) * DK)
+            wide[tile, 0:HALO] = rim_ref[:, at].astype(F32)[RIM - HALO :]
 
     @pl.when(step > 0)
     def _():
@@ -407,15 +392,16 @@
     taps = tap_ref[...].astype(F32) * 0.5
     queries = []
     for tile in range(kheads):
-        at = slice(tile * DK, (tile + 1) * DK)
-        queries.append(unit(conv(query_ref[:, at], wide, tile, taps[:, at]), DK**-0.5))
+        at = slice(query_from + tile * DK, query_from + (tile + 1) * DK)
+        queries.append(unit(conv(query_ref[now_rows, at], wide, tile, taps[:, at]), DK**-0.5))
 
     rows, cols = iotas((CHUNK, CHUNK))
     lower = rows >= cols
-    cums = sums(gate_ref[...] * LOG2E, span)
-    strengths = log_weights(logit_ref[...])
+    cums = sums(gate_ref[:, now_rows] * LOG2E, span)
+    strengths = log_weights(logit_ref[:, now_rows])
     for part in range(span // CHUNK):
         here = slice(part * CHUNK, (part + 1) * CHUNK)
+        place_rows = pl.ds(base + part * CHUNK, CHUNK)
         cum_flat = cums[part]
         cum = cum_flat.T
         lift = strengths[:, here] - cum_flat
@@ -423,7 +409,7 @@
             query = queries[khead][here]
             gram = lax.dot_general(
                 query,
-                key_ref[here, khead * DK : (khead + 1) * DK],
+                key_ref[place_rows, khead * DK : (khead + 1) * DK],
                 (((1,), (1,)), ((), ())),
                 preferred_element_type=F32,
             )
@@ -434,11 +420,11 @@
                 cum_col = jnp.broadcast_to(cum[:, place : place + 1], (CHUNK, CHUNK))
                 powers = cum_col + lift[place : place + 1]
                 scores = (gram * jnp.exp2(jnp.where(lower, powers, -jnp.inf))).astype(BF16)
-                product = dot(scores, solved_ref[here, head * WIDE : (head + 1) * WIDE])
+                product = dot(scores, solved_ref[place_rows, head * WIDE : (head + 1) * WIDE])
                 meet = query.astype(F32) * jnp.exp2(cum_col) - product[:, :DK]
-                final = dot(meet.astype(BF16), before_ref[part, head])
-                rows_ref[here, there] = final[:, :DK].astype(BF16)
-                local_ref[here, there] = (final[:, DK:] + product[:, DK:]).astype(BF16)
+                final = dot(meet.astype(BF16), before_ref[step * (span // CHUNK) + part, head])
+                rows_ref[place_rows, there] = final[:, :DK].astype(BF16)
+                local_ref[place_rows, there] = (final[:, DK:] + product[:, DK:]).astype(BF16)
 
 
 def rows_pass(part, query_raw, rim, conv_query, keys, gate_flat, logit_flat, solved, before):
@@ -448,32 +434,20 @@
     vheads = all_vheads // PARTS
     span = min(SPAN_Y, tok_count)
 
-    def along(width, column):
-        return pl.BlockSpec((span, width), lambda i: (i, column))
-
     def kernel(*refs):
-        rows_kernel(kheads, vheads, part * vheads, *refs)
+        rows_kernel(kheads, vheads, part, span, *refs)
 
     return pl.pallas_call(
         kernel,
         grid=(tok_count // span,),
-        in_specs=[
-            along(kheads * DK, part),
-            pl.BlockSpec((RIM, kheads * DK), lambda i: (0, part)),
-            pl.BlockSpec((KW, kheads * DK), lambda i: (0, part)),
-            along(kheads * DK, 0),
-            pl.BlockSpec((all_vheads, span), lambda i: (0, i)),
-            pl.BlockSpec((all_vheads, span), lambda i: (0, i)),
-            along(vheads * WIDE, 0),
-            pl.BlockSpec((span // CHUNK, vheads, DK, WIDE), lambda i: (i, 0, 0, 0)),
-        ],
-        out_specs=[along(vheads * DV, 0), along(vheads * DV, 0)],
+        in_specs=[VMEM] * 8,
+        out_specs=[VMEM] * 2,
         out_shape=[
             jax.ShapeDtypeStruct((tok_count, vheads * DV), BF16),
             jax.ShapeDtypeStruct((tok_count, vheads * DV), BF16),
         ],
         scratch_shapes=[pltpu.VMEM((kheads, span + HALO, 128), F32)],
-        compiler_params=pltpu.CompilerParams(vmem_limit_bytes=32 * 1024 * 1024),
+        compiler_params=pltpu.CompilerParams(vmem_limit_bytes=16 * 1024 * 1024),
         cost_estimate=pl.CostEstimate(
             flops=2 * tok_count * vheads * 1000 * 500, bytes_accessed=1 << 23, transcendentals=0
         ),
@@ -484,10 +458,12 @@
 def final_kernel(vheads, rows_ref, local_ref, early_ref, late_ref, gain_ref, *rest):
     out_ref = rest[-1]
     gain = gain_ref[...]
+    span = out_ref.shape[0]
+    now_rows = pl.ds(pl.multiple_of(pl.program_id(0) * span, span), span)
     for head in range(vheads):
         there = slice(head * DV, (head + 1) * DV)
         start = early_ref[head] + late_ref[head]
-        output = dot(rows_ref[:, there], start) + local_ref[:, there].astype(F32)
+        output = dot(rows_ref[now_rows, there], start) + local_ref[now_rows, there].astype(F32)
         square = output * output
         if head % 2:
             total = row_sums(square)
@@ -508,15 +484,8 @@
     def kernel(*refs):
         final_kernel(vheads, *refs)
 
-    whole = pl.BlockSpec((vheads, DK, DV), lambda i: (0, 0, 0))
     arrays = [rows, local, early, late, gain]
-    specs = [
-        along(vheads * DV, 0),
-        along(vheads * DV, 0),
-        whole,
-        whole,
-        pl.BlockSpec((1, DV), lambda i: (0, 0)),
-    ]
+    specs = [VMEM] * 5
     if earlier is not None:
         arrays.append(earlier)
         specs.append(pl.BlockSpec(memory_space=pl.ANY))
@@ -527,7 +496,7 @@
         out_specs=along(vheads * DV, part),
         out_shape=jax.ShapeDtypeStruct((tok_count, PARTS * vheads * DV), BF16),
         input_output_aliases={} if earlier is None else {5: 0},
-        compiler_params=pltpu.CompilerParams(vmem_limit_bytes=32 * 1024 * 1024),
+        compiler_params=pltpu.CompilerParams(vmem_limit_bytes=12 * 1024 * 1024),
         name="final_pass",
     )(*arrays)
 

time: 48.5 us -> 48.3 us (level)
  no operation moved by 1% of the time
where the time goes in v4:
time: 48.3 us; the launch traced here: 48.1 us
  Pallas kernels  31.5 us (65%)
  starting transfers between devices  13.2 us (27%)
  waiting for transfers between devices  2.22 us (5%)
  matrix products  0.72 us (1%)
    pallas_call x2, Pallas kernels, memory_pass(): pl.pallas_call(kernel, grid=(blocks,), in_specs=[VMEM] * 7, out_specs=[VM...  17.1 us
    pallas_call x2, Pallas kernels, rows_pass(): pl.pallas_call(kernel, grid=(tok_count // span,), in_specs=[VMEM] * 8, ou...  8.99 us
    ppermute x6, starting transfers between devices, send(): lax.ppermute(moved[part][source], 'ctx', [(source, source + 1)])  8.29 us
    ppermute x1, starting transfers between devices, shards(): lax.ppermute(pack_rim(query_raw, key_raw, value_raw), 'ctx', [(at, at + 1...  4.93 us
    pallas_call x2, Pallas kernels, final_pass(): pl.pallas_call(kernel, grid=(tok_count // span,), in_specs=specs, out_spe...  3.87 us
    ppermute x1, waiting for transfers between devices, shards(): lax.ppermute(pack_rim(query_raw, key_raw, value_raw), 'ctx', [(at, at + 1...  2.2 us
    pallas_call x1, Pallas kernels, pack_rim(): pl.pallas_call(rim_kernel, grid=(1,), in_specs=[pl.BlockSpec((RIM, width)...  1.58 us
  transfers between devices with their start and end apart: 7, of which 1 were waited for; matrix products, arithmetic and copies ran while one was open for 2% of the time, Pallas kernels for 40%

profile of v4, /device:TPU:0, one launch (start us, length us, event | category | flops | bytes accessed | tf_op | source)
XLA Modules:
  0.0 48.1 jit_solution(10338585086738521337)
XLA Ops:
  0.0 0.0 copy-start
  0.0 0.0 copy-start.1
  0.0 0.0 copy-start.6
  0.0 0.0 copy-start.7
  0.0 0.0 copy-start.5
  0.0 0.0 copy-start.4
  0.0 1.6 %pack_rim.1 = bf16[16,2048]{1,0:T(8,128)(2,1)} custom-call(bf16[1024,512]{1,0:T(8,128)(2,1)} %refs_0_.7, bf16[1024,512]{1,0:T(8,128)(2,1)} %refs_0_.5, bf16[1024,1024]{1,0:T(8,128)(2,1)} %refs_1_.3), custom_call_target="tpu_custom_call" | custom-call | tf_op jit(solution)/shard_map/pack_rim/pallas_call | solution.py:161
  1.6 4.9 %collective-permute-start = (bf16[16,2048]{1,0:T(8,128)(2,1)}, bf16[16,2048]{1,0:T(8,128)(2,1)S(1)}, u32[]{:S(2)}, u32[]{:S(2)}) collective-permute-start(bf16[16,2048]{1,0:T(8,128)(2,1)} %pack_rim.1), channel_id=1, source_target_pairs={{0,4},{4,8},{8,12},{1,5},{5,9},{9,13},{2,6},{6,10},{10,14},{3,7},{... | collective-permute-start | bytes 196616 | tf_op jit(solution)/shard_map/ppermute | solution.py:508
  6.5 2.2 %collective-permute-done.refs_2_.refs_1_ = bf16[16,2048]{1,0:T(8,128)(2,1)S(1)} collective-permute-done((bf16[16,2048]{1,0:T(8,128)(2,1)}, bf16[16,2048]{1,0:T(8,128)(2,1)S(1)}, u32[]{:S(2)}, u32[]{:S(2)}) %collective-permute-start) | collective-permute-done | bytes 65568 | tf_op jit(solution)/shard_map/ppermute | solution.py:508
  8.7 0.0 copy-done
  8.7 0.0 copy-done.1
  8.7 0.0 copy-done.6
  8.8 0.0 copy-done.7
  8.8 0.0 copy-done.5
  8.8 0.0 copy-done.4
  8.8 8.6 %memory_pass.3 = (bf16[1024,256]{1,0:T(8,128)(2,1)S(1)}, bf16[1024,1024]{1,0:T(8,128)(2,1)S(1)}, bf16[8,4,128,256]{3,2,1,0:T(8,128)(2,1)S(1)}, bf16[4,128,128]{2,1,0:T(8,128)(2,1)S(1)}, f32[4,128,128]{2,1,0:T(8,128)S(1)}) custom-call(bf16[1024,512]{1,0:T(8,128)(2,1)S(1)} %copy-done.1, bf16[1024,1024]{1,0:T(8,128)(2,1)S(1)} %copy-done, ...), custom_call_target="tpu_custom_call" | custom-call | flops 8192000000 | bytes 8388608 | tf_op jit(solution)/shard_map/memory_pass/pallas_call | solution.py:328
  17.4 0.0 copy-start.2
  17.4 0.0 copy-start.8
  17.4 4.3 %collective-permute-start.1 = (bf16[4,128,128]{2,1,0:T(8,128)(2,1)S(1)}, bf16[4,128,128]{2,1,0:T(8,128)(2,1)S(1)}, u32[]{:S(2)}, u32[]{:S(2)}) collective-permute-start(bf16[4,128,128]{2,1,0:T(8,128)(2,1)S(1)} %convert_element_type.18), channel_id=1, source_target_pairs={{0,4},{1,5},{2,6},{3,7},{16,20},{17,21},{18,22},{19,23}} | collective-permute-start | bytes 393224 | tf_op jit(solution)/shard_map/ppermute | solution.py:526
  21.7 8.5 %memory_pass.2 = (bf16[1024,256]{1,0:T(8,128)(2,1)S(1)}, bf16[1024,1024]{1,0:T(8,128)(2,1)S(1)}, bf16[8,4,128,256]{3,2,1,0:T(8,128)(2,1)S(1)}, bf16[4,128,128]{2,1,0:T(8,128)(2,1)S(1)}, f32[4,128,128]{2,1,0:T(8,128)S(1)}) custom-call(bf16[1024,512]{1,0:T(8,128)(2,1)S(1)} %copy-done.1, bf16[1024,1024]{1,0:T(8,128)(2,1)S(1)} %copy-done, ...), custom_call_target="tpu_custom_call" | custom-call | flops 8192000000 | bytes 8388608 | tf_op jit(solution)/shard_map/memory_pass/pallas_call | solution.py:328
  30.3 1.3 %collective-permute-start.3 = (bf16[4,128,128]{2,1,0:T(8,128)(2,1)S(1)}, bf16[4,128,128]{2,1,0:T(8,128)(2,1)S(1)}, u32[]{:S(2)}, u32[]{:S(2)}) collective-permute-start(bf16[4,128,128]{2,1,0:T(8,128)(2,1)S(1)} %convert_element_type.21), channel_id=1, source_target_pairs={{0,4},{1,5},{2,6},{3,7},{16,20},{17,21},{18,22},{19,23}} | collective-permute-start | bytes 393224 | tf_op jit(solution)/shard_map/ppermute | solution.py:526
  31.6 0.0 collective-permute-done.1
  31.6 0.2 fusion
  31.8 0.7 %collective-permute-start.2 = (bf16[4,128,128]{2,1,0:T(8,128)(2,1)S(1)}, bf16[4,128,128]{2,1,0:T(8,128)(2,1)S(1)}, u32[]{:S(2)}, u32[]{:S(2)}) collective-permute-start(bf16[4,128,128]{2,1,0:T(8,128)(2,1)S(1)} %fusion), channel_id=1, source_target_pairs={{4,8},{5,9},{6,10},{7,11},{20,24},{21,25},{22,26},{23,27}} | collective-permute-start | bytes 393224 | tf_op jit(solution)/shard_map/ppermute | solution.py:526
  32.5 0.0 copy-done.2
  32.5 0.0 copy-done.8
  32.5 4.5 %rows_pass.2 = (bf16[1024,512]{1,0:T(8,128)(2,1)S(1)}, bf16[1024,512]{1,0:T(8,128)(2,1)S(1)}) custom-call(bf16[1024,512]{1,0:T(8,128)(2,1)S(1)} %copy-done.2, bf16[16,2048]{1,0:T(8,128)(2,1)S(1)} %collective-permute-done.refs_2_.refs_1_, bf16[4,512]{1,0:T(4,128)(2,1)S(1)} %copy-done.8, bf16[1024,256]{1,0:T(8,128)(2,1)S(1)} %get-tuple-element.30.refs_3_, ...), custom_call_target="tpu_custom_call" | custom-call | flops 4096000000 | bytes 8388608 | tf_op jit(solution)/shard_map/rows_pass/pallas_call | solution.py:440
  37.0 0.0 collective-permute-done.3
  37.0 0.2 fusion.2
  37.2 0.7 %collective-permute-start.4 = (bf16[4,128,128]{2,1,0:T(8,128)(2,1)S(1)}, bf16[4,128,128]{2,1,0:T(8,128)(2,1)S(1)}, u32[]{:S(2)}, u32[]{:S(2)}) collective-permute-start(bf16[4,128,128]{2,1,0:T(8,128)(2,1)S(1)} %fusion.2), channel_id=1, source_target_pairs={{4,8},{5,9},{6,10},{7,11},{20,24},{21,25},{22,26},{23,27}} | collective-permute-start | bytes 393224 | tf_op jit(solution)/shard_map/ppermute | solution.py:526
  37.9 0.0 collective-permute-done.2
  37.9 0.2 fusion.1
  38.1 0.7 %collective-permute-start.6 = (bf16[4,128,128]{2,1,0:T(8,128)(2,1)S(1)}, bf16[4,128,128]{2,1,0:T(8,128)(2,1)S(1)}, u32[]{:S(2)}, u32[]{:S(2)}) collective-permute-start(bf16[4,128,128]{2,1,0:T(8,128)(2,1)S(1)} %fusion.1), channel_id=1, source_target_pairs={{8,12},{9,13},{10,14},{11,15},{24,28},{25,29},{26,30},{27,31}} | collective-permute-start | bytes 393224 | tf_op jit(solution)/shard_map/ppermute | solution.py:526
  38.7 0.0 copy-start.3
  38.8 4.5 %rows_pass.3 = (bf16[1024,512]{1,0:T(8,128)(2,1)S(1)}, bf16[1024,512]{1,0:T(8,128)(2,1)S(1)}) custom-call(bf16[1024,512]{1,0:T(8,128)(2,1)S(1)} %copy-done.2, bf16[16,2048]{1,0:T(8,128)(2,1)S(1)} %collective-permute-done.refs_2_.refs_1_, bf16[4,512]{1,0:T(4,128)(2,1)S(1)} %copy-done.8, bf16[1024,256]{1,0:T(8,128)(2,1)S(1)} %get-tuple-element.24.refs_3_, ...), custom_call_target="tpu_custom_call" | custom-call | flops 4096000000 | bytes 8388608 | tf_op jit(solution)/shard_map/rows_pass/pallas_call | solution.py:440
  43.3 0.0 collective-permute-done.4
  43.3 0.2 fusion.3
  43.5 0.7 %collective-permute-start.5 = (bf16[4,128,128]{2,1,0:T(8,128)(2,1)S(1)}, bf16[4,128,128]{2,1,0:T(8,128)(2,1)S(1)}, u32[]{:S(2)}, u32[]{:S(2)}) collective-permute-start(bf16[4,128,128]{2,1,0:T(8,128)(2,1)S(1)} %fusion.3), channel_id=1, source_target_pairs={{8,12},{9,13},{10,14},{11,15},{24,28},{25,29},{26,30},{27,31}} | collective-permute-start | bytes 393224 | tf_op jit(solution)/shard_map/ppermute | solution.py:526
  44.2 0.0 collective-permute-done.6.refs_3_
  44.2 0.0 copy-done.3
  44.3 1.9 %final_pass.2.refs_5_ = bf16[1024,1024]{1,0:T(8,128)(2,1)} custom-call(bf16[1024,512]{1,0:T(8,128)(2,1)S(1)} %get-tuple-element.41.refs_0_, bf16[1024,512]{1,0:T(8,128)(2,1)S(1)} %get-tuple-element.34.refs_1_, bf16[4,128,128]{2,1,0:T(8,128)(2,1)S(1)} %add.23.refs_2_, bf16[4,128,128]{2,1,0:T(8,128)(2,1)S(1)} %collective-permute-done.6.refs_3_, ...), custom_call_target="tpu_custom_call" | custom-call | tf_op jit(solution)/shard_map/final_pass/pallas_call | solution.py:492
  46.2 0.0 collective-permute-done.5.refs_3_
  46.2 1.9 %final_pass.3 = bf16[1024,1024]{1,0:T(8,128)(2,1)} custom-call(bf16[1024,512]{1,0:T(8,128)(2,1)S(1)} %get-tuple-element.38.refs_0_, bf16[1024,512]{1,0:T(8,128)(2,1)S(1)} %get-tuple-element.39.refs_1_, bf16[4,128,128]{2,1,0:T(8,128)(2,1)S(1)} %add.21.refs_2_, ...), custom_call_target="tpu_custom_call", output_to_operand_aliasing={{}: (5, {})} | custom-call | tf_op jit(solution)/shard_map/final_pass/pallas_call | solution.py:492
  (4 shorter events, 0.1 us)
Async XLA Ops:
  0.0 8.7 %copy-start = (bf16[1024,1024]{1,0:T(8,128)(2,1)S(1)}, bf16[1024,1024]{1,0:T(8,128)(2,1)}, u32[]{:S(2)}) copy-start(bf16[1024,1024]{1,0:T(8,128)(2,1)} %refs_1_.3) | copy-start | bytes 6291460
  0.0 8.7 %copy-start.1 = (bf16[1024,512]{1,0:T(8,128)(2,1)S(1)}, bf16[1024,512]{1,0:T(8,128)(2,1)}, u32[]{:S(2)}) copy-start(bf16[1024,512]{1,0:T(8,128)(2,1)} %refs_0_.5) | copy-start | bytes 3145732
  0.0 8.7 %copy-start.6 = (bf16[4,1024]{1,0:T(4,128)(2,1)S(1)}, bf16[4,1024]{1,0:T(4,128)(2,1)}, u32[]{:S(2)}) copy-start(bf16[4,1024]{1,0:T(4,128)(2,1)} %refs_4_.3) | copy-start | bytes 24580
  0.0 8.7 %copy-start.7 = (bf16[4,512]{1,0:T(4,128)(2,1)S(1)}, bf16[4,512]{1,0:T(4,128)(2,1)}, u32[]{:S(2)}) copy-start(bf16[4,512]{1,0:T(4,128)(2,1)} %refs_3_.3) | copy-start | bytes 12292
  0.0 8.8 %copy-start.5 = (f32[1024,8]{0,1:T(8,128)S(1)}, f32[1024,8]{0,1:T(8,128)}, u32[]{:S(2)}) copy-start(f32[1024,8]{0,1:T(8,128)} %param.16) | copy-start | bytes 98308
  0.0 8.8 %copy-start.4 = (f32[1024,8]{0,1:T(8,128)S(1)}, f32[1024,8]{0,1:T(8,128)}, u32[]{:S(2)}) copy-start(f32[1024,8]{0,1:T(8,128)} %param.15) | copy-start | bytes 98308
  1.6 7.1 %collective-permute-start = (bf16[16,2048]{1,0:T(8,128)(2,1)}, bf16[16,2048]{1,0:T(8,128)(2,1)S(1)}, u32[]{:S(2)}, u32[]{:S(2)}) collective-permute-start(bf16[16,2048]{1,0:T(8,128)(2,1)} %pack_rim.1), channel_id=1, source_target_pairs={{0,4},{4,8},{8,12},{1,5},{5,9},{9,13},{2,6},{6,10},{10,14},{3,7},{... | collective-permute-start | bytes 196616 | tf_op jit(solution)/shard_map/ppermute | solution.py:508
  17.4 15.1 %copy-start.2 = (bf16[1024,512]{1,0:T(8,128)(2,1)S(1)}, bf16[1024,512]{1,0:T(8,128)(2,1)}, u32[]{:S(2)}) copy-start(bf16[1024,512]{1,0:T(8,128)(2,1)} %refs_0_.7) | copy-start | bytes 3145732
  17.4 15.1 %copy-start.8 = (bf16[4,512]{1,0:T(4,128)(2,1)S(1)}, bf16[4,512]{1,0:T(4,128)(2,1)}, u32[]{:S(2)}) copy-start(bf16[4,512]{1,0:T(4,128)(2,1)} %refs_2_.3) | copy-start | bytes 12292
  17.4 14.2 %collective-permute-start.1 = (bf16[4,128,128]{2,1,0:T(8,128)(2,1)S(1)}, bf16[4,128,128]{2,1,0:T(8,128)(2,1)S(1)}, u32[]{:S(2)}, u32[]{:S(2)}) collective-permute-start(bf16[4,128,128]{2,1,0:T(8,128)(2,1)S(1)} %convert_element_type.18), channel_id=1, source_target_pairs={{0,4},{1,5},{2,6},{3,7},{16,20},{17,21},{18,22},{19,23}} | collective-permute-start | bytes 393224 | tf_op jit(solution)/shard_map/ppermute | solution.py:526
  30.3 6.7 %collective-permute-start.3 = (bf16[4,128,128]{2,1,0:T(8,128)(2,1)S(1)}, bf16[4,128,128]{2,1,0:T(8,128)(2,1)S(1)}, u32[]{:S(2)}, u32[]{:S(2)}) collective-permute-start(bf16[4,128,128]{2,1,0:T(8,128)(2,1)S(1)} %convert_element_type.21), channel_id=1, source_target_pairs={{0,4},{1,5},{2,6},{3,7},{16,20},{17,21},{18,22},{19,23}} | collective-permute-start | bytes 393224 | tf_op jit(solution)/shard_map/ppermute | solution.py:526
  31.8 6.1 %collective-permute-start.2 = (bf16[4,128,128]{2,1,0:T(8,128)(2,1)S(1)}, bf16[4,128,128]{2,1,0:T(8,128)(2,1)S(1)}, u32[]{:S(2)}, u32[]{:S(2)}) collective-permute-start(bf16[4,128,128]{2,1,0:T(8,128)(2,1)S(1)} %fusion), channel_id=1, source_target_pairs={{4,8},{5,9},{6,10},{7,11},{20,24},{21,25},{22,26},{23,27}} | collective-permute-start | bytes 393224 | tf_op jit(solution)/shard_map/ppermute | solution.py:526
  37.2 6.1 %collective-permute-start.4 = (bf16[4,128,128]{2,1,0:T(8,128)(2,1)S(1)}, bf16[4,128,128]{2,1,0:T(8,128)(2,1)S(1)}, u32[]{:S(2)}, u32[]{:S(2)}) collective-permute-start(bf16[4,128,128]{2,1,0:T(8,128)(2,1)S(1)} %fusion.2), channel_id=1, source_target_pairs={{4,8},{5,9},{6,10},{7,11},{20,24},{21,25},{22,26},{23,27}} | collective-permute-start | bytes 393224 | tf_op jit(solution)/shard_map/ppermute | solution.py:526
  38.1 6.2 %collective-permute-start.6 = (bf16[4,128,128]{2,1,0:T(8,128)(2,1)S(1)}, bf16[4,128,128]{2,1,0:T(8,128)(2,1)S(1)}, u32[]{:S(2)}, u32[]{:S(2)}) collective-permute-start(bf16[4,128,128]{2,1,0:T(8,128)(2,1)S(1)} %fusion.1), channel_id=1, source_target_pairs={{8,12},{9,13},{10,14},{11,15},{24,28},{25,29},{26,30},{27,31}} | collective-permute-start | bytes 393224 | tf_op jit(solution)/shard_map/ppermute | solution.py:526
  38.7 5.5 %copy-start.3 = (f32[128]{0:T(128)S(1)}, f32[128]{0:T(128)}, u32[]{:S(2)}) copy-start(f32[128]{0:T(128)} %param.17) | copy-start | bytes 1540
  43.5 2.7 %collective-permute-start.5 = (bf16[4,128,128]{2,1,0:T(8,128)(2,1)S(1)}, bf16[4,128,128]{2,1,0:T(8,128)(2,1)S(1)}, u32[]{:S(2)}, u32[]{:S(2)}) collective-permute-start(bf16[4,128,128]{2,1,0:T(8,128)(2,1)S(1)} %fusion.3), channel_id=1, source_target_pairs={{8,12},{9,13},{10,14},{11,15},{24,28},{25,29},{26,30},{27,31}} | collective-permute-start | bytes 393224 | tf_op jit(solution)/shard_map/ppermute | solution.py:526

commit v5 on v4

--- a/solution.py
+++ b/solution.py
@@ -16,6 +16,7 @@
 PARTS = 2
 SPAN_X = 512
 SPAN_Y = 512
+SPAN_Z = 256
 EPSILON = 1e-06
 LOG2E = 1.4426950408889634
 F32 = jnp.float32
@@ -148,22 +149,30 @@
     return [total[at * heads : (at + 1) * heads] for at in range(span // CHUNK)]
 
 
-def rim_kernel(query_ref, key_ref, value_ref, out_ref):
-    first, second = query_ref.shape[1], key_ref.shape[1]
-    out_ref[:, :first] = query_ref[...]
-    out_ref[:, first : first + second] = key_ref[...]
-    out_ref[:, first + second :] = value_ref[...]
+def rim_kernel(query_ref, key_ref, value_ref, out_ref, done):
+    copies = []
+    at = 0
+    for place, ref in enumerate((query_ref, key_ref, value_ref)):
+        rows, width = ref.shape
+        source = ref.at[pl.ds(rows - RIM, RIM), :]
+        target = out_ref.at[:, pl.ds(at, width)]
+        copies.append(pltpu.make_async_copy(source, target, done.at[place]))
+        at += width
+    for copy in copies:
+        copy.start()
+    for copy in copies:
+        copy.wait()
 
 
 def pack_rim(query_raw, key_raw, value_raw):
-    last = query_raw.shape[0] // RIM - 1
-    widths = [array.shape[1] for array in (query_raw, key_raw, value_raw)]
+    width = query_raw.shape[1] + key_raw.shape[1] + value_raw.shape[1]
+    anywhere = pl.BlockSpec(memory_space=pl.ANY)
     return pl.pallas_call(
         rim_kernel,
-        grid=(1,),
-        in_specs=[pl.BlockSpec((RIM, width), lambda i: (last, 0)) for width in widths],
-        out_specs=pl.BlockSpec((RIM, sum(widths)), lambda i: (0, 0)),
-        out_shape=jax.ShapeDtypeStruct((RIM, sum(widths)), BF16),
+        in_specs=[anywhere] * 3,
+        out_specs=anywhere,
+        out_shape=jax.ShapeDtypeStruct((RIM, width), BF16),
+        scratch_shapes=[pltpu.SemaphoreType.DMA((3,))],
         name="pack_rim",
     )(query_raw, key_raw, value_raw)
 
@@ -197,14 +206,10 @@
     right_ref,
     sum_ref,
 ):
-    step = pl.program_id(0)
-    last_step = pl.num_programs(0) - 1
     ratio = vheads // kheads
     tiles = kheads + vheads
     parts = span // CHUNK
     first_head = part * vheads
-    base = pl.multiple_of(step * span, span)
-    now_rows = pl.ds(base, span)
     key_from = part * kheads * DK
     value_from = part * vheads * DV
     rim_from = (key_ref.shape[1] + key_from, 2 * key_ref.shape[1] + value_from)
@@ -219,7 +224,8 @@
             at = rim_from[0] + tile * DK if tile < kheads else rim_from[1] + (tile - kheads) * DV
             wide[tile, 0:HALO] = rim_ref[:, at : at + 128].astype(F32)[RIM - HALO :]
 
-    def prepare():
+    def prepare(step):
+        now_rows = pl.ds(pl.multiple_of(step * span, span), span)
         tap_key = tap_key_ref[...].astype(F32) * 0.5
         tap_value = tap_value_ref[...].astype(F32) * 0.5
         keys = []
@@ -264,7 +270,8 @@
                     tail_ref[item] = flat * ends[place : place + 1].astype(BF16)
                     right_ref[item, :, :DK] = key * jnp.exp2(cum_col).astype(BF16)
 
-    def finish():
+    def finish(step):
+        base = pl.multiple_of(step * span, span)
         negs = [neg_ref[item] for item in range(len(places))]
         found = half_inverses(negs, diag_ref)
         tops = [
@@ -296,18 +303,16 @@
             state[head, :, :DK] = now[:, :DK] * tail + change[:, :DK]
             state[head, :, DK:] = now[:, DK:] * tail + (change[:, DK:] - writes[item])
 
-    @pl.when(step == 0)
-    def _():
-        set_up()
-
-    prepare()
-    finish()
-
-    @pl.when(step == last_step)
-    def _():
-        for head in range(vheads):
-            transit_ref[head] = state[head, :, :DK].astype(BF16)
-            memory_ref[head] = state[head, :, DK:]
+    def advance(step, carry):
+        prepare(step)
+        finish(step)
+        return carry
+
+    set_up()
+    lax.fori_loop(0, key_ref.shape[0] // span, advance, 0)
+    for head in range(vheads):
+        transit_ref[head] = state[head, :, :DK].astype(BF16)
+        memory_ref[head] = state[head, :, DK:]
 
 
 def memory_pass(part, key_raw, value_raw, rim, conv_key, conv_value, gate_flat, logit_flat):
@@ -319,7 +324,6 @@
     span = min(SPAN_X, tok_count)
     chunks = tok_count // CHUNK
     items = span // CHUNK * vheads
-    blocks = tok_count // span
     count = len(levels())
 
     def kernel(*refs):
@@ -327,7 +331,6 @@
 
     return pl.pallas_call(
         kernel,
-        grid=(blocks,),
         in_specs=[VMEM] * 7,
         out_specs=[VMEM] * 5,
         out_shape=[
@@ -371,60 +374,57 @@
     local_ref,
     wide,
 ):
-    step = pl.program_id(0)
     ratio = vheads // kheads
     first_head = group * vheads
-    base = pl.multiple_of(step * span, span)
-    now_rows = pl.ds(base, span)
     query_from = group * kheads * DK
-
-    @pl.when(step == 0)
-    def _():
+    for tile in range(kheads):
+        at = slice(query_from + tile * DK, query_from + (tile + 1) * DK)
+        wide[tile, 0:HALO] = rim_ref[:, at].astype(F32)[RIM - HALO :]
+
+    def advance(step, carry):
+        base = pl.multiple_of(step * span, span)
+        now_rows = pl.ds(base, span)
+        taps = tap_ref[...].astype(F32) * 0.5
+        queries = []
         for tile in range(kheads):
             at = slice(query_from + tile * DK, query_from + (tile + 1) * DK)
-            wide[tile, 0:HALO] = rim_ref[:, at].astype(F32)[RIM - HALO :]
-
-    @pl.when(step > 0)
-    def _():
+            queries.append(unit(conv(query_ref[now_rows, at], wide, tile, taps[:, at]), DK**-0.5))
+
         for tile in range(kheads):
             wide[tile, 0:HALO] = wide[tile, span : span + HALO]
-
-    taps = tap_ref[...].astype(F32) * 0.5
-    queries = []
-    for tile in range(kheads):
-        at = slice(query_from + tile * DK, query_from + (tile + 1) * DK)
-        queries.append(unit(conv(query_ref[now_rows, at], wide, tile, taps[:, at]), DK**-0.5))
-
-    rows, cols = iotas((CHUNK, CHUNK))
-    lower = rows >= cols
-    cums = sums(gate_ref[:, now_rows] * LOG2E, span)
-    strengths = log_weights(logit_ref[:, now_rows])
-    for part in range(span // CHUNK):
-        here = slice(part * CHUNK, (part + 1) * CHUNK)
-        place_rows = pl.ds(base + part * CHUNK, CHUNK)
-        cum_flat = cums[part]
-        cum = cum_flat.T
-        lift = strengths[:, here] - cum_flat
-        for khead in range(kheads):
-            query = queries[khead][here]
-            gram = lax.dot_general(
-                query,
-                key_ref[place_rows, khead * DK : (khead + 1) * DK],
-                (((1,), (1,)), ((), ())),
-                preferred_element_type=F32,
-            )
-            for which in range(ratio):
-                head = khead * ratio + which
-                place = first_head + head
-                there = slice(head * DV, (head + 1) * DV)
-                cum_col = jnp.broadcast_to(cum[:, place : place + 1], (CHUNK, CHUNK))
-                powers = cum_col + lift[place : place + 1]
-                scores = (gram * jnp.exp2(jnp.where(lower, powers, -jnp.inf))).astype(BF16)
-                product = dot(scores, solved_ref[place_rows, head * WIDE : (head + 1) * WIDE])
-                meet = query.astype(F32) * jnp.exp2(cum_col) - product[:, :DK]
-                final = dot(meet.astype(BF16), before_ref[step * (span // CHUNK) + part, head])
-                rows_ref[place_rows, there] = final[:, :DK].astype(BF16)
-                local_ref[place_rows, there] = (final[:, DK:] + product[:, DK:]).astype(BF16)
+        rows, cols = iotas((CHUNK, CHUNK))
+        lower = rows >= cols
+        cums = sums(gate_ref[:, now_rows] * LOG2E, span)
+        strengths = log_weights(logit_ref[:, now_rows])
+        for part in range(span // CHUNK):
+            here = slice(part * CHUNK, (part + 1) * CHUNK)
+            place_rows = pl.ds(base + part * CHUNK, CHUNK)
+            cum_flat = cums[part]
+            cum = cum_flat.T
+            lift = strengths[:, here] - cum_flat
+            for khead in range(kheads):
+                query = queries[khead][here]
+                gram = lax.dot_general(
+                    query,
+                    key_ref[place_rows, khead * DK : (khead + 1) * DK],
+                    (((1,), (1,)), ((), ())),
+                    preferred_element_type=F32,
+                )
+                for which in range(ratio):
+                    head = khead * ratio + which
+                    place = first_head + head
+                    there = slice(head * DV, (head + 1) * DV)
+                    cum_col = jnp.broadcast_to(cum[:, place : place + 1], (CHUNK, CHUNK))
+                    powers = cum_col + lift[place : place + 1]
+                    scores = (gram * jnp.exp2(jnp.where(lower, powers, -jnp.inf))).astype(BF16)
+                    product = dot(scores, solved_ref[place_rows, head * WIDE : (head + 1) * WIDE])
+                    meet = query.astype(F32) * jnp.exp2(cum_col) - product[:, :DK]
+                    final = dot(meet.astype(BF16), before_ref[step * (span // CHUNK) + part, head])
+                    rows_ref[place_rows, there] = final[:, :DK].astype(BF16)
+                    local_ref[place_rows, there] = (final[:, DK:] + product[:, DK:]).astype(BF16)
+        return carry
+
+    lax.fori_loop(0, query_ref.shape[0] // span, advance, 0)
 
 
 def rows_pass(part, query_raw, rim, conv_query, keys, gate_flat, logit_flat, solved, before):
@@ -439,7 +439,6 @@
 
     return pl.pallas_call(
         kernel,
-        grid=(tok_count // span,),
         in_specs=[VMEM] * 8,
         out_specs=[VMEM] * 2,
         out_shape=[
@@ -455,46 +454,56 @@
     )(query_raw, rim, conv_query, keys, gate_flat, logit_flat, solved, before)
 
 
-def final_kernel(vheads, rows_ref, local_ref, early_ref, late_ref, gain_ref, *rest):
-    out_ref = rest[-1]
+def final_kernel(part, span, rows_ref, local_ref, early_ref, late_ref, gain_ref, *rest):
+    out_ref, ready, done = rest[-3:]
     gain = gain_ref[...]
-    span = out_ref.shape[0]
-    now_rows = pl.ds(pl.multiple_of(pl.program_id(0) * span, span), span)
-    for head in range(vheads):
-        there = slice(head * DV, (head + 1) * DV)
-        start = early_ref[head] + late_ref[head]
-        output = dot(rows_ref[now_rows, there], start) + local_ref[now_rows, there].astype(F32)
-        square = output * output
-        if head % 2:
-            total = row_sums(square)
-        else:
-            total = jnp.sum(square, axis=-1, keepdims=True)
-        mean = total * (1.0 / DV)
-        out_ref[:, there] = (output * lax.rsqrt(mean + EPSILON) * gain).astype(BF16)
+    vheads = early_ref.shape[0]
+    width = vheads * DV
+    starts = [early_ref[head] + late_ref[head] for head in range(vheads)]
+    copies = []
+    for turn in range(rows_ref.shape[0] // span):
+        here = slice(turn * span, (turn + 1) * span)
+        for head in range(vheads):
+            there = slice(head * DV, (head + 1) * DV)
+            output = dot(rows_ref[here, there], starts[head]) + local_ref[here, there].astype(F32)
+            square = output * output
+            if head % 2:
+                total = row_sums(square)
+            else:
+                total = jnp.sum(square, axis=-1, keepdims=True)
+            scale = lax.rsqrt(total * (1.0 / DV) + EPSILON)
+            ready[here, there] = (output * scale * gain).astype(BF16)
+        target = out_ref.at[pl.ds(turn * span, span), pl.ds(part * width, width)]
+        source = ready.at[pl.ds(turn * span, span), :]
+        copies.append(pltpu.make_async_copy(source, target, done.at[turn]))
+        copies[-1].start()
+    for copy in copies:
+        copy.wait()
 
 
 def final_pass(part, rows, local, early, late, gain, earlier):
     tok_count = rows.shape[0]
     vheads = early.shape[0]
-    span = min(512, tok_count)
-
-    def along(width, column):
-        return pl.BlockSpec((span, width), lambda i: (i, column))
+    span = min(SPAN_Z, tok_count)
 
     def kernel(*refs):
-        final_kernel(vheads, *refs)
-
+        final_kernel(part, span, *refs)
+
+    anywhere = pl.BlockSpec(memory_space=pl.ANY)
     arrays = [rows, local, early, late, gain]
     specs = [VMEM] * 5
     if earlier is not None:
         arrays.append(earlier)
-        specs.append(pl.BlockSpec(memory_space=pl.ANY))
+        specs.append(anywhere)
     return pl.pallas_call(
         kernel,
-        grid=(tok_count // span,),
         in_specs=specs,
-        out_specs=along(vheads * DV, part),
+        out_specs=anywhere,
         out_shape=jax.ShapeDtypeStruct((tok_count, PARTS * vheads * DV), BF16),
+        scratch_shapes=[
+            pltpu.VMEM((tok_count, vheads * DV), BF16),
+            pltpu.SemaphoreType.DMA((tok_count // span,)),
+        ],
         input_output_aliases={} if earlier is None else {5: 0},
         compiler_params=pltpu.CompilerParams(vmem_limit_bytes=12 * 1024 * 1024),
         name="final_pass",

time: 48.3 us -> 50.1 us (1.037)
  Pallas kernels: 31.5 us -> 33.2 us
    pallas_call x7, Pallas kernels: 31.5 us -> 33.2 us  [the longest x2 16.9 us: memory_pass(): pl.pallas_call(kernel, in_specs=[VMEM] * 7, out_specs=[VMEM] * 5, out_sha...]
  transfers between devices with their start and end apart: 7 -> 7, of which waited for: 1 -> 1; matrix products, arithmetic and copies ran while one was open for 2% -> 2% of each run, Pallas kernels for 40% -> 39%
where the time goes in v5:
time: 50.1 us; the launch traced here: 49.8 us
  Pallas kernels  33.2 us (66%)
  starting transfers between devices  13.2 us (26%)
  waiting for transfers between devices  2.22 us (4%)
  matrix products  0.72 us (1%)
    pallas_call x2, Pallas kernels, memory_pass(): pl.pallas_call(kernel, in_specs=[VMEM] * 7, out_specs=[VMEM] * 5, out_sha...  16.9 us
    pallas_call x2, Pallas kernels, rows_pass(): pl.pallas_call(kernel, in_specs=[VMEM] * 8, out_specs=[VMEM] * 2, out_sha...  8.89 us
    ppermute x6, starting transfers between devices, send(): lax.ppermute(moved[part][source], 'ctx', [(source, source + 1)])  8.28 us
    ppermute x1, starting transfers between devices, shards(): lax.ppermute(pack_rim(query_raw, key_raw, value_raw), 'ctx', [(at, at + 1...  4.95 us
    pallas_call x2, Pallas kernels, final_pass(): pl.pallas_call(kernel, in_specs=specs, out_specs=anywhere, out_shape=jax....  4.29 us
    pallas_call x1, Pallas kernels, pack_rim(): pl.pallas_call(rim_kernel, in_specs=[anywhere] * 3, out_specs=anywhere, o...  3.12 us
    ppermute x1, waiting for transfers between devices, shards(): lax.ppermute(pack_rim(query_raw, key_raw, value_raw), 'ctx', [(at, at + 1...  2.2 us
  transfers between devices with their start and end apart: 7, of which 1 were waited for; matrix products, arithmetic and copies ran while one was open for 2% of the time, Pallas kernels for 39%

profile of v5, /device:TPU:0, one launch (start us, length us, event | category | flops | bytes accessed | tf_op | source)
XLA Modules:
  0.0 49.8 jit_solution(6658950143092384519)
XLA Ops:
  0.0 0.0 copy-start
  0.0 0.0 copy-start.1
  0.0 0.0 copy-start.6
  0.0 0.0 copy-start.7
  0.0 0.0 copy-start.5
  0.0 0.0 copy-start.4
  0.0 3.1 %pack_rim.1 = bf16[16,2048]{1,0:T(8,128)(2,1)} custom-call(bf16[1024,512]{1,0:T(8,128)(2,1)} %refs_0_.7, bf16[1024,512]{1,0:T(8,128)(2,1)} %refs_0_.5, bf16[1024,1024]{1,0:T(8,128)(2,1)} %refs_1_.3), custom_call_target="tpu_custom_call" | custom-call | tf_op jit(solution)/shard_map/pack_rim/pallas_call | solution.py:170
  3.1 4.9 %collective-permute-start = (bf16[16,2048]{1,0:T(8,128)(2,1)}, bf16[16,2048]{1,0:T(8,128)(2,1)S(1)}, u32[]{:S(2)}, u32[]{:S(2)}) collective-permute-start(bf16[16,2048]{1,0:T(8,128)(2,1)} %pack_rim.1), channel_id=1, source_target_pairs={{0,4},{4,8},{8,12},{1,5},{5,9},{9,13},{2,6},{6,10},{10,14},{3,7},{... | collective-permute-start | bytes 196616 | tf_op jit(solution)/shard_map/ppermute | solution.py:517
  8.1 2.2 %collective-permute-done.refs_2_.refs_1_ = bf16[16,2048]{1,0:T(8,128)(2,1)S(1)} collective-permute-done((bf16[16,2048]{1,0:T(8,128)(2,1)}, bf16[16,2048]{1,0:T(8,128)(2,1)S(1)}, u32[]{:S(2)}, u32[]{:S(2)}) %collective-permute-start) | collective-permute-done | bytes 65568 | tf_op jit(solution)/shard_map/ppermute | solution.py:517
  10.3 0.0 copy-done
  10.3 0.0 copy-done.1
  10.3 0.0 copy-done.6
  10.3 0.0 copy-done.7
  10.3 0.0 copy-done.5
  10.3 0.0 copy-done.4
  10.3 8.5 %memory_pass.3 = (bf16[1024,256]{1,0:T(8,128)(2,1)S(1)}, bf16[1024,1024]{1,0:T(8,128)(2,1)S(1)}, bf16[8,4,128,256]{3,2,1,0:T(8,128)(2,1)S(1)}, bf16[4,128,128]{2,1,0:T(8,128)(2,1)S(1)}, f32[4,128,128]{2,1,0:T(8,128)S(1)}) custom-call(bf16[1024,512]{1,0:T(8,128)(2,1)S(1)} %copy-done.1, bf16[1024,1024]{1,0:T(8,128)(2,1)S(1)} %copy-done, ...), custom_call_target="tpu_custom_call" | custom-call | flops 8192000000 | bytes 8388608 | tf_op jit(solution)/shard_map/memory_pass/pallas_call | solution.py:332
  18.8 0.0 copy-start.2
  18.8 0.0 copy-start.8
  18.9 4.3 %collective-permute-start.1 = (bf16[4,128,128]{2,1,0:T(8,128)(2,1)S(1)}, bf16[4,128,128]{2,1,0:T(8,128)(2,1)S(1)}, u32[]{:S(2)}, u32[]{:S(2)}) collective-permute-start(bf16[4,128,128]{2,1,0:T(8,128)(2,1)S(1)} %convert_element_type.18), channel_id=1, source_target_pairs={{0,4},{1,5},{2,6},{3,7},{16,20},{17,21},{18,22},{19,23}} | collective-permute-start | bytes 393224 | tf_op jit(solution)/shard_map/ppermute | solution.py:535
  23.2 8.5 %memory_pass.2 = (bf16[1024,256]{1,0:T(8,128)(2,1)S(1)}, bf16[1024,1024]{1,0:T(8,128)(2,1)S(1)}, bf16[8,4,128,256]{3,2,1,0:T(8,128)(2,1)S(1)}, bf16[4,128,128]{2,1,0:T(8,128)(2,1)S(1)}, f32[4,128,128]{2,1,0:T(8,128)S(1)}) custom-call(bf16[1024,512]{1,0:T(8,128)(2,1)S(1)} %copy-done.1, bf16[1024,1024]{1,0:T(8,128)(2,1)S(1)} %copy-done, ...), custom_call_target="tpu_custom_call" | custom-call | flops 8192000000 | bytes 8388608 | tf_op jit(solution)/shard_map/memory_pass/pallas_call | solution.py:332
  31.7 1.3 %collective-permute-start.3 = (bf16[4,128,128]{2,1,0:T(8,128)(2,1)S(1)}, bf16[4,128,128]{2,1,0:T(8,128)(2,1)S(1)}, u32[]{:S(2)}, u32[]{:S(2)}) collective-permute-start(bf16[4,128,128]{2,1,0:T(8,128)(2,1)S(1)} %convert_element_type.21), channel_id=1, source_target_pairs={{0,4},{1,5},{2,6},{3,7},{16,20},{17,21},{18,22},{19,23}} | collective-permute-start | bytes 393224 | tf_op jit(solution)/shard_map/ppermute | solution.py:535
  33.0 0.0 collective-permute-done.1
  33.0 0.2 fusion
  33.2 0.7 %collective-permute-start.2 = (bf16[4,128,128]{2,1,0:T(8,128)(2,1)S(1)}, bf16[4,128,128]{2,1,0:T(8,128)(2,1)S(1)}, u32[]{:S(2)}, u32[]{:S(2)}) collective-permute-start(bf16[4,128,128]{2,1,0:T(8,128)(2,1)S(1)} %fusion), channel_id=1, source_target_pairs={{4,8},{5,9},{6,10},{7,11},{20,24},{21,25},{22,26},{23,27}} | collective-permute-start | bytes 393224 | tf_op jit(solution)/shard_map/ppermute | solution.py:535
  33.9 0.0 copy-done.2
  33.9 0.0 copy-done.8
  33.9 4.4 %rows_pass.2 = (bf16[1024,512]{1,0:T(8,128)(2,1)S(1)}, bf16[1024,512]{1,0:T(8,128)(2,1)S(1)}) custom-call(bf16[1024,512]{1,0:T(8,128)(2,1)S(1)} %copy-done.2, bf16[16,2048]{1,0:T(8,128)(2,1)S(1)} %collective-permute-done.refs_2_.refs_1_, bf16[4,512]{1,0:T(4,128)(2,1)S(1)} %copy-done.8, bf16[1024,256]{1,0:T(8,128)(2,1)S(1)} %get-tuple-element.30.refs_3_, ...), custom_call_target="tpu_custom_call" | custom-call | flops 4096000000 | bytes 8388608 | tf_op jit(solution)/shard_map/rows_pass/pallas_call | solution.py:440
  38.3 0.0 collective-permute-done.3
  38.3 0.2 fusion.2
  38.5 0.7 %collective-permute-start.4 = (bf16[4,128,128]{2,1,0:T(8,128)(2,1)S(1)}, bf16[4,128,128]{2,1,0:T(8,128)(2,1)S(1)}, u32[]{:S(2)}, u32[]{:S(2)}) collective-permute-start(bf16[4,128,128]{2,1,0:T(8,128)(2,1)S(1)} %fusion.2), channel_id=1, source_target_pairs={{4,8},{5,9},{6,10},{7,11},{20,24},{21,25},{22,26},{23,27}} | collective-permute-start | bytes 393224 | tf_op jit(solution)/shard_map/ppermute | solution.py:535
  39.2 0.0 collective-permute-done.2
  39.2 0.2 fusion.1
  39.4 0.7 %collective-permute-start.6 = (bf16[4,128,128]{2,1,0:T(8,128)(2,1)S(1)}, bf16[4,128,128]{2,1,0:T(8,128)(2,1)S(1)}, u32[]{:S(2)}, u32[]{:S(2)}) collective-permute-start(bf16[4,128,128]{2,1,0:T(8,128)(2,1)S(1)} %fusion.1), channel_id=1, source_target_pairs={{8,12},{9,13},{10,14},{11,15},{24,28},{25,29},{26,30},{27,31}} | collective-permute-start | bytes 393224 | tf_op jit(solution)/shard_map/ppermute | solution.py:535
  40.1 0.0 copy-start.3
  40.1 4.4 %rows_pass.3 = (bf16[1024,512]{1,0:T(8,128)(2,1)S(1)}, bf16[1024,512]{1,0:T(8,128)(2,1)S(1)}) custom-call(bf16[1024,512]{1,0:T(8,128)(2,1)S(1)} %copy-done.2, bf16[16,2048]{1,0:T(8,128)(2,1)S(1)} %collective-permute-done.refs_2_.refs_1_, bf16[4,512]{1,0:T(4,128)(2,1)S(1)} %copy-done.8, bf16[1024,256]{1,0:T(8,128)(2,1)S(1)} %get-tuple-element.24.refs_3_, ...), custom_call_target="tpu_custom_call" | custom-call | flops 4096000000 | bytes 8388608 | tf_op jit(solution)/shard_map/rows_pass/pallas_call | solution.py:440
  44.5 0.0 collective-permute-done.4
  44.6 0.2 fusion.3
  44.7 0.7 %collective-permute-start.5 = (bf16[4,128,128]{2,1,0:T(8,128)(2,1)S(1)}, bf16[4,128,128]{2,1,0:T(8,128)(2,1)S(1)}, u32[]{:S(2)}, u32[]{:S(2)}) collective-permute-start(bf16[4,128,128]{2,1,0:T(8,128)(2,1)S(1)} %fusion.3), channel_id=1, source_target_pairs={{8,12},{9,13},{10,14},{11,15},{24,28},{25,29},{26,30},{27,31}} | collective-permute-start | bytes 393224 | tf_op jit(solution)/shard_map/ppermute | solution.py:535
  45.5 0.0 collective-permute-done.6.refs_3_
  45.5 0.0 copy-done.3
  45.5 2.1 %final_pass.2.refs_5_ = bf16[1024,1024]{1,0:T(8,128)(2,1)} custom-call(bf16[1024,512]{1,0:T(8,128)(2,1)S(1)} %get-tuple-element.41.refs_0_, bf16[1024,512]{1,0:T(8,128)(2,1)S(1)} %get-tuple-element.34.refs_1_, bf16[4,128,128]{2,1,0:T(8,128)(2,1)S(1)} %add.23.refs_2_, bf16[4,128,128]{2,1,0:T(8,128)(2,1)S(1)} %collective-permute-done.6.refs_3_, ...), custom_call_target="tpu_custom_call" | custom-call | tf_op jit(solution)/shard_map/final_pass/pallas_call | solution.py:498
  47.7 0.0 collective-permute-done.5.refs_3_
  47.7 2.1 %final_pass.3 = bf16[1024,1024]{1,0:T(8,128)(2,1)} custom-call(bf16[1024,512]{1,0:T(8,128)(2,1)S(1)} %get-tuple-element.38.refs_0_, bf16[1024,512]{1,0:T(8,128)(2,1)S(1)} %get-tuple-element.39.refs_1_, bf16[4,128,128]{2,1,0:T(8,128)(2,1)S(1)} %add.21.refs_2_, ...), custom_call_target="tpu_custom_call", output_to_operand_aliasing={{}: (5, {})} | custom-call | tf_op jit(solution)/shard_map/final_pass/pallas_call | solution.py:498
  (4 shorter events, 0.1 us)
Async XLA Ops:
  0.0 10.3 %copy-start = (bf16[1024,1024]{1,0:T(8,128)(2,1)S(1)}, bf16[1024,1024]{1,0:T(8,128)(2,1)}, u32[]{:S(2)}) copy-start(bf16[1024,1024]{1,0:T(8,128)(2,1)} %refs_1_.3) | copy-start | bytes 6291460
  0.0 10.3 %copy-start.1 = (bf16[1024,512]{1,0:T(8,128)(2,1)S(1)}, bf16[1024,512]{1,0:T(8,128)(2,1)}, u32[]{:S(2)}) copy-start(bf16[1024,512]{1,0:T(8,128)(2,1)} %refs_0_.5) | copy-start | bytes 3145732
  0.0 10.3 %copy-start.6 = (bf16[4,1024]{1,0:T(4,128)(2,1)S(1)}, bf16[4,1024]{1,0:T(4,128)(2,1)}, u32[]{:S(2)}) copy-start(bf16[4,1024]{1,0:T(4,128)(2,1)} %refs_4_.3) | copy-start | bytes 24580
  0.0 10.3 %copy-start.7 = (bf16[4,512]{1,0:T(4,128)(2,1)S(1)}, bf16[4,512]{1,0:T(4,128)(2,1)}, u32[]{:S(2)}) copy-start(bf16[4,512]{1,0:T(4,128)(2,1)} %refs_3_.3) | copy-start | bytes 12292
  0.0 10.3 %copy-start.5 = (f32[1024,8]{0,1:T(8,128)S(1)}, f32[1024,8]{0,1:T(8,128)}, u32[]{:S(2)}) copy-start(f32[1024,8]{0,1:T(8,128)} %param.16) | copy-start | bytes 98308
  0.0 10.3 %copy-start.4 = (f32[1024,8]{0,1:T(8,128)S(1)}, f32[1024,8]{0,1:T(8,128)}, u32[]{:S(2)}) copy-start(f32[1024,8]{0,1:T(8,128)} %param.15) | copy-start | bytes 98308
  3.1 7.2 %collective-permute-start = (bf16[16,2048]{1,0:T(8,128)(2,1)}, bf16[16,2048]{1,0:T(8,128)(2,1)S(1)}, u32[]{:S(2)}, u32[]{:S(2)}) collective-permute-start(bf16[16,2048]{1,0:T(8,128)(2,1)} %pack_rim.1), channel_id=1, source_target_pairs={{0,4},{4,8},{8,12},{1,5},{5,9},{9,13},{2,6},{6,10},{10,14},{3,7},{... | collective-permute-start | bytes 196616 | tf_op jit(solution)/shard_map/ppermute | solution.py:517
  18.8 15.0 %copy-start.2 = (bf16[1024,512]{1,0:T(8,128)(2,1)S(1)}, bf16[1024,512]{1,0:T(8,128)(2,1)}, u32[]{:S(2)}) copy-start(bf16[1024,512]{1,0:T(8,128)(2,1)} %refs_0_.7) | copy-start | bytes 3145732
  18.8 15.0 %copy-start.8 = (bf16[4,512]{1,0:T(4,128)(2,1)S(1)}, bf16[4,512]{1,0:T(4,128)(2,1)}, u32[]{:S(2)}) copy-start(bf16[4,512]{1,0:T(4,128)(2,1)} %refs_2_.3) | copy-start | bytes 12292
  18.9 14.1 %collective-permute-start.1 = (bf16[4,128,128]{2,1,0:T(8,128)(2,1)S(1)}, bf16[4,128,128]{2,1,0:T(8,128)(2,1)S(1)}, u32[]{:S(2)}, u32[]{:S(2)}) collective-permute-start(bf16[4,128,128]{2,1,0:T(8,128)(2,1)S(1)} %convert_element_type.18), channel_id=1, source_target_pairs={{0,4},{1,5},{2,6},{3,7},{16,20},{17,21},{18,22},{19,23}} | collective-permute-start | bytes 393224 | tf_op jit(solution)/shard_map/ppermute | solution.py:535
  31.7 6.7 %collective-permute-start.3 = (bf16[4,128,128]{2,1,0:T(8,128)(2,1)S(1)}, bf16[4,128,128]{2,1,0:T(8,128)(2,1)S(1)}, u32[]{:S(2)}, u32[]{:S(2)}) collective-permute-start(bf16[4,128,128]{2,1,0:T(8,128)(2,1)S(1)} %convert_element_type.21), channel_id=1, source_target_pairs={{0,4},{1,5},{2,6},{3,7},{16,20},{17,21},{18,22},{19,23}} | collective-permute-start | bytes 393224 | tf_op jit(solution)/shard_map/ppermute | solution.py:535
  33.2 6.0 %collective-permute-start.2 = (bf16[4,128,128]{2,1,0:T(8,128)(2,1)S(1)}, bf16[4,128,128]{2,1,0:T(8,128)(2,1)S(1)}, u32[]{:S(2)}, u32[]{:S(2)}) collective-permute-start(bf16[4,128,128]{2,1,0:T(8,128)(2,1)S(1)} %fusion), channel_id=1, source_target_pairs={{4,8},{5,9},{6,10},{7,11},{20,24},{21,25},{22,26},{23,27}} | collective-permute-start | bytes 393224 | tf_op jit(solution)/shard_map/ppermute | solution.py:535
  38.5 6.0 %collective-permute-start.4 = (bf16[4,128,128]{2,1,0:T(8,128)(2,1)S(1)}, bf16[4,128,128]{2,1,0:T(8,128)(2,1)S(1)}, u32[]{:S(2)}, u32[]{:S(2)}) collective-permute-start(bf16[4,128,128]{2,1,0:T(8,128)(2,1)S(1)} %fusion.2), channel_id=1, source_target_pairs={{4,8},{5,9},{6,10},{7,11},{20,24},{21,25},{22,26},{23,27}} | collective-permute-start | bytes 393224 | tf_op jit(solution)/shard_map/ppermute | solution.py:535
  39.4 6.1 %collective-permute-start.6 = (bf16[4,128,128]{2,1,0:T(8,128)(2,1)S(1)}, bf16[4,128,128]{2,1,0:T(8,128)(2,1)S(1)}, u32[]{:S(2)}, u32[]{:S(2)}) collective-permute-start(bf16[4,128,128]{2,1,0:T(8,128)(2,1)S(1)} %fusion.1), channel_id=1, source_target_pairs={{8,12},{9,13},{10,14},{11,15},{24,28},{25,29},{26,30},{27,31}} | collective-permute-start | bytes 393224 | tf_op jit(solution)/shard_map/ppermute | solution.py:535
  40.1 5.5 %copy-start.3 = (f32[128]{0:T(128)S(1)}, f32[128]{0:T(128)}, u32[]{:S(2)}) copy-start(f32[128]{0:T(128)} %param.17) | copy-start | bytes 1540
  44.7 2.9 %collective-permute-start.5 = (bf16[4,128,128]{2,1,0:T(8,128)(2,1)S(1)}, bf16[4,128,128]{2,1,0:T(8,128)(2,1)S(1)}, u32[]{:S(2)}, u32[]{:S(2)}) collective-permute-start(bf16[4,128,128]{2,1,0:T(8,128)(2,1)S(1)} %fusion.3), channel_id=1, source_target_pairs={{8,12},{9,13},{10,14},{11,15},{24,28},{25,29},{26,30},{27,31}} | collective-permute-start | bytes 393224 | tf_op jit(solution)/shard_map/ppermute | solution.py:535

commit v6 on v5

--- a/solution.py
+++ b/solution.py
@@ -15,7 +15,7 @@
 RIM = 16
 PARTS = 2
 SPAN_X = 512
-SPAN_Y = 512
+SPAN_Y = 256
 SPAN_Z = 256
 EPSILON = 1e-06
 LOG2E = 1.4426950408889634
@@ -149,30 +149,22 @@
     return [total[at * heads : (at + 1) * heads] for at in range(span // CHUNK)]
 
 
-def rim_kernel(query_ref, key_ref, value_ref, out_ref, done):
-    copies = []
-    at = 0
-    for place, ref in enumerate((query_ref, key_ref, value_ref)):
-        rows, width = ref.shape
-        source = ref.at[pl.ds(rows - RIM, RIM), :]
-        target = out_ref.at[:, pl.ds(at, width)]
-        copies.append(pltpu.make_async_copy(source, target, done.at[place]))
-        at += width
-    for copy in copies:
-        copy.start()
-    for copy in copies:
-        copy.wait()
+def rim_kernel(query_ref, key_ref, value_ref, out_ref):
+    first, second = query_ref.shape[1], key_ref.shape[1]
+    out_ref[:, :first] = query_ref[...]
+    out_ref[:, first : first + second] = key_ref[...]
+    out_ref[:, first + second :] = value_ref[...]
 
 
 def pack_rim(query_raw, key_raw, value_raw):
-    width = query_raw.shape[1] + key_raw.shape[1] + value_raw.shape[1]
-    anywhere = pl.BlockSpec(memory_space=pl.ANY)
+    last = query_raw.shape[0] // RIM - 1
+    widths = [array.shape[1] for array in (query_raw, key_raw, value_raw)]
     return pl.pallas_call(
         rim_kernel,
-        in_specs=[anywhere] * 3,
-        out_specs=anywhere,
-        out_shape=jax.ShapeDtypeStruct((RIM, width), BF16),
-        scratch_shapes=[pltpu.SemaphoreType.DMA((3,))],
+        grid=(1,),
+        in_specs=[pl.BlockSpec((RIM, width), lambda i: (last, 0)) for width in widths],
+        out_specs=pl.BlockSpec((RIM, sum(widths)), lambda i: (0, 0)),
+        out_shape=jax.ShapeDtypeStruct((RIM, sum(widths)), BF16),
         name="pack_rim",
     )(query_raw, key_raw, value_raw)
 
@@ -184,7 +176,6 @@
 def memory_kernel(
     kheads,
     vheads,
-    part,
     span,
     key_ref,
     value_ref,
@@ -209,34 +200,44 @@
     ratio = vheads // kheads
     tiles = kheads + vheads
     parts = span // CHUNK
-    first_head = part * vheads
-    key_from = part * kheads * DK
-    value_from = part * vheads * DV
-    rim_from = (key_ref.shape[1] + key_from, 2 * key_ref.shape[1] + value_from)
+    blocks = key_ref.shape[0] // span
+    all_keys = key_ref.shape[1]
+
+    def lanes(at, size):
+        return pl.ds(pl.multiple_of(at, 128), size)
+
+    def pick(part, options):
+        out = options[0]
+        for turn in range(1, PARTS):
+            out = jnp.where(part == turn, options[turn], out)
+        return out
+
     places = [(chunk, head) for chunk in range(parts) for head in range(vheads)]
 
-    def set_up():
-        fill_masks(diag_ref)
+    def set_up(part):
         rows, cols = iotas((DK, WIDE))
         for head in range(vheads):
             state[head] = (rows == cols).astype(F32)
         for tile in range(tiles):
-            at = rim_from[0] + tile * DK if tile < kheads else rim_from[1] + (tile - kheads) * DV
-            wide[tile, 0:HALO] = rim_ref[:, at : at + 128].astype(F32)[RIM - HALO :]
-
-    def prepare(step):
+            if tile < kheads:
+                at = all_keys + (part * kheads + tile) * DK
+            else:
+                at = 2 * all_keys + (part * vheads + tile - kheads) * DV
+            wide[tile, 0:HALO] = rim_ref[:, lanes(at, 128)].astype(F32)[RIM - HALO :]
+
+    def prepare(part, step):
         now_rows = pl.ds(pl.multiple_of(step * span, span), span)
-        tap_key = tap_key_ref[...].astype(F32) * 0.5
-        tap_value = tap_value_ref[...].astype(F32) * 0.5
         keys = []
         for tile in range(kheads):
             at = slice(tile * DK, (tile + 1) * DK)
-            place = slice(key_from + tile * DK, key_from + (tile + 1) * DK)
-            keys.append(unit(conv(key_ref[now_rows, place], wide, tile, tap_key[:, place]), 1.0))
-            unit_ref[now_rows, at] = keys[tile]
+            place = lanes((part * kheads + tile) * DK, DK)
+            tap = tap_key_ref[:, place].astype(F32) * 0.5
+            keys.append(unit(conv(key_ref[now_rows, place], wide, tile, tap), 1.0))
+            unit_ref[part, now_rows, at] = keys[tile]
         for tile in range(vheads):
-            place = slice(value_from + tile * DV, value_from + (tile + 1) * DV)
-            value = conv(value_ref[now_rows, place], wide, kheads + tile, tap_value[:, place])
+            place = lanes((part * vheads + tile) * DV, DV)
+            tap = tap_value_ref[:, place].astype(F32) * 0.5
+            value = conv(value_ref[now_rows, place], wide, kheads + tile, tap)
             for chunk in range(parts):
                 right_ref[chunk * vheads + tile, :, DK:] = value[
                     chunk * CHUNK : (chunk + 1) * CHUNK
@@ -262,15 +263,17 @@
                 for which in range(ratio):
                     head = khead * ratio + which
                     item = chunk * vheads + head
-                    place = first_head + head
-                    cum_col = jnp.broadcast_to(cum[:, place : place + 1], (CHUNK, CHUNK))
-                    powers = cum_col + lift[place : place + 1]
+                    choices = range(head, PARTS * vheads, vheads)
+                    cum_col = pick(part, [cum[:, at : at + 1] for at in choices])
+                    cum_col = jnp.broadcast_to(cum_col, (CHUNK, CHUNK))
+                    powers = cum_col + pick(part, [lift[at : at + 1] for at in choices])
+                    end = pick(part, [ends[at : at + 1] for at in choices])
                     decays = jnp.exp2(jnp.where(strict, powers, -jnp.inf))
                     neg_ref[item] = gram * decays
-                    tail_ref[item] = flat * ends[place : place + 1].astype(BF16)
+                    tail_ref[item] = flat * end.astype(BF16)
                     right_ref[item, :, :DK] = key * jnp.exp2(cum_col).astype(BF16)
 
-    def finish(step):
+    def finish(part, step):
         base = pl.multiple_of(step * span, span)
         negs = [neg_ref[item] for item in range(len(places))]
         found = half_inverses(negs, diag_ref)
@@ -290,32 +293,44 @@
         for item, (chunk, head) in enumerate(places):
             there = slice(head * WIDE, (head + 1) * WIDE)
             solved = jnp.concatenate([tops[item], lows[item]], axis=0)
-            solved_ref[pl.ds(base + chunk * CHUNK, CHUNK), there] = solved
+            solved_ref[part, pl.ds(base + chunk * CHUNK, CHUNK), there] = solved
             product = dot(tail_ref[item], solved)
             erases.append(product[:, :DK].astype(BF16))
             writes.append(product[:, DK:])
         for item, (chunk, head) in enumerate(places):
             now = state[head]
             short = now.astype(BF16)
-            before_ref[step * parts + chunk, head] = short
-            tail = sum_ref[chunk, first_head + head : first_head + head + 1]
+            before_ref[part, step * parts + chunk, head] = short
+            choices = range(head, PARTS * vheads, vheads)
+            tail = pick(part, [sum_ref[chunk, at : at + 1] for at in choices])
+            tail = jnp.broadcast_to(tail, (DK, CHUNK))
             change = dot(erases[item], short)
             state[head, :, :DK] = now[:, :DK] * tail + change[:, :DK]
             state[head, :, DK:] = now[:, DK:] * tail + (change[:, DK:] - writes[item])
 
-    def advance(step, carry):
-        prepare(step)
-        finish(step)
+    def advance(turn, carry):
+        part, step = turn // blocks, turn % blocks
+
+        @pl.when(step == 0)
+        def _():
+            set_up(part)
+
+        prepare(part, step)
+        finish(part, step)
+
+        @pl.when(step == blocks - 1)
+        def _():
+            for head in range(vheads):
+                transit_ref[part, head] = state[head, :, :DK].astype(BF16)
+                memory_ref[part, head] = state[head, :, DK:]
+
         return carry
 
-    set_up()
-    lax.fori_loop(0, key_ref.shape[0] // span, advance, 0)
-    for head in range(vheads):
-        transit_ref[head] = state[head, :, :DK].astype(BF16)
-        memory_ref[head] = state[head, :, DK:]
-
-
-def memory_pass(part, key_raw, value_raw, rim, conv_key, conv_value, gate_flat, logit_flat):
+    fill_masks(diag_ref)
+    lax.fori_loop(0, PARTS * blocks, advance, 0)
+
+
+def memory_pass(key_raw, value_raw, rim, conv_key, conv_value, gate_flat, logit_flat):
     tok_count = key_raw.shape[0]
     all_kheads = key_raw.shape[1] // DK
     all_vheads = value_raw.shape[1] // DV
@@ -327,18 +342,18 @@
     count = len(levels())
 
     def kernel(*refs):
-        memory_kernel(kheads, vheads, part, span, *refs)
+        memory_kernel(kheads, vheads, span, *refs)
 
     return pl.pallas_call(
         kernel,
         in_specs=[VMEM] * 7,
         out_specs=[VMEM] * 5,
         out_shape=[
-            jax.ShapeDtypeStruct((tok_count, kheads * DK), BF16),
-            jax.ShapeDtypeStruct((tok_count, vheads * WIDE), BF16),
-            jax.ShapeDtypeStruct((chunks, vheads, DK, WIDE), BF16),
-            jax.ShapeDtypeStruct((vheads, DK, DK), BF16),
-            jax.ShapeDtypeStruct((vheads, DK, DV), F32),
+            jax.ShapeDtypeStruct((PARTS, tok_count, kheads * DK), BF16),
+            jax.ShapeDtypeStruct((PARTS, tok_count, vheads * WIDE), BF16),
+            jax.ShapeDtypeStruct((PARTS, chunks, vheads, DK, WIDE), BF16),
+            jax.ShapeDtypeStruct((PARTS, vheads, DK, DK), BF16),
+            jax.ShapeDtypeStruct((PARTS, vheads, DK, DV), F32),
         ],
         scratch_shapes=[
             pltpu.VMEM((tiles, span + HALO, 128), F32),
@@ -406,7 +421,7 @@
                 query = queries[khead][here]
                 gram = lax.dot_general(
                     query,
-                    key_ref[place_rows, khead * DK : (khead + 1) * DK],
+                    key_ref[group, place_rows, khead * DK : (khead + 1) * DK],
                     (((1,), (1,)), ((), ())),
                     preferred_element_type=F32,
                 )
@@ -417,9 +432,9 @@
                     cum_col = jnp.broadcast_to(cum[:, place : place + 1], (CHUNK, CHUNK))
                     powers = cum_col + lift[place : place + 1]
                     scores = (gram * jnp.exp2(jnp.where(lower, powers, -jnp.inf))).astype(BF16)
-                    product = dot(scores, solved_ref[place_rows, head * WIDE : (head + 1) * WIDE])
+                    product = dot(scores, solved_ref[group, place_rows, head * WIDE : (head + 1) * WIDE])
                     meet = query.astype(F32) * jnp.exp2(cum_col) - product[:, :DK]
-                    final = dot(meet.astype(BF16), before_ref[step * (span // CHUNK) + part, head])
+                    final = dot(meet.astype(BF16), before_ref[group, step * (span // CHUNK) + part, head])
                     rows_ref[place_rows, there] = final[:, :DK].astype(BF16)
                     local_ref[place_rows, there] = (final[:, DK:] + product[:, DK:]).astype(BF16)
         return carry
@@ -460,9 +475,14 @@
     vheads = early_ref.shape[0]
     width = vheads * DV
     starts = [early_ref[head] + late_ref[head] for head in range(vheads)]
-    copies = []
-    for turn in range(rows_ref.shape[0] // span):
-        here = slice(turn * span, (turn + 1) * span)
+
+    def copy_of(turn):
+        here = pl.ds(pl.multiple_of(turn * span, span), span)
+        target = out_ref.at[here, pl.ds(part * width, width)]
+        return pltpu.make_async_copy(ready.at[here, :], target, done.at[turn])
+
+    def advance(turn, carry):
+        here = pl.ds(pl.multiple_of(turn * span, span), span)
         for head in range(vheads):
             there = slice(head * DV, (head + 1) * DV)
             output = dot(rows_ref[here, there], starts[head]) + local_ref[here, there].astype(F32)
@@ -473,12 +493,13 @@
                 total = jnp.sum(square, axis=-1, keepdims=True)
             scale = lax.rsqrt(total * (1.0 / DV) + EPSILON)
             ready[here, there] = (output * scale * gain).astype(BF16)
-        target = out_ref.at[pl.ds(turn * span, span), pl.ds(part * width, width)]
-        source = ready.at[pl.ds(turn * span, span), :]
-        copies.append(pltpu.make_async_copy(source, target, done.at[turn]))
-        copies[-1].start()
-    for copy in copies:
-        copy.wait()
+        copy_of(turn).start()
+        return carry
+
+    turns = rows_ref.shape[0] // span
+    lax.fori_loop(0, turns, advance, 0)
+    for turn in range(turns):
+        copy_of(turn).wait()
 
 
 def final_pass(part, rows, local, early, late, gain, earlier):
@@ -519,15 +540,14 @@
     )
     gate_flat, logit_flat = gate_log.T, beta_logit.T
     gain = norm_gain.reshape(1, DV)
-    first = [
-        memory_pass(part, key_raw, value_raw, rim, conv_key, conv_value, gate_flat, logit_flat)
-        for part in range(PARTS)
-    ]
+    keys, solved, before, transit, memory = memory_pass(
+        key_raw, value_raw, rim, conv_key, conv_value, gate_flat, logit_flat
+    )
     def after(value, *others):
         return lax.optimization_barrier((value, *others))[0]
 
-    moved = [[found[4].astype(BF16)] for found in first]
-    got = [[] for _ in first]
+    moved = [[memory[part].astype(BF16)] for part in range(PARTS)]
+    got = [[] for _ in range(PARTS)]
     second = [None] * PARTS
 
     def send(part):
@@ -535,13 +555,11 @@
         got[part].append(lax.ppermute(moved[part][source], "ctx", [(source, source + 1)]))
 
     def carry(part, *others):
-        transit, memory = first[part][3:]
         arrived = after(got[part][-1], *others)
-        ahead = jnp.einsum("hab,hbc->hac", transit, arrived, preferred_element_type=F32)
-        moved[part].append((ahead + memory).astype(BF16))
+        ahead = jnp.einsum("hab,hbc->hac", transit[part], arrived, preferred_element_type=F32)
+        moved[part].append((ahead + memory[part]).astype(BF16))
 
     def rows_of(part, *others):
-        keys, solved, before = first[part][:3]
         second[part] = rows_pass(
             part,
             query_raw,

time: 50.1 us -> 54.1 us (1.080); the launches traced: 49.8 us -> 53.2 us
  Pallas kernels: 33.2 us -> 35.1 us
  waiting for transfers between devices: 2.22 us -> 3.89 us
    pallas_call x2, Pallas kernels: 8.89 us -> 10.8 us  [rows_pass(): pl.pallas_call(kernel, in_specs=[VMEM] * 8, out_specs=[VMEM] * 2, out_sha...]
    ppermute x6, waiting for transfers between devices: 0.02 us -> 1.69 us  [send(): lax.ppermute(moved[part][source], 'ctx', [(source, source + 1)])]
    pallas_call x1, Pallas kernels: 3.12 us -> 1.58 us  [pack_rim(): pl.pallas_call(rim_kernel, grid=(1,), in_specs=[pl.BlockSpec((RIM, width)...]
    pallas_call x2, Pallas kernels: 4.29 us -> 5.34 us  [final_pass(): pl.pallas_call(kernel, in_specs=specs, out_specs=anywhere, out_shape=jax....]
    pallas_call x2 -> x1, Pallas kernels: 16.9 us -> 17.4 us  [memory_pass(): pl.pallas_call(kernel, in_specs=[VMEM] * 7, out_specs=[VMEM] * 5, out_sha...]
  transfers between devices with their start and end apart: 7 -> 7, of which waited for: 1 -> 2; matrix products, arithmetic and copies ran while one was open for 2% -> 1% of each run, Pallas kernels for 39% -> 25%
where the time goes in v6:
time: 54.1 us; the launch traced here: 53.2 us
  Pallas kernels  35.1 us (65%)
  starting transfers between devices  13.1 us (24%)
  waiting for transfers between devices  3.89 us (7%)
  matrix products  0.71 us (1%)
    pallas_call x1, Pallas kernels, memory_pass(): pl.pallas_call(kernel, in_specs=[VMEM] * 7, out_specs=[VMEM] * 5, out_sha...  17.4 us
    pallas_call x2, Pallas kernels, rows_pass(): pl.pallas_call(kernel, in_specs=[VMEM] * 8, out_specs=[VMEM] * 2, out_sha...  10.8 us
    ppermute x6, starting transfers between devices, send(): lax.ppermute(moved[part][source], 'ctx', [(source, source + 1)])  8.15 us
    pallas_call x2, Pallas kernels, final_pass(): pl.pallas_call(kernel, in_specs=specs, out_specs=anywhere, out_shape=jax....  5.34 us
    ppermute x1, starting transfers between devices, shards(): lax.ppermute(pack_rim(query_raw, key_raw, value_raw), 'ctx', [(at, at + 1...  4.93 us
    ppermute x1, waiting for transfers between devices, shards(): lax.ppermute(pack_rim(query_raw, key_raw, value_raw), 'ctx', [(at, at + 1...  2.2 us
    ppermute x6, waiting for transfers between devices, send(): lax.ppermute(moved[part][source], 'ctx', [(source, source + 1)])  1.69 us
    pallas_call x1, Pallas kernels, pack_rim(): pl.pallas_call(rim_kernel, grid=(1,), in_specs=[pl.BlockSpec((RIM, width)...  1.58 us
  transfers between devices with their start and end apart: 7, of which 2 were waited for; matrix products, arithmetic and copies ran while one was open for 1% of the time, Pallas kernels for 25%

profile of v6, /device:TPU:0, one launch (start us, length us, event | category | flops | bytes accessed | tf_op | source)
XLA Modules:
  0.0 53.2 jit_solution(10441859497233023157)
XLA Ops:
  0.0 0.0 copy-start
  0.0 0.0 copy-start.1
  0.0 0.0 copy-start.5
  0.0 0.0 copy-start.4
  0.0 0.0 copy-start.6
  0.0 0.0 copy-start.7
  0.0 1.6 %pack_rim.1 = bf16[16,2048]{1,0:T(8,128)(2,1)} custom-call(bf16[1024,512]{1,0:T(8,128)(2,1)} %refs_0_.5, bf16[1024,512]{1,0:T(8,128)(2,1)} %refs_0_.3, bf16[1024,1024]{1,0:T(8,128)(2,1)} %refs_1_.1), custom_call_target="tpu_custom_call" | custom-call | tf_op jit(solution)/shard_map/pack_rim/pallas_call | solution.py:162
  1.6 4.9 %collective-permute-start = (bf16[16,2048]{1,0:T(8,128)(2,1)}, bf16[16,2048]{1,0:T(8,128)(2,1)S(1)}, u32[]{:S(2)}, u32[]{:S(2)}) collective-permute-start(bf16[16,2048]{1,0:T(8,128)(2,1)} %pack_rim.1), channel_id=1, source_target_pairs={{0,4},{4,8},{8,12},{1,5},{5,9},{9,13},{2,6},{6,10},{10,14},{3,7},{... | collective-permute-start | bytes 196616 | tf_op jit(solution)/shard_map/ppermute | solution.py:538
  6.5 2.2 %collective-permute-done.refs_2_.refs_1_ = bf16[16,2048]{1,0:T(8,128)(2,1)S(1)} collective-permute-done((bf16[16,2048]{1,0:T(8,128)(2,1)}, bf16[16,2048]{1,0:T(8,128)(2,1)S(1)}, u32[]{:S(2)}, u32[]{:S(2)}) %collective-permute-start) | collective-permute-done | bytes 65568 | tf_op jit(solution)/shard_map/ppermute | solution.py:538
  8.7 0.0 copy-done
  8.7 0.0 copy-done.1
  8.7 0.0 copy-done.5
  8.8 0.0 copy-done.4
  8.8 0.0 copy-done.6
  8.8 0.0 copy-done.7
  8.8 0.0 copy-start.2
  8.8 0.0 copy-start.8
  8.8 17.4 %memory_pass.1 = (bf16[2,1024,256]{2,1,0:T(8,128)(2,1)S(1)}, bf16[2,1024,1024]{2,1,0:T(8,128)(2,1)S(1)}, bf16[2,8,4,128,256]{4,3,2,1,0:T(8,128)(2,1)S(1)}, bf16[...) custom-call(bf16[1024,512]{1,0:T(8,128)(2,1)S(1)} %copy-done.1, bf16[1024,1024]{1,0:T(8,128)(2,1)S(1)} %copy-done, ...), custom_call_target="tpu_custom_call" | custom-call | flops 8192000000 | bytes 8388608 | tf_op jit(solution)/shard_map/memory_pass/pallas_call | solution.py:347
  26.2 4.2 %collective-permute-start.1 = (bf16[4,128,128]{2,1,0:T(8,128)(2,1)S(1)}, bf16[4,128,128]{2,1,0:T(8,128)(2,1)S(1)}, u32[]{:S(2)}, u32[]{:S(2)}) collective-permute-start(bf16[4,128,128]{2,1,0:T(8,128)(2,1)S(1)} %get-tuple-element.34), channel_id=1, source_target_pairs={{0,4},{1,5},{2,6},{3,7},{16,20},{17,21},{18,22},{19,23}} | collective-permute-start | bytes 393224 | tf_op jit(solution)/shard_map/ppermute | solution.py:555
  30.4 1.3 %collective-permute-start.3 = (bf16[4,128,128]{2,1,0:T(8,128)(2,1)S(1)}, bf16[4,128,128]{2,1,0:T(8,128)(2,1)S(1)}, u32[]{:S(2)}, u32[]{:S(2)}) collective-permute-start(bf16[4,128,128]{2,1,0:T(8,128)(2,1)S(1)} %get-tuple-element.33), channel_id=1, source_target_pairs={{0,4},{1,5},{2,6},{3,7},{16,20},{17,21},{18,22},{19,23}} | collective-permute-start | bytes 393224 | tf_op jit(solution)/shard_map/ppermute | solution.py:555
  31.7 1.7 %collective-permute-done.1 = bf16[4,128,128]{2,1,0:T(8,128)(2,1)S(1)} collective-permute-done((bf16[4,128,128]{2,1,0:T(8,128)(2,1)S(1)}, bf16[4,128,128]{2,1,0:T(8,128)(2,1)S(1)}, u32[]{:S(2)}, u32[]{:S(2)}) %collective-permute-start.1) | collective-permute-done | bytes 131104 | tf_op jit(solution)/shard_map/ppermute | solution.py:555
  33.4 0.2 fusion
  33.6 0.7 %collective-permute-start.2 = (bf16[4,128,128]{2,1,0:T(8,128)(2,1)S(1)}, bf16[4,128,128]{2,1,0:T(8,128)(2,1)S(1)}, u32[]{:S(2)}, u32[]{:S(2)}) collective-permute-start(bf16[4,128,128]{2,1,0:T(8,128)(2,1)S(1)} %fusion), channel_id=1, source_target_pairs={{4,8},{5,9},{6,10},{7,11},{20,24},{21,25},{22,26},{23,27}} | collective-permute-start | bytes 393224 | tf_op jit(solution)/shard_map/ppermute | solution.py:555
  34.3 0.0 copy-done.2
  34.3 0.0 copy-done.8
  34.3 5.4 %rows_pass.2 = (bf16[1024,512]{1,0:T(8,128)(2,1)S(1)}, bf16[1024,512]{1,0:T(8,128)(2,1)S(1)}) custom-call(bf16[1024,512]{1,0:T(8,128)(2,1)S(1)} %copy-done.2, bf16[16,2048]{1,0:T(8,128)(2,1)S(1)} %collective-permute-done.refs_2_.refs_1_, bf16[4,512]{1,0:T(4,128)(2,1)S(1)} %copy-done.8, bf16[2,1024,256]{2,1,0:T(8,128)(2,1)S(1)} %get-tuple-element.19.refs_3_, ...), custom_call_target="tpu_custom_call" | custom-call | flops 4096000000 | bytes 8388608 | tf_op jit(solution)/shard_map/rows_pass/pallas_call | solution.py:455
  39.7 0.0 collective-permute-done.3
  39.7 0.2 fusion.2
  39.9 0.7 %collective-permute-start.4 = (bf16[4,128,128]{2,1,0:T(8,128)(2,1)S(1)}, bf16[4,128,128]{2,1,0:T(8,128)(2,1)S(1)}, u32[]{:S(2)}, u32[]{:S(2)}) collective-permute-start(bf16[4,128,128]{2,1,0:T(8,128)(2,1)S(1)} %fusion.2), channel_id=1, source_target_pairs={{4,8},{5,9},{6,10},{7,11},{20,24},{21,25},{22,26},{23,27}} | collective-permute-start | bytes 393224 | tf_op jit(solution)/shard_map/ppermute | solution.py:555
  40.6 0.0 collective-permute-done.2
  40.6 0.2 fusion.1
  40.8 0.0 copy-start.3
  40.8 0.7 %collective-permute-start.6 = (bf16[4,128,128]{2,1,0:T(8,128)(2,1)S(1)}, bf16[4,128,128]{2,1,0:T(8,128)(2,1)S(1)}, u32[]{:S(2)}, u32[]{:S(2)}) collective-permute-start(bf16[4,128,128]{2,1,0:T(8,128)(2,1)S(1)} %fusion.1), channel_id=1, source_target_pairs={{8,12},{9,13},{10,14},{11,15},{24,28},{25,29},{26,30},{27,31}} | collective-permute-start | bytes 393224 | tf_op jit(solution)/shard_map/ppermute | solution.py:555
  41.4 5.4 %rows_pass.3 = (bf16[1024,512]{1,0:T(8,128)(2,1)S(1)}, bf16[1024,512]{1,0:T(8,128)(2,1)S(1)}) custom-call(bf16[1024,512]{1,0:T(8,128)(2,1)S(1)} %copy-done.2, bf16[16,2048]{1,0:T(8,128)(2,1)S(1)} %collective-permute-done.refs_2_.refs_1_, bf16[4,512]{1,0:T(4,128)(2,1)S(1)} %copy-done.8, bf16[2,1024,256]{2,1,0:T(8,128)(2,1)S(1)} %get-tuple-element.19.refs_3_, ...), custom_call_target="tpu_custom_call" | custom-call | flops 4096000000 | bytes 8388608 | tf_op jit(solution)/shard_map/rows_pass/pallas_call | solution.py:455
  46.8 0.0 collective-permute-done.4
  46.8 0.2 fusion.3
  47.0 0.7 %collective-permute-start.5 = (bf16[4,128,128]{2,1,0:T(8,128)(2,1)S(1)}, bf16[4,128,128]{2,1,0:T(8,128)(2,1)S(1)}, u32[]{:S(2)}, u32[]{:S(2)}) collective-permute-start(bf16[4,128,128]{2,1,0:T(8,128)(2,1)S(1)} %fusion.3), channel_id=1, source_target_pairs={{8,12},{9,13},{10,14},{11,15},{24,28},{25,29},{26,30},{27,31}} | collective-permute-start | bytes 393224 | tf_op jit(solution)/shard_map/ppermute | solution.py:555
  47.8 0.0 collective-permute-done.6.refs_3_
  47.8 0.0 copy-done.3
  47.8 2.7 %final_pass.2.refs_5_ = bf16[1024,1024]{1,0:T(8,128)(2,1)} custom-call(bf16[1024,512]{1,0:T(8,128)(2,1)S(1)} %get-tuple-element.31.refs_0_, bf16[1024,512]{1,0:T(8,128)(2,1)S(1)} %get-tuple-element.25.refs_1_, bf16[4,128,128]{2,1,0:T(8,128)(2,1)S(1)} %add.23.refs_2_, bf16[4,128,128]{2,1,0:T(8,128)(2,1)S(1)} %collective-permute-done.6.refs_3_, ...), custom_call_target="tpu_custom_call" | custom-call | tf_op jit(solution)/shard_map/final_pass/pallas_call | solution.py:519
  50.5 0.0 collective-permute-done.5.refs_3_
  50.5 2.7 %final_pass.3 = bf16[1024,1024]{1,0:T(8,128)(2,1)} custom-call(bf16[1024,512]{1,0:T(8,128)(2,1)S(1)} %get-tuple-element.28.refs_0_, bf16[1024,512]{1,0:T(8,128)(2,1)S(1)} %get-tuple-element.29.refs_1_, bf16[4,128,128]{2,1,0:T(8,128)(2,1)S(1)} %add.21.refs_2_, ...), custom_call_target="tpu_custom_call", output_to_operand_aliasing={{}: (5, {})} | custom-call | tf_op jit(solution)/shard_map/final_pass/pallas_call | solution.py:519
  (3 shorter events, 0.1 us)
Async XLA Ops:
  0.0 8.7 %copy-start = (bf16[1024,1024]{1,0:T(8,128)(2,1)S(1)}, bf16[1024,1024]{1,0:T(8,128)(2,1)}, u32[]{:S(2)}) copy-start(bf16[1024,1024]{1,0:T(8,128)(2,1)} %refs_1_.1) | copy-start | bytes 6291460
  0.0 8.7 %copy-start.1 = (bf16[1024,512]{1,0:T(8,128)(2,1)S(1)}, bf16[1024,512]{1,0:T(8,128)(2,1)}, u32[]{:S(2)}) copy-start(bf16[1024,512]{1,0:T(8,128)(2,1)} %refs_0_.3) | copy-start | bytes 3145732
  0.0 8.7 %copy-start.5 = (f32[1024,8]{0,1:T(8,128)S(1)}, f32[1024,8]{0,1:T(8,128)}, u32[]{:S(2)}) copy-start(f32[1024,8]{0,1:T(8,128)} %param.16) | copy-start | bytes 98308
  0.0 8.7 %copy-start.4 = (f32[1024,8]{0,1:T(8,128)S(1)}, f32[1024,8]{0,1:T(8,128)}, u32[]{:S(2)}) copy-start(f32[1024,8]{0,1:T(8,128)} %param.15) | copy-start | bytes 98308
  0.0 8.8 %copy-start.6 = (bf16[4,1024]{1,0:T(4,128)(2,1)S(1)}, bf16[4,1024]{1,0:T(4,128)(2,1)}, u32[]{:S(2)}) copy-start(bf16[4,1024]{1,0:T(4,128)(2,1)} %refs_4_.1) | copy-start | bytes 24580
  0.0 8.8 %copy-start.7 = (bf16[4,512]{1,0:T(4,128)(2,1)S(1)}, bf16[4,512]{1,0:T(4,128)(2,1)}, u32[]{:S(2)}) copy-start(bf16[4,512]{1,0:T(4,128)(2,1)} %refs_3_.1) | copy-start | bytes 12292
  1.6 7.1 %collective-permute-start = (bf16[16,2048]{1,0:T(8,128)(2,1)}, bf16[16,2048]{1,0:T(8,128)(2,1)S(1)}, u32[]{:S(2)}, u32[]{:S(2)}) collective-permute-start(bf16[16,2048]{1,0:T(8,128)(2,1)} %pack_rim.1), channel_id=1, source_target_pairs={{0,4},{4,8},{8,12},{1,5},{5,9},{9,13},{2,6},{6,10},{10,14},{3,7},{... | collective-permute-start | bytes 196616 | tf_op jit(solution)/shard_map/ppermute | solution.py:538
  8.8 25.5 %copy-start.2 = (bf16[1024,512]{1,0:T(8,128)(2,1)S(1)}, bf16[1024,512]{1,0:T(8,128)(2,1)}, u32[]{:S(2)}) copy-start(bf16[1024,512]{1,0:T(8,128)(2,1)} %refs_0_.5) | copy-start | bytes 3145732
  8.8 25.5 %copy-start.8 = (bf16[4,512]{1,0:T(4,128)(2,1)S(1)}, bf16[4,512]{1,0:T(4,128)(2,1)}, u32[]{:S(2)}) copy-start(bf16[4,512]{1,0:T(4,128)(2,1)} %refs_2_.3) | copy-start | bytes 12292
  26.2 7.2 %collective-permute-start.1 = (bf16[4,128,128]{2,1,0:T(8,128)(2,1)S(1)}, bf16[4,128,128]{2,1,0:T(8,128)(2,1)S(1)}, u32[]{:S(2)}, u32[]{:S(2)}) collective-permute-start(bf16[4,128,128]{2,1,0:T(8,128)(2,1)S(1)} %get-tuple-element.34), channel_id=1, source_target_pairs={{0,4},{1,5},{2,6},{3,7},{16,20},{17,21},{18,22},{19,23}} | collective-permute-start | bytes 393224 | tf_op jit(solution)/shard_map/ppermute | solution.py:555
  30.4 9.3 %collective-permute-start.3 = (bf16[4,128,128]{2,1,0:T(8,128)(2,1)S(1)}, bf16[4,128,128]{2,1,0:T(8,128)(2,1)S(1)}, u32[]{:S(2)}, u32[]{:S(2)}) collective-permute-start(bf16[4,128,128]{2,1,0:T(8,128)(2,1)S(1)} %get-tuple-element.33), channel_id=1, source_target_pairs={{0,4},{1,5},{2,6},{3,7},{16,20},{17,21},{18,22},{19,23}} | collective-permute-start | bytes 393224 | tf_op jit(solution)/shard_map/ppermute | solution.py:555
  33.6 7.0 %collective-permute-start.2 = (bf16[4,128,128]{2,1,0:T(8,128)(2,1)S(1)}, bf16[4,128,128]{2,1,0:T(8,128)(2,1)S(1)}, u32[]{:S(2)}, u32[]{:S(2)}) collective-permute-start(bf16[4,128,128]{2,1,0:T(8,128)(2,1)S(1)} %fusion), channel_id=1, source_target_pairs={{4,8},{5,9},{6,10},{7,11},{20,24},{21,25},{22,26},{23,27}} | collective-permute-start | bytes 393224 | tf_op jit(solution)/shard_map/ppermute | solution.py:555
  39.9 7.0 %collective-permute-start.4 = (bf16[4,128,128]{2,1,0:T(8,128)(2,1)S(1)}, bf16[4,128,128]{2,1,0:T(8,128)(2,1)S(1)}, u32[]{:S(2)}, u32[]{:S(2)}) collective-permute-start(bf16[4,128,128]{2,1,0:T(8,128)(2,1)S(1)} %fusion.2), channel_id=1, source_target_pairs={{4,8},{5,9},{6,10},{7,11},{20,24},{21,25},{22,26},{23,27}} | collective-permute-start | bytes 393224 | tf_op jit(solution)/shard_map/ppermute | solution.py:555
  40.8 7.1 %copy-start.3 = (f32[128]{0:T(128)S(1)}, f32[128]{0:T(128)}, u32[]{:S(2)}) copy-start(f32[128]{0:T(128)} %param.17) | copy-start | bytes 1540
  40.8 7.0 %collective-permute-start.6 = (bf16[4,128,128]{2,1,0:T(8,128)(2,1)S(1)}, bf16[4,128,128]{2,1,0:T(8,128)(2,1)S(1)}, u32[]{:S(2)}, u32[]{:S(2)}) collective-permute-start(bf16[4,128,128]{2,1,0:T(8,128)(2,1)S(1)} %fusion.1), channel_id=1, source_target_pairs={{8,12},{9,13},{10,14},{11,15},{24,28},{25,29},{26,30},{27,31}} | collective-permute-start | bytes 393224 | tf_op jit(solution)/shard_map/ppermute | solution.py:555
  47.0 3.5 %collective-permute-start.5 = (bf16[4,128,128]{2,1,0:T(8,128)(2,1)S(1)}, bf16[4,128,128]{2,1,0:T(8,128)(2,1)S(1)}, u32[]{:S(2)}, u32[]{:S(2)}) collective-permute-start(bf16[4,128,128]{2,1,0:T(8,128)(2,1)S(1)} %fusion.3), channel_id=1, source_target_pairs={{8,12},{9,13},{10,14},{11,15},{24,28},{25,29},{26,30},{27,31}} | collective-permute-start | bytes 393224 | tf_op jit(solution)/shard_map/ppermute | solution.py:555

commit v7 on v5

--- a/solution.py
+++ b/solution.py
@@ -13,10 +13,10 @@
 BASE = 8
 HALO = 8
 RIM = 16
+FOLD = 4
 PARTS = 2
 SPAN_X = 512
 SPAN_Y = 512
-SPAN_Z = 256
 EPSILON = 1e-06
 LOG2E = 1.4426950408889634
 F32 = jnp.float32
@@ -149,32 +149,43 @@
     return [total[at * heads : (at + 1) * heads] for at in range(span // CHUNK)]
 
 
-def rim_kernel(query_ref, key_ref, value_ref, out_ref, done):
-    copies = []
+def rim_kernel(query_ref, key_ref, value_ref, out_ref, rows):
+    piece = rows.shape[1]
+    rows[...] = jnp.zeros_like(rows)
     at = 0
-    for place, ref in enumerate((query_ref, key_ref, value_ref)):
-        rows, width = ref.shape
-        source = ref.at[pl.ds(rows - RIM, RIM), :]
-        target = out_ref.at[:, pl.ds(at, width)]
-        copies.append(pltpu.make_async_copy(source, target, done.at[place]))
-        at += width
-    for copy in copies:
-        copy.start()
-    for copy in copies:
-        copy.wait()
+    for ref in (query_ref, key_ref, value_ref):
+        last = ref[...].astype(F32)
+        for tile in range(0, ref.shape[1], 128):
+            place, lane = (at + tile) // piece, (at + tile) % piece
+            for back in range(KW - 1):
+                row = back * FOLD + place
+                source = RIM - (KW - 1) + back
+                rows[row : row + 1, lane : lane + 128] = last[source : source + 1, tile : tile + 128]
+        at += ref.shape[1]
+    out_ref[...] = rows[...].astype(BF16)
 
 
 def pack_rim(query_raw, key_raw, value_raw):
-    width = query_raw.shape[1] + key_raw.shape[1] + value_raw.shape[1]
-    anywhere = pl.BlockSpec(memory_space=pl.ANY)
+    last = query_raw.shape[0] // RIM - 1
+    widths = [array.shape[1] for array in (query_raw, key_raw, value_raw)]
+    piece = sum(widths) // FOLD
     return pl.pallas_call(
         rim_kernel,
-        in_specs=[anywhere] * 3,
-        out_specs=anywhere,
-        out_shape=jax.ShapeDtypeStruct((RIM, width), BF16),
-        scratch_shapes=[pltpu.SemaphoreType.DMA((3,))],
+        grid=(1,),
+        in_specs=[pl.BlockSpec((RIM, width), lambda i: (last, 0)) for width in widths],
+        out_specs=pl.BlockSpec((RIM, piece), lambda i: (0, 0)),
+        out_shape=jax.ShapeDtypeStruct((RIM, piece), BF16),
+        scratch_shapes=[pltpu.VMEM((RIM, piece), F32)],
         name="pack_rim",
     )(query_raw, key_raw, value_raw)
+
+
+def unpack_rim(rim, wide, tile, at):
+    piece = rim.shape[1]
+    for back in range(KW - 1):
+        row = back * FOLD + at // piece
+        place = HALO - (KW - 1) + back
+        wide[tile, place : place + 1] = rim[row : row + 1, at % piece : at % piece + 128]
 
 
 def log_weights(logit):
@@ -220,9 +231,10 @@
         rows, cols = iotas((DK, WIDE))
         for head in range(vheads):
             state[head] = (rows == cols).astype(F32)
+        rim = rim_ref[...].astype(F32)
         for tile in range(tiles):
             at = rim_from[0] + tile * DK if tile < kheads else rim_from[1] + (tile - kheads) * DV
-            wide[tile, 0:HALO] = rim_ref[:, at : at + 128].astype(F32)[RIM - HALO :]
+            unpack_rim(rim, wide, tile, at)
 
     def prepare(step):
         now_rows = pl.ds(pl.multiple_of(step * span, span), span)
@@ -378,8 +390,7 @@
     first_head = group * vheads
     query_from = group * kheads * DK
     for tile in range(kheads):
-        at = slice(query_from + tile * DK, query_from + (tile + 1) * DK)
-        wide[tile, 0:HALO] = rim_ref[:, at].astype(F32)[RIM - HALO :]
+        unpack_rim(rim_ref[...].astype(F32), wide, tile, query_from + tile * DK)
 
     def advance(step, carry):
         base = pl.multiple_of(step * span, span)
@@ -454,56 +465,46 @@
     )(query_raw, rim, conv_query, keys, gate_flat, logit_flat, solved, before)
 
 
-def final_kernel(part, span, rows_ref, local_ref, early_ref, late_ref, gain_ref, *rest):
-    out_ref, ready, done = rest[-3:]
+def final_kernel(vheads, rows_ref, local_ref, early_ref, late_ref, gain_ref, *rest):
+    out_ref = rest[-1]
     gain = gain_ref[...]
-    vheads = early_ref.shape[0]
-    width = vheads * DV
-    starts = [early_ref[head] + late_ref[head] for head in range(vheads)]
-    copies = []
-    for turn in range(rows_ref.shape[0] // span):
-        here = slice(turn * span, (turn + 1) * span)
-        for head in range(vheads):
-            there = slice(head * DV, (head + 1) * DV)
-            output = dot(rows_ref[here, there], starts[head]) + local_ref[here, there].astype(F32)
-            square = output * output
-            if head % 2:
-                total = row_sums(square)
-            else:
-                total = jnp.sum(square, axis=-1, keepdims=True)
-            scale = lax.rsqrt(total * (1.0 / DV) + EPSILON)
-            ready[here, there] = (output * scale * gain).astype(BF16)
-        target = out_ref.at[pl.ds(turn * span, span), pl.ds(part * width, width)]
-        source = ready.at[pl.ds(turn * span, span), :]
-        copies.append(pltpu.make_async_copy(source, target, done.at[turn]))
-        copies[-1].start()
-    for copy in copies:
-        copy.wait()
+    span = out_ref.shape[0]
+    now_rows = pl.ds(pl.multiple_of(pl.program_id(0) * span, span), span)
+    for head in range(vheads):
+        there = slice(head * DV, (head + 1) * DV)
+        start = early_ref[head] + late_ref[head]
+        output = dot(rows_ref[now_rows, there], start) + local_ref[now_rows, there].astype(F32)
+        square = output * output
+        if head % 2:
+            total = row_sums(square)
+        else:
+            total = jnp.sum(square, axis=-1, keepdims=True)
+        mean = total * (1.0 / DV)
+        out_ref[:, there] = (output * lax.rsqrt(mean + EPSILON) * gain).astype(BF16)
 
 
 def final_pass(part, rows, local, early, late, gain, earlier):
     tok_count = rows.shape[0]
     vheads = early.shape[0]
-    span = min(SPAN_Z, tok_count)
+    span = min(512, tok_count)
+
+    def along(width, column):
+        return pl.BlockSpec((span, width), lambda i: (i, column))
 
     def kernel(*refs):
-        final_kernel(part, span, *refs)
-
-    anywhere = pl.BlockSpec(memory_space=pl.ANY)
+        final_kernel(vheads, *refs)
+
     arrays = [rows, local, early, late, gain]
     specs = [VMEM] * 5
     if earlier is not None:
         arrays.append(earlier)
-        specs.append(anywhere)
+        specs.append(pl.BlockSpec(memory_space=pl.ANY))
     return pl.pallas_call(
         kernel,
+        grid=(tok_count // span,),
         in_specs=specs,
-        out_specs=anywhere,
+        out_specs=along(vheads * DV, part),
         out_shape=jax.ShapeDtypeStruct((tok_count, PARTS * vheads * DV), BF16),
-        scratch_shapes=[
-            pltpu.VMEM((tok_count, vheads * DV), BF16),
-            pltpu.SemaphoreType.DMA((tok_count // span,)),
-        ],
         input_output_aliases={} if earlier is None else {5: 0},
         compiler_params=pltpu.CompilerParams(vmem_limit_bytes=12 * 1024 * 1024),
         name="final_pass",

time: 50.1 us -> 47.5 us (0.948)
  Pallas kernels: 33.2 us -> 31.3 us
  waiting for transfers between devices: 2.22 us -> 1.65 us
    pallas_call x3, Pallas kernels: 7.4 us -> 5.45 us  [the longest x2 3.87 us: final_pass(): pl.pallas_call(kernel, grid=(tok_count // span,), in_specs=specs, out_spe...]
    ppermute x1, waiting for transfers between devices: 2.2 us -> 1.64 us  [shards(): lax.ppermute(pack_rim(query_raw, key_raw, value_raw), 'ctx', [(at, at + 1...]
  transfers between devices with their start and end apart: 7 -> 7, of which waited for: 1 -> 1; matrix products, arithmetic and copies ran while one was open for 2% -> 2% of each run, Pallas kernels for 39% -> 41%
where the time goes in v7:
time: 47.5 us; the launch traced here: 47.3 us
  Pallas kernels  31.3 us (66%)
  starting transfers between devices  13.2 us (28%)
  waiting for transfers between devices  1.65 us (3%)
  matrix products  0.71 us (1%)
    pallas_call x2, Pallas kernels, memory_pass(): pl.pallas_call(kernel, in_specs=[VMEM] * 7, out_specs=[VMEM] * 5, out_sha...  16.9 us
    pallas_call x2, Pallas kernels, rows_pass(): pl.pallas_call(kernel, in_specs=[VMEM] * 8, out_specs=[VMEM] * 2, out_sha...  8.9 us
    ppermute x6, starting transfers between devices, send(): lax.ppermute(moved[part][source], 'ctx', [(source, source + 1)])  8.32 us
    ppermute x1, starting transfers between devices, shards(): lax.ppermute(pack_rim(query_raw, key_raw, value_raw), 'ctx', [(at, at + 1...  4.93 us
    pallas_call x2, Pallas kernels, final_pass(): pl.pallas_call(kernel, grid=(tok_count // span,), in_specs=specs, out_spe...  3.87 us
    ppermute x1, waiting for transfers between devices, shards(): lax.ppermute(pack_rim(query_raw, key_raw, value_raw), 'ctx', [(at, at + 1...  1.64 us
    pallas_call x1, Pallas kernels, pack_rim(): pl.pallas_call(rim_kernel, grid=(1,), in_specs=[pl.BlockSpec((RIM, width)...  1.57 us
  transfers between devices with their start and end apart: 7, of which 1 were waited for; matrix products, arithmetic and copies ran while one was open for 2% of the time, Pallas kernels for 41%

profile of v7, /device:TPU:0, one launch (start us, length us, event | category | flops | bytes accessed | tf_op | source)
XLA Modules:
  0.0 47.3 jit_solution(15554006605809402312)
XLA Ops:
  0.0 0.0 copy-start
  0.0 0.0 copy-start.1
  0.0 0.0 copy-start.6
  0.0 0.0 copy-start.7
  0.0 0.0 copy-start.5
  0.0 0.0 copy-start.4
  0.0 1.6 %pack_rim.1 = bf16[16,512]{1,0:T(8,128)(2,1)} custom-call(bf16[1024,512]{1,0:T(8,128)(2,1)} %refs_0_.7, bf16[1024,512]{1,0:T(8,128)(2,1)} %refs_0_.5, bf16[1024,1024]{1,0:T(8,128)(2,1)} %refs_1_.3), custom_call_target="tpu_custom_call" | custom-call | tf_op jit(solution)/shard_map/pack_rim/pallas_call | solution.py:172
  1.6 4.9 %collective-permute-start = (bf16[16,512]{1,0:T(8,128)(2,1)}, bf16[16,512]{1,0:T(8,128)(2,1)S(1)}, u32[]{:S(2)}, u32[]{:S(2)}) collective-permute-start(bf16[16,512]{1,0:T(8,128)(2,1)} %pack_rim.1), channel_id=1, source_target_pairs={{0,4},{4,8},{8,12},{1,5},{5,9},{9,13},{2,6},{6,10},{10,14},{3,7},{... | collective-permute-start | bytes 49160 | tf_op jit(solution)/shard_map/ppermute | solution.py:518
  6.5 1.6 %collective-permute-done.refs_2_.refs_1_ = bf16[16,512]{1,0:T(8,128)(2,1)S(1)} collective-permute-done((bf16[16,512]{1,0:T(8,128)(2,1)}, bf16[16,512]{1,0:T(8,128)(2,1)S(1)}, u32[]{:S(2)}, u32[]{:S(2)}) %collective-permute-start) | collective-permute-done | bytes 16416 | tf_op jit(solution)/shard_map/ppermute | solution.py:518
  8.2 0.0 copy-done
  8.2 0.0 copy-done.1
  8.2 0.0 copy-done.6
  8.2 0.0 copy-done.7
  8.2 0.0 copy-done.5
  8.2 0.0 copy-done.4
  8.2 8.5 %memory_pass.3 = (bf16[1024,256]{1,0:T(8,128)(2,1)S(1)}, bf16[1024,1024]{1,0:T(8,128)(2,1)S(1)}, bf16[8,4,128,256]{3,2,1,0:T(8,128)(2,1)S(1)}, bf16[4,128,128]{2,1,0:T(8,128)(2,1)S(1)}, f32[4,128,128]{2,1,0:T(8,128)S(1)}) custom-call(bf16[1024,512]{1,0:T(8,128)(2,1)S(1)} %copy-done.1, bf16[1024,1024]{1,0:T(8,128)(2,1)S(1)} %copy-done, ...), custom_call_target="tpu_custom_call" | custom-call | flops 8192000000 | bytes 8388608 | tf_op jit(solution)/shard_map/memory_pass/pallas_call | solution.py:344
  16.7 0.0 copy-start.2
  16.7 0.0 copy-start.8
  16.7 4.3 %collective-permute-start.1 = (bf16[4,128,128]{2,1,0:T(8,128)(2,1)S(1)}, bf16[4,128,128]{2,1,0:T(8,128)(2,1)S(1)}, u32[]{:S(2)}, u32[]{:S(2)}) collective-permute-start(bf16[4,128,128]{2,1,0:T(8,128)(2,1)S(1)} %convert_element_type.18), channel_id=1, source_target_pairs={{0,4},{1,5},{2,6},{3,7},{16,20},{17,21},{18,22},{19,23}} | collective-permute-start | bytes 393224 | tf_op jit(solution)/shard_map/ppermute | solution.py:536
  21.1 8.5 %memory_pass.2 = (bf16[1024,256]{1,0:T(8,128)(2,1)S(1)}, bf16[1024,1024]{1,0:T(8,128)(2,1)S(1)}, bf16[8,4,128,256]{3,2,1,0:T(8,128)(2,1)S(1)}, bf16[4,128,128]{2,1,0:T(8,128)(2,1)S(1)}, f32[4,128,128]{2,1,0:T(8,128)S(1)}) custom-call(bf16[1024,512]{1,0:T(8,128)(2,1)S(1)} %copy-done.1, bf16[1024,1024]{1,0:T(8,128)(2,1)S(1)} %copy-done, ...), custom_call_target="tpu_custom_call" | custom-call | flops 8192000000 | bytes 8388608 | tf_op jit(solution)/shard_map/memory_pass/pallas_call | solution.py:344
  29.6 1.3 %collective-permute-start.3 = (bf16[4,128,128]{2,1,0:T(8,128)(2,1)S(1)}, bf16[4,128,128]{2,1,0:T(8,128)(2,1)S(1)}, u32[]{:S(2)}, u32[]{:S(2)}) collective-permute-start(bf16[4,128,128]{2,1,0:T(8,128)(2,1)S(1)} %convert_element_type.21), channel_id=1, source_target_pairs={{0,4},{1,5},{2,6},{3,7},{16,20},{17,21},{18,22},{19,23}} | collective-permute-start | bytes 393224 | tf_op jit(solution)/shard_map/ppermute | solution.py:536
  30.9 0.0 collective-permute-done.1
  30.9 0.2 fusion
  31.1 0.7 %collective-permute-start.2 = (bf16[4,128,128]{2,1,0:T(8,128)(2,1)S(1)}, bf16[4,128,128]{2,1,0:T(8,128)(2,1)S(1)}, u32[]{:S(2)}, u32[]{:S(2)}) collective-permute-start(bf16[4,128,128]{2,1,0:T(8,128)(2,1)S(1)} %fusion), channel_id=1, source_target_pairs={{4,8},{5,9},{6,10},{7,11},{20,24},{21,25},{22,26},{23,27}} | collective-permute-start | bytes 393224 | tf_op jit(solution)/shard_map/ppermute | solution.py:536
  31.8 0.0 copy-done.2
  31.8 0.0 copy-done.8
  31.8 4.5 %rows_pass.2 = (bf16[1024,512]{1,0:T(8,128)(2,1)S(1)}, bf16[1024,512]{1,0:T(8,128)(2,1)S(1)}) custom-call(bf16[1024,512]{1,0:T(8,128)(2,1)S(1)} %copy-done.2, bf16[16,512]{1,0:T(8,128)(2,1)S(1)} %collective-permute-done.refs_2_.refs_1_, bf16[4,512]{1,0:T(4,128)(2,1)S(1)} %copy-done.8, bf16[1024,256]{1,0:T(8,128)(2,1)S(1)} %get-tuple-element.30.refs_3_, ...), custom_call_target="tpu_custom_call" | custom-call | flops 4096000000 | bytes 8388608 | tf_op jit(solution)/shard_map/rows_pass/pallas_call | solution.py:451
  36.2 0.0 collective-permute-done.3
  36.2 0.2 fusion.2
  36.4 0.7 %collective-permute-start.4 = (bf16[4,128,128]{2,1,0:T(8,128)(2,1)S(1)}, bf16[4,128,128]{2,1,0:T(8,128)(2,1)S(1)}, u32[]{:S(2)}, u32[]{:S(2)}) collective-permute-start(bf16[4,128,128]{2,1,0:T(8,128)(2,1)S(1)} %fusion.2), channel_id=1, source_target_pairs={{4,8},{5,9},{6,10},{7,11},{20,24},{21,25},{22,26},{23,27}} | collective-permute-start | bytes 393224 | tf_op jit(solution)/shard_map/ppermute | solution.py:536
  37.1 0.0 collective-permute-done.2
  37.1 0.2 fusion.1
  37.3 0.7 %collective-permute-start.6 = (bf16[4,128,128]{2,1,0:T(8,128)(2,1)S(1)}, bf16[4,128,128]{2,1,0:T(8,128)(2,1)S(1)}, u32[]{:S(2)}, u32[]{:S(2)}) collective-permute-start(bf16[4,128,128]{2,1,0:T(8,128)(2,1)S(1)} %fusion.1), channel_id=1, source_target_pairs={{8,12},{9,13},{10,14},{11,15},{24,28},{25,29},{26,30},{27,31}} | collective-permute-start | bytes 393224 | tf_op jit(solution)/shard_map/ppermute | solution.py:536
  38.0 0.0 copy-start.3
  38.0 4.4 %rows_pass.3 = (bf16[1024,512]{1,0:T(8,128)(2,1)S(1)}, bf16[1024,512]{1,0:T(8,128)(2,1)S(1)}) custom-call(bf16[1024,512]{1,0:T(8,128)(2,1)S(1)} %copy-done.2, bf16[16,512]{1,0:T(8,128)(2,1)S(1)} %collective-permute-done.refs_2_.refs_1_, bf16[4,512]{1,0:T(4,128)(2,1)S(1)} %copy-done.8, bf16[1024,256]{1,0:T(8,128)(2,1)S(1)} %get-tuple-element.24.refs_3_, ...), custom_call_target="tpu_custom_call" | custom-call | flops 4096000000 | bytes 8388608 | tf_op jit(solution)/shard_map/rows_pass/pallas_call | solution.py:451
  42.5 0.0 collective-permute-done.4
  42.5 0.2 fusion.3
  42.7 0.7 %collective-permute-start.5 = (bf16[4,128,128]{2,1,0:T(8,128)(2,1)S(1)}, bf16[4,128,128]{2,1,0:T(8,128)(2,1)S(1)}, u32[]{:S(2)}, u32[]{:S(2)}) collective-permute-start(bf16[4,128,128]{2,1,0:T(8,128)(2,1)S(1)} %fusion.3), channel_id=1, source_target_pairs={{8,12},{9,13},{10,14},{11,15},{24,28},{25,29},{26,30},{27,31}} | collective-permute-start | bytes 393224 | tf_op jit(solution)/shard_map/ppermute | solution.py:536
  43.4 0.0 collective-permute-done.6.refs_3_
  43.4 0.0 copy-done.3
  43.4 1.9 %final_pass.2.refs_5_ = bf16[1024,1024]{1,0:T(8,128)(2,1)} custom-call(bf16[1024,512]{1,0:T(8,128)(2,1)S(1)} %get-tuple-element.41.refs_0_, bf16[1024,512]{1,0:T(8,128)(2,1)S(1)} %get-tuple-element.34.refs_1_, bf16[4,128,128]{2,1,0:T(8,128)(2,1)S(1)} %add.23.refs_2_, bf16[4,128,128]{2,1,0:T(8,128)(2,1)S(1)} %collective-permute-done.6.refs_3_, ...), custom_call_target="tpu_custom_call" | custom-call | tf_op jit(solution)/shard_map/final_pass/pallas_call | solution.py:502
  45.4 0.0 collective-permute-done.5.refs_3_
  45.4 1.9 %final_pass.3 = bf16[1024,1024]{1,0:T(8,128)(2,1)} custom-call(bf16[1024,512]{1,0:T(8,128)(2,1)S(1)} %get-tuple-element.38.refs_0_, bf16[1024,512]{1,0:T(8,128)(2,1)S(1)} %get-tuple-element.39.refs_1_, bf16[4,128,128]{2,1,0:T(8,128)(2,1)S(1)} %add.21.refs_2_, ...), custom_call_target="tpu_custom_call", output_to_operand_aliasing={{}: (5, {})} | custom-call | tf_op jit(solution)/shard_map/final_pass/pallas_call | solution.py:502
  (4 shorter events, 0.1 us)
Async XLA Ops:
  0.0 8.2 %copy-start = (bf16[1024,1024]{1,0:T(8,128)(2,1)S(1)}, bf16[1024,1024]{1,0:T(8,128)(2,1)}, u32[]{:S(2)}) copy-start(bf16[1024,1024]{1,0:T(8,128)(2,1)} %refs_1_.3) | copy-start | bytes 6291460
  0.0 8.2 %copy-start.1 = (bf16[1024,512]{1,0:T(8,128)(2,1)S(1)}, bf16[1024,512]{1,0:T(8,128)(2,1)}, u32[]{:S(2)}) copy-start(bf16[1024,512]{1,0:T(8,128)(2,1)} %refs_0_.5) | copy-start | bytes 3145732
  0.0 8.2 %copy-start.6 = (bf16[4,1024]{1,0:T(4,128)(2,1)S(1)}, bf16[4,1024]{1,0:T(4,128)(2,1)}, u32[]{:S(2)}) copy-start(bf16[4,1024]{1,0:T(4,128)(2,1)} %refs_4_.3) | copy-start | bytes 24580
  0.0 8.2 %copy-start.7 = (bf16[4,512]{1,0:T(4,128)(2,1)S(1)}, bf16[4,512]{1,0:T(4,128)(2,1)}, u32[]{:S(2)}) copy-start(bf16[4,512]{1,0:T(4,128)(2,1)} %refs_3_.3) | copy-start | bytes 12292
  0.0 8.2 %copy-start.5 = (f32[1024,8]{0,1:T(8,128)S(1)}, f32[1024,8]{0,1:T(8,128)}, u32[]{:S(2)}) copy-start(f32[1024,8]{0,1:T(8,128)} %param.16) | copy-start | bytes 98308
  0.0 8.2 %copy-start.4 = (f32[1024,8]{0,1:T(8,128)S(1)}, f32[1024,8]{0,1:T(8,128)}, u32[]{:S(2)}) copy-start(f32[1024,8]{0,1:T(8,128)} %param.15) | copy-start | bytes 98308
  1.6 6.6 %collective-permute-start = (bf16[16,512]{1,0:T(8,128)(2,1)}, bf16[16,512]{1,0:T(8,128)(2,1)S(1)}, u32[]{:S(2)}, u32[]{:S(2)}) collective-permute-start(bf16[16,512]{1,0:T(8,128)(2,1)} %pack_rim.1), channel_id=1, source_target_pairs={{0,4},{4,8},{8,12},{1,5},{5,9},{9,13},{2,6},{6,10},{10,14},{3,7},{... | collective-permute-start | bytes 49160 | tf_op jit(solution)/shard_map/ppermute | solution.py:518
  16.7 15.1 %copy-start.2 = (bf16[1024,512]{1,0:T(8,128)(2,1)S(1)}, bf16[1024,512]{1,0:T(8,128)(2,1)}, u32[]{:S(2)}) copy-start(bf16[1024,512]{1,0:T(8,128)(2,1)} %refs_0_.7) | copy-start | bytes 3145732
  16.7 15.1 %copy-start.8 = (bf16[4,512]{1,0:T(4,128)(2,1)S(1)}, bf16[4,512]{1,0:T(4,128)(2,1)}, u32[]{:S(2)}) copy-start(bf16[4,512]{1,0:T(4,128)(2,1)} %refs_2_.3) | copy-start | bytes 12292
  16.7 14.2 %collective-permute-start.1 = (bf16[4,128,128]{2,1,0:T(8,128)(2,1)S(1)}, bf16[4,128,128]{2,1,0:T(8,128)(2,1)S(1)}, u32[]{:S(2)}, u32[]{:S(2)}) collective-permute-start(bf16[4,128,128]{2,1,0:T(8,128)(2,1)S(1)} %convert_element_type.18), channel_id=1, source_target_pairs={{0,4},{1,5},{2,6},{3,7},{16,20},{17,21},{18,22},{19,23}} | collective-permute-start | bytes 393224 | tf_op jit(solution)/shard_map/ppermute | solution.py:536
  29.6 6.7 %collective-permute-start.3 = (bf16[4,128,128]{2,1,0:T(8,128)(2,1)S(1)}, bf16[4,128,128]{2,1,0:T(8,128)(2,1)S(1)}, u32[]{:S(2)}, u32[]{:S(2)}) collective-permute-start(bf16[4,128,128]{2,1,0:T(8,128)(2,1)S(1)} %convert_element_type.21), channel_id=1, source_target_pairs={{0,4},{1,5},{2,6},{3,7},{16,20},{17,21},{18,22},{19,23}} | collective-permute-start | bytes 393224 | tf_op jit(solution)/shard_map/ppermute | solution.py:536
  31.1 6.0 %collective-permute-start.2 = (bf16[4,128,128]{2,1,0:T(8,128)(2,1)S(1)}, bf16[4,128,128]{2,1,0:T(8,128)(2,1)S(1)}, u32[]{:S(2)}, u32[]{:S(2)}) collective-permute-start(bf16[4,128,128]{2,1,0:T(8,128)(2,1)S(1)} %fusion), channel_id=1, source_target_pairs={{4,8},{5,9},{6,10},{7,11},{20,24},{21,25},{22,26},{23,27}} | collective-permute-start | bytes 393224 | tf_op jit(solution)/shard_map/ppermute | solution.py:536
  36.4 6.0 %collective-permute-start.4 = (bf16[4,128,128]{2,1,0:T(8,128)(2,1)S(1)}, bf16[4,128,128]{2,1,0:T(8,128)(2,1)S(1)}, u32[]{:S(2)}, u32[]{:S(2)}) collective-permute-start(bf16[4,128,128]{2,1,0:T(8,128)(2,1)S(1)} %fusion.2), channel_id=1, source_target_pairs={{4,8},{5,9},{6,10},{7,11},{20,24},{21,25},{22,26},{23,27}} | collective-permute-start | bytes 393224 | tf_op jit(solution)/shard_map/ppermute | solution.py:536
  37.3 6.1 %collective-permute-start.6 = (bf16[4,128,128]{2,1,0:T(8,128)(2,1)S(1)}, bf16[4,128,128]{2,1,0:T(8,128)(2,1)S(1)}, u32[]{:S(2)}, u32[]{:S(2)}) collective-permute-start(bf16[4,128,128]{2,1,0:T(8,128)(2,1)S(1)} %fusion.1), channel_id=1, source_target_pairs={{8,12},{9,13},{10,14},{11,15},{24,28},{25,29},{26,30},{27,31}} | collective-permute-start | bytes 393224 | tf_op jit(solution)/shard_map/ppermute | solution.py:536
  38.0 5.4 %copy-start.3 = (f32[128]{0:T(128)S(1)}, f32[128]{0:T(128)}, u32[]{:S(2)}) copy-start(f32[128]{0:T(128)} %param.17) | copy-start | bytes 1540
  42.7 2.7 %collective-permute-start.5 = (bf16[4,128,128]{2,1,0:T(8,128)(2,1)S(1)}, bf16[4,128,128]{2,1,0:T(8,128)(2,1)S(1)}, u32[]{:S(2)}, u32[]{:S(2)}) collective-permute-start(bf16[4,128,128]{2,1,0:T(8,128)(2,1)S(1)} %fusion.3), channel_id=1, source_target_pairs={{8,12},{9,13},{10,14},{11,15},{24,28},{25,29},{26,30},{27,31}} | collective-permute-start | bytes 393224 | tf_op jit(solution)/shard_map/ppermute | solution.py:536

commit v8 on v7

--- a/solution.py
+++ b/solution.py
@@ -15,7 +15,7 @@
 RIM = 16
 FOLD = 4
 PARTS = 2
-SPAN_X = 512
+SPAN_X = 1024
 SPAN_Y = 512
 EPSILON = 1e-06
 LOG2E = 1.4426950408889634
@@ -361,7 +361,7 @@
             pltpu.VMEM((items, CHUNK, WIDE), BF16),
             pltpu.VMEM((span // CHUNK, all_vheads, CHUNK), F32),
         ],
-        compiler_params=pltpu.CompilerParams(vmem_limit_bytes=20 * 1024 * 1024),
+        compiler_params=pltpu.CompilerParams(vmem_limit_bytes=32 * 1024 * 1024),
         cost_estimate=pl.CostEstimate(
             flops=2 * tok_count * vheads * 1000 * 1000, bytes_accessed=1 << 23, transcendentals=0
         ),

time: 47.5 us -> 44.6 us (0.939)
  Pallas kernels: 31.3 us -> 28.2 us
    pallas_call x2, Pallas kernels: 16.9 us -> 13.9 us  [memory_pass(): pl.pallas_call(kernel, in_specs=[VMEM] * 7, out_specs=[VMEM] * 5, out_sha...]
  transfers between devices with their start and end apart: 7 -> 7, of which waited for: 1 -> 1; matrix products, arithmetic and copies ran while one was open for 2% -> 2% of each run, Pallas kernels for 41% -> 40%
where the time goes in v8:
time: 44.6 us; the launch traced here: 44.4 us
  Pallas kernels  28.2 us (63%)
  starting transfers between devices  13.4 us (30%)
  waiting for transfers between devices  1.65 us (4%)
  matrix products  0.71 us (2%)
    pallas_call x2, Pallas kernels, memory_pass(): pl.pallas_call(kernel, in_specs=[VMEM] * 7, out_specs=[VMEM] * 5, out_sha...  13.9 us
    pallas_call x2, Pallas kernels, rows_pass(): pl.pallas_call(kernel, in_specs=[VMEM] * 8, out_specs=[VMEM] * 2, out_sha...  8.89 us
    ppermute x6, starting transfers between devices, send(): lax.ppermute(moved[part][source], 'ctx', [(source, source + 1)])  8.5 us
    ppermute x1, starting transfers between devices, shards(): lax.ppermute(pack_rim(query_raw, key_raw, value_raw), 'ctx', [(at, at + 1...  4.93 us
    pallas_call x2, Pallas kernels, final_pass(): pl.pallas_call(kernel, grid=(tok_count // span,), in_specs=specs, out_spe...  3.88 us
    ppermute x1, waiting for transfers between devices, shards(): lax.ppermute(pack_rim(query_raw, key_raw, value_raw), 'ctx', [(at, at + 1...  1.64 us
    pallas_call x1, Pallas kernels, pack_rim(): pl.pallas_call(rim_kernel, grid=(1,), in_specs=[pl.BlockSpec((RIM, width)...  1.57 us
  transfers between devices with their start and end apart: 7, of which 1 were waited for; matrix products, arithmetic and copies ran while one was open for 2% of the time, Pallas kernels for 40%

profile of v8, /device:TPU:0, one launch (start us, length us, event | category | flops | bytes accessed | tf_op | source)
XLA Modules:
  0.0 44.4 jit_solution(6744516339988567617)
XLA Ops:
  0.0 0.0 copy-start
  0.0 0.0 copy-start.1
  0.0 0.0 copy-start.6
  0.0 0.0 copy-start.7
  0.0 0.0 copy-start.5
  0.0 0.0 copy-start.4
  0.0 1.6 %pack_rim.1 = bf16[16,512]{1,0:T(8,128)(2,1)} custom-call(bf16[1024,512]{1,0:T(8,128)(2,1)} %refs_0_.7, bf16[1024,512]{1,0:T(8,128)(2,1)} %refs_0_.5, bf16[1024,1024]{1,0:T(8,128)(2,1)} %refs_1_.3), custom_call_target="tpu_custom_call" | custom-call | tf_op jit(solution)/shard_map/pack_rim/pallas_call | solution.py:172
  1.6 4.9 %collective-permute-start = (bf16[16,512]{1,0:T(8,128)(2,1)}, bf16[16,512]{1,0:T(8,128)(2,1)S(1)}, u32[]{:S(2)}, u32[]{:S(2)}) collective-permute-start(bf16[16,512]{1,0:T(8,128)(2,1)} %pack_rim.1), channel_id=1, source_target_pairs={{0,4},{4,8},{8,12},{1,5},{5,9},{9,13},{2,6},{6,10},{10,14},{3,7},{... | collective-permute-start | bytes 49160 | tf_op jit(solution)/shard_map/ppermute | solution.py:518
  6.5 1.6 %collective-permute-done.refs_2_.refs_1_ = bf16[16,512]{1,0:T(8,128)(2,1)S(1)} collective-permute-done((bf16[16,512]{1,0:T(8,128)(2,1)}, bf16[16,512]{1,0:T(8,128)(2,1)S(1)}, u32[]{:S(2)}, u32[]{:S(2)}) %collective-permute-start) | collective-permute-done | bytes 16416 | tf_op jit(solution)/shard_map/ppermute | solution.py:518
  8.2 0.0 copy-done
  8.2 0.0 copy-done.1
  8.2 0.0 copy-done.6
  8.2 0.0 copy-done.7
  8.2 0.0 copy-done.5
  8.2 0.0 copy-done.4
  8.2 6.9 %memory_pass.3 = (bf16[1024,256]{1,0:T(8,128)(2,1)S(1)}, bf16[1024,1024]{1,0:T(8,128)(2,1)S(1)}, bf16[8,4,128,256]{3,2,1,0:T(8,128)(2,1)S(1)}, bf16[4,128,128]{2,1,0:T(8,128)(2,1)S(1)}, f32[4,128,128]{2,1,0:T(8,128)S(1)}) custom-call(bf16[1024,512]{1,0:T(8,128)(2,1)S(1)} %copy-done.1, bf16[1024,1024]{1,0:T(8,128)(2,1)S(1)} %copy-done, ...), custom_call_target="tpu_custom_call" | custom-call | flops 8192000000 | bytes 8388608 | tf_op jit(solution)/shard_map/memory_pass/pallas_call | solution.py:344
  15.2 0.0 copy-start.2
  15.2 0.0 copy-start.8
  15.2 4.5 %collective-permute-start.1 = (bf16[4,128,128]{2,1,0:T(8,128)(2,1)S(1)}, bf16[4,128,128]{2,1,0:T(8,128)(2,1)S(1)}, u32[]{:S(2)}, u32[]{:S(2)}) collective-permute-start(bf16[4,128,128]{2,1,0:T(8,128)(2,1)S(1)} %convert_element_type.18), channel_id=1, source_target_pairs={{0,4},{1,5},{2,6},{3,7},{16,20},{17,21},{18,22},{19,23}} | collective-permute-start | bytes 393224 | tf_op jit(solution)/shard_map/ppermute | solution.py:536
  19.7 6.9 %memory_pass.2 = (bf16[1024,256]{1,0:T(8,128)(2,1)S(1)}, bf16[1024,1024]{1,0:T(8,128)(2,1)S(1)}, bf16[8,4,128,256]{3,2,1,0:T(8,128)(2,1)S(1)}, bf16[4,128,128]{2,1,0:T(8,128)(2,1)S(1)}, f32[4,128,128]{2,1,0:T(8,128)S(1)}) custom-call(bf16[1024,512]{1,0:T(8,128)(2,1)S(1)} %copy-done.1, bf16[1024,1024]{1,0:T(8,128)(2,1)S(1)} %copy-done, ...), custom_call_target="tpu_custom_call" | custom-call | flops 8192000000 | bytes 8388608 | tf_op jit(solution)/shard_map/memory_pass/pallas_call | solution.py:344
  26.7 1.3 %collective-permute-start.3 = (bf16[4,128,128]{2,1,0:T(8,128)(2,1)S(1)}, bf16[4,128,128]{2,1,0:T(8,128)(2,1)S(1)}, u32[]{:S(2)}, u32[]{:S(2)}) collective-permute-start(bf16[4,128,128]{2,1,0:T(8,128)(2,1)S(1)} %convert_element_type.21), channel_id=1, source_target_pairs={{0,4},{1,5},{2,6},{3,7},{16,20},{17,21},{18,22},{19,23}} | collective-permute-start | bytes 393224 | tf_op jit(solution)/shard_map/ppermute | solution.py:536
  28.0 0.0 collective-permute-done.1
  28.0 0.2 fusion
  28.2 0.7 %collective-permute-start.2 = (bf16[4,128,128]{2,1,0:T(8,128)(2,1)S(1)}, bf16[4,128,128]{2,1,0:T(8,128)(2,1)S(1)}, u32[]{:S(2)}, u32[]{:S(2)}) collective-permute-start(bf16[4,128,128]{2,1,0:T(8,128)(2,1)S(1)} %fusion), channel_id=1, source_target_pairs={{4,8},{5,9},{6,10},{7,11},{20,24},{21,25},{22,26},{23,27}} | collective-permute-start | bytes 393224 | tf_op jit(solution)/shard_map/ppermute | solution.py:536
  28.9 0.0 copy-done.2
  28.9 0.0 copy-done.8
  28.9 4.4 %rows_pass.2 = (bf16[1024,512]{1,0:T(8,128)(2,1)S(1)}, bf16[1024,512]{1,0:T(8,128)(2,1)S(1)}) custom-call(bf16[1024,512]{1,0:T(8,128)(2,1)S(1)} %copy-done.2, bf16[16,512]{1,0:T(8,128)(2,1)S(1)} %collective-permute-done.refs_2_.refs_1_, bf16[4,512]{1,0:T(4,128)(2,1)S(1)} %copy-done.8, bf16[1024,256]{1,0:T(8,128)(2,1)S(1)} %get-tuple-element.30.refs_3_, ...), custom_call_target="tpu_custom_call" | custom-call | flops 4096000000 | bytes 8388608 | tf_op jit(solution)/shard_map/rows_pass/pallas_call | solution.py:451
  33.4 0.0 collective-permute-done.3
  33.4 0.2 fusion.2
  33.6 0.7 %collective-permute-start.4 = (bf16[4,128,128]{2,1,0:T(8,128)(2,1)S(1)}, bf16[4,128,128]{2,1,0:T(8,128)(2,1)S(1)}, u32[]{:S(2)}, u32[]{:S(2)}) collective-permute-start(bf16[4,128,128]{2,1,0:T(8,128)(2,1)S(1)} %fusion.2), channel_id=1, source_target_pairs={{4,8},{5,9},{6,10},{7,11},{20,24},{21,25},{22,26},{23,27}} | collective-permute-start | bytes 393224 | tf_op jit(solution)/shard_map/ppermute | solution.py:536
  34.2 0.0 collective-permute-done.2
  34.2 0.2 fusion.1
  34.4 0.7 %collective-permute-start.6 = (bf16[4,128,128]{2,1,0:T(8,128)(2,1)S(1)}, bf16[4,128,128]{2,1,0:T(8,128)(2,1)S(1)}, u32[]{:S(2)}, u32[]{:S(2)}) collective-permute-start(bf16[4,128,128]{2,1,0:T(8,128)(2,1)S(1)} %fusion.1), channel_id=1, source_target_pairs={{8,12},{9,13},{10,14},{11,15},{24,28},{25,29},{26,30},{27,31}} | collective-permute-start | bytes 393224 | tf_op jit(solution)/shard_map/ppermute | solution.py:536
  35.1 0.0 copy-start.3
  35.1 4.4 %rows_pass.3 = (bf16[1024,512]{1,0:T(8,128)(2,1)S(1)}, bf16[1024,512]{1,0:T(8,128)(2,1)S(1)}) custom-call(bf16[1024,512]{1,0:T(8,128)(2,1)S(1)} %copy-done.2, bf16[16,512]{1,0:T(8,128)(2,1)S(1)} %collective-permute-done.refs_2_.refs_1_, bf16[4,512]{1,0:T(4,128)(2,1)S(1)} %copy-done.8, bf16[1024,256]{1,0:T(8,128)(2,1)S(1)} %get-tuple-element.24.refs_3_, ...), custom_call_target="tpu_custom_call" | custom-call | flops 4096000000 | bytes 8388608 | tf_op jit(solution)/shard_map/rows_pass/pallas_call | solution.py:451
  39.6 0.0 collective-permute-done.4
  39.6 0.2 fusion.3
  39.8 0.7 %collective-permute-start.5 = (bf16[4,128,128]{2,1,0:T(8,128)(2,1)S(1)}, bf16[4,128,128]{2,1,0:T(8,128)(2,1)S(1)}, u32[]{:S(2)}, u32[]{:S(2)}) collective-permute-start(bf16[4,128,128]{2,1,0:T(8,128)(2,1)S(1)} %fusion.3), channel_id=1, source_target_pairs={{8,12},{9,13},{10,14},{11,15},{24,28},{25,29},{26,30},{27,31}} | collective-permute-start | bytes 393224 | tf_op jit(solution)/shard_map/ppermute | solution.py:536
  40.5 0.0 collective-permute-done.6.refs_3_
  40.5 0.0 copy-done.3
  40.6 1.9 %final_pass.2.refs_5_ = bf16[1024,1024]{1,0:T(8,128)(2,1)} custom-call(bf16[1024,512]{1,0:T(8,128)(2,1)S(1)} %get-tuple-element.41.refs_0_, bf16[1024,512]{1,0:T(8,128)(2,1)S(1)} %get-tuple-element.34.refs_1_, bf16[4,128,128]{2,1,0:T(8,128)(2,1)S(1)} %add.23.refs_2_, bf16[4,128,128]{2,1,0:T(8,128)(2,1)S(1)} %collective-permute-done.6.refs_3_, ...), custom_call_target="tpu_custom_call" | custom-call | tf_op jit(solution)/shard_map/final_pass/pallas_call | solution.py:502
  42.5 0.0 collective-permute-done.5.refs_3_
  42.5 1.9 %final_pass.3 = bf16[1024,1024]{1,0:T(8,128)(2,1)} custom-call(bf16[1024,512]{1,0:T(8,128)(2,1)S(1)} %get-tuple-element.38.refs_0_, bf16[1024,512]{1,0:T(8,128)(2,1)S(1)} %get-tuple-element.39.refs_1_, bf16[4,128,128]{2,1,0:T(8,128)(2,1)S(1)} %add.21.refs_2_, ...), custom_call_target="tpu_custom_call", output_to_operand_aliasing={{}: (5, {})} | custom-call | tf_op jit(solution)/shard_map/final_pass/pallas_call | solution.py:502
  (4 shorter events, 0.1 us)
Async XLA Ops:
  0.0 8.2 %copy-start = (bf16[1024,1024]{1,0:T(8,128)(2,1)S(1)}, bf16[1024,1024]{1,0:T(8,128)(2,1)}, u32[]{:S(2)}) copy-start(bf16[1024,1024]{1,0:T(8,128)(2,1)} %refs_1_.3) | copy-start | bytes 6291460
  0.0 8.2 %copy-start.1 = (bf16[1024,512]{1,0:T(8,128)(2,1)S(1)}, bf16[1024,512]{1,0:T(8,128)(2,1)}, u32[]{:S(2)}) copy-start(bf16[1024,512]{1,0:T(8,128)(2,1)} %refs_0_.5) | copy-start | bytes 3145732
  0.0 8.2 %copy-start.6 = (bf16[4,1024]{1,0:T(4,128)(2,1)S(1)}, bf16[4,1024]{1,0:T(4,128)(2,1)}, u32[]{:S(2)}) copy-start(bf16[4,1024]{1,0:T(4,128)(2,1)} %refs_4_.3) | copy-start | bytes 24580
  0.0 8.2 %copy-start.7 = (bf16[4,512]{1,0:T(4,128)(2,1)S(1)}, bf16[4,512]{1,0:T(4,128)(2,1)}, u32[]{:S(2)}) copy-start(bf16[4,512]{1,0:T(4,128)(2,1)} %refs_3_.3) | copy-start | bytes 12292
  0.0 8.2 %copy-start.5 = (f32[1024,8]{0,1:T(8,128)S(1)}, f32[1024,8]{0,1:T(8,128)}, u32[]{:S(2)}) copy-start(f32[1024,8]{0,1:T(8,128)} %param.16) | copy-start | bytes 98308
  0.0 8.2 %copy-start.4 = (f32[1024,8]{0,1:T(8,128)S(1)}, f32[1024,8]{0,1:T(8,128)}, u32[]{:S(2)}) copy-start(f32[1024,8]{0,1:T(8,128)} %param.15) | copy-start | bytes 98308
  1.6 6.6 %collective-permute-start = (bf16[16,512]{1,0:T(8,128)(2,1)}, bf16[16,512]{1,0:T(8,128)(2,1)S(1)}, u32[]{:S(2)}, u32[]{:S(2)}) collective-permute-start(bf16[16,512]{1,0:T(8,128)(2,1)} %pack_rim.1), channel_id=1, source_target_pairs={{0,4},{4,8},{8,12},{1,5},{5,9},{9,13},{2,6},{6,10},{10,14},{3,7},{... | collective-permute-start | bytes 49160 | tf_op jit(solution)/shard_map/ppermute | solution.py:518
  15.2 13.7 %copy-start.2 = (bf16[1024,512]{1,0:T(8,128)(2,1)S(1)}, bf16[1024,512]{1,0:T(8,128)(2,1)}, u32[]{:S(2)}) copy-start(bf16[1024,512]{1,0:T(8,128)(2,1)} %refs_0_.7) | copy-start | bytes 3145732
  15.2 13.7 %copy-start.8 = (bf16[4,512]{1,0:T(4,128)(2,1)S(1)}, bf16[4,512]{1,0:T(4,128)(2,1)}, u32[]{:S(2)}) copy-start(bf16[4,512]{1,0:T(4,128)(2,1)} %refs_2_.3) | copy-start | bytes 12292
  15.2 12.8 %collective-permute-start.1 = (bf16[4,128,128]{2,1,0:T(8,128)(2,1)S(1)}, bf16[4,128,128]{2,1,0:T(8,128)(2,1)S(1)}, u32[]{:S(2)}, u32[]{:S(2)}) collective-permute-start(bf16[4,128,128]{2,1,0:T(8,128)(2,1)S(1)} %convert_element_type.18), channel_id=1, source_target_pairs={{0,4},{1,5},{2,6},{3,7},{16,20},{17,21},{18,22},{19,23}} | collective-permute-start | bytes 393224 | tf_op jit(solution)/shard_map/ppermute | solution.py:536
  26.7 6.7 %collective-permute-start.3 = (bf16[4,128,128]{2,1,0:T(8,128)(2,1)S(1)}, bf16[4,128,128]{2,1,0:T(8,128)(2,1)S(1)}, u32[]{:S(2)}, u32[]{:S(2)}) collective-permute-start(bf16[4,128,128]{2,1,0:T(8,128)(2,1)S(1)} %convert_element_type.21), channel_id=1, source_target_pairs={{0,4},{1,5},{2,6},{3,7},{16,20},{17,21},{18,22},{19,23}} | collective-permute-start | bytes 393224 | tf_op jit(solution)/shard_map/ppermute | solution.py:536
  28.2 6.0 %collective-permute-start.2 = (bf16[4,128,128]{2,1,0:T(8,128)(2,1)S(1)}, bf16[4,128,128]{2,1,0:T(8,128)(2,1)S(1)}, u32[]{:S(2)}, u32[]{:S(2)}) collective-permute-start(bf16[4,128,128]{2,1,0:T(8,128)(2,1)S(1)} %fusion), channel_id=1, source_target_pairs={{4,8},{5,9},{6,10},{7,11},{20,24},{21,25},{22,26},{23,27}} | collective-permute-start | bytes 393224 | tf_op jit(solution)/shard_map/ppermute | solution.py:536
  33.6 6.0 %collective-permute-start.4 = (bf16[4,128,128]{2,1,0:T(8,128)(2,1)S(1)}, bf16[4,128,128]{2,1,0:T(8,128)(2,1)S(1)}, u32[]{:S(2)}, u32[]{:S(2)}) collective-permute-start(bf16[4,128,128]{2,1,0:T(8,128)(2,1)S(1)} %fusion.2), channel_id=1, source_target_pairs={{4,8},{5,9},{6,10},{7,11},{20,24},{21,25},{22,26},{23,27}} | collective-permute-start | bytes 393224 | tf_op jit(solution)/shard_map/ppermute | solution.py:536
  34.4 6.1 %collective-permute-start.6 = (bf16[4,128,128]{2,1,0:T(8,128)(2,1)S(1)}, bf16[4,128,128]{2,1,0:T(8,128)(2,1)S(1)}, u32[]{:S(2)}, u32[]{:S(2)}) collective-permute-start(bf16[4,128,128]{2,1,0:T(8,128)(2,1)S(1)} %fusion.1), channel_id=1, source_target_pairs={{8,12},{9,13},{10,14},{11,15},{24,28},{25,29},{26,30},{27,31}} | collective-permute-start | bytes 393224 | tf_op jit(solution)/shard_map/ppermute | solution.py:536
  35.1 5.4 %copy-start.3 = (f32[128]{0:T(128)S(1)}, f32[128]{0:T(128)}, u32[]{:S(2)}) copy-start(f32[128]{0:T(128)} %param.17) | copy-start | bytes 1540
  39.8 2.7 %collective-permute-start.5 = (bf16[4,128,128]{2,1,0:T(8,128)(2,1)S(1)}, bf16[4,128,128]{2,1,0:T(8,128)(2,1)S(1)}, u32[]{:S(2)}, u32[]{:S(2)}) collective-permute-start(bf16[4,128,128]{2,1,0:T(8,128)(2,1)S(1)} %fusion.3), channel_id=1, source_target_pairs={{8,12},{9,13},{10,14},{11,15},{24,28},{25,29},{26,30},{27,31}} | collective-permute-start | bytes 393224 | tf_op jit(solution)/shard_map/ppermute | solution.py:536

commit v9 on v8

--- a/solution.py
+++ b/solution.py
@@ -16,7 +16,7 @@
 FOLD = 4
 PARTS = 2
 SPAN_X = 1024
-SPAN_Y = 512
+SPAN_Y = 1024
 EPSILON = 1e-06
 LOG2E = 1.4426950408889634
 F32 = jnp.float32
@@ -457,7 +457,7 @@
             jax.ShapeDtypeStruct((tok_count, vheads * DV), BF16),
         ],
         scratch_shapes=[pltpu.VMEM((kheads, span + HALO, 128), F32)],
-        compiler_params=pltpu.CompilerParams(vmem_limit_bytes=16 * 1024 * 1024),
+        compiler_params=pltpu.CompilerParams(vmem_limit_bytes=24 * 1024 * 1024),
         cost_estimate=pl.CostEstimate(
             flops=2 * tok_count * vheads * 1000 * 500, bytes_accessed=1 << 23, transcendentals=0
         ),

time: 44.6 us -> 43.9 us (0.984)
  Pallas kernels: 28.2 us -> 27.3 us
    pallas_call x2, Pallas kernels: 8.89 us -> 7.96 us  [rows_pass(): pl.pallas_call(kernel, in_specs=[VMEM] * 8, out_specs=[VMEM] * 2, out_sha...]
  transfers between devices with their start and end apart: 7 -> 7, of which waited for: 1 -> 1; matrix products, arithmetic and copies ran while one was open for 2% -> 2% of each run, Pallas kernels for 40% -> 39%
where the time goes in v9:
time: 43.9 us; the launch traced here: 43.7 us
  Pallas kernels  27.3 us (62%)
  starting transfers between devices  13.7 us (31%)
  waiting for transfers between devices  1.65 us (4%)
  matrix products  0.71 us (2%)
    pallas_call x2, Pallas kernels, memory_pass(): pl.pallas_call(kernel, in_specs=[VMEM] * 7, out_specs=[VMEM] * 5, out_sha...  13.9 us
    ppermute x6, starting transfers between devices, send(): lax.ppermute(moved[part][source], 'ctx', [(source, source + 1)])  8.72 us
    pallas_call x2, Pallas kernels, rows_pass(): pl.pallas_call(kernel, in_specs=[VMEM] * 8, out_specs=[VMEM] * 2, out_sha...  7.96 us
    ppermute x1, starting transfers between devices, shards(): lax.ppermute(pack_rim(query_raw, key_raw, value_raw), 'ctx', [(at, at + 1...  4.93 us
    pallas_call x2, Pallas kernels, final_pass(): pl.pallas_call(kernel, grid=(tok_count // span,), in_specs=specs, out_spe...  3.87 us
    ppermute x1, waiting for transfers between devices, shards(): lax.ppermute(pack_rim(query_raw, key_raw, value_raw), 'ctx', [(at, at + 1...  1.64 us
    pallas_call x1, Pallas kernels, pack_rim(): pl.pallas_call(rim_kernel, grid=(1,), in_specs=[pl.BlockSpec((RIM, width)...  1.57 us
  transfers between devices with their start and end apart: 7, of which 1 were waited for; matrix products, arithmetic and copies ran while one was open for 2% of the time, Pallas kernels for 39%

profile of v9, /device:TPU:0, one launch (start us, length us, event | category | flops | bytes accessed | tf_op | source)
XLA Modules:
  0.0 43.7 jit_solution(11644779227836757167)
XLA Ops:
  0.0 0.0 copy-start
  0.0 0.0 copy-start.1
  0.0 0.0 copy-start.6
  0.0 0.0 copy-start.7
  0.0 0.0 copy-start.5
  0.0 0.0 copy-start.4
  0.0 1.6 %pack_rim.1 = bf16[16,512]{1,0:T(8,128)(2,1)} custom-call(bf16[1024,512]{1,0:T(8,128)(2,1)} %refs_0_.7, bf16[1024,512]{1,0:T(8,128)(2,1)} %refs_0_.5, bf16[1024,1024]{1,0:T(8,128)(2,1)} %refs_1_.3), custom_call_target="tpu_custom_call" | custom-call | tf_op jit(solution)/shard_map/pack_rim/pallas_call | solution.py:172
  1.6 4.9 %collective-permute-start = (bf16[16,512]{1,0:T(8,128)(2,1)}, bf16[16,512]{1,0:T(8,128)(2,1)S(1)}, u32[]{:S(2)}, u32[]{:S(2)}) collective-permute-start(bf16[16,512]{1,0:T(8,128)(2,1)} %pack_rim.1), channel_id=1, source_target_pairs={{0,4},{4,8},{8,12},{1,5},{5,9},{9,13},{2,6},{6,10},{10,14},{3,7},{... | collective-permute-start | bytes 49160 | tf_op jit(solution)/shard_map/ppermute | solution.py:518
  6.5 1.6 %collective-permute-done.refs_2_.refs_1_ = bf16[16,512]{1,0:T(8,128)(2,1)S(1)} collective-permute-done((bf16[16,512]{1,0:T(8,128)(2,1)}, bf16[16,512]{1,0:T(8,128)(2,1)S(1)}, u32[]{:S(2)}, u32[]{:S(2)}) %collective-permute-start) | collective-permute-done | bytes 16416 | tf_op jit(solution)/shard_map/ppermute | solution.py:518
  8.2 0.0 copy-done
  8.2 0.0 copy-done.1
  8.2 0.0 copy-done.6
  8.2 0.0 copy-done.7
  8.2 0.0 copy-done.5
  8.2 0.0 copy-done.4
  8.2 6.9 %memory_pass.3 = (bf16[1024,256]{1,0:T(8,128)(2,1)S(1)}, bf16[1024,1024]{1,0:T(8,128)(2,1)S(1)}, bf16[8,4,128,256]{3,2,1,0:T(8,128)(2,1)S(1)}, bf16[4,128,128]{2,1,0:T(8,128)(2,1)S(1)}, f32[4,128,128]{2,1,0:T(8,128)S(1)}) custom-call(bf16[1024,512]{1,0:T(8,128)(2,1)S(1)} %copy-done.1, bf16[1024,1024]{1,0:T(8,128)(2,1)S(1)} %copy-done, ...), custom_call_target="tpu_custom_call" | custom-call | flops 8192000000 | bytes 8388608 | tf_op jit(solution)/shard_map/memory_pass/pallas_call | solution.py:344
  15.2 0.0 copy-start.2
  15.2 0.0 copy-start.8
  15.2 4.5 %collective-permute-start.1 = (bf16[4,128,128]{2,1,0:T(8,128)(2,1)S(1)}, bf16[4,128,128]{2,1,0:T(8,128)(2,1)S(1)}, u32[]{:S(2)}, u32[]{:S(2)}) collective-permute-start(bf16[4,128,128]{2,1,0:T(8,128)(2,1)S(1)} %convert_element_type.18), channel_id=1, source_target_pairs={{0,4},{1,5},{2,6},{3,7},{16,20},{17,21},{18,22},{19,23}} | collective-permute-start | bytes 393224 | tf_op jit(solution)/shard_map/ppermute | solution.py:536
  19.7 6.9 %memory_pass.2 = (bf16[1024,256]{1,0:T(8,128)(2,1)S(1)}, bf16[1024,1024]{1,0:T(8,128)(2,1)S(1)}, bf16[8,4,128,256]{3,2,1,0:T(8,128)(2,1)S(1)}, bf16[4,128,128]{2,1,0:T(8,128)(2,1)S(1)}, f32[4,128,128]{2,1,0:T(8,128)S(1)}) custom-call(bf16[1024,512]{1,0:T(8,128)(2,1)S(1)} %copy-done.1, bf16[1024,1024]{1,0:T(8,128)(2,1)S(1)} %copy-done, ...), custom_call_target="tpu_custom_call" | custom-call | flops 8192000000 | bytes 8388608 | tf_op jit(solution)/shard_map/memory_pass/pallas_call | solution.py:344
  26.7 1.3 %collective-permute-start.3 = (bf16[4,128,128]{2,1,0:T(8,128)(2,1)S(1)}, bf16[4,128,128]{2,1,0:T(8,128)(2,1)S(1)}, u32[]{:S(2)}, u32[]{:S(2)}) collective-permute-start(bf16[4,128,128]{2,1,0:T(8,128)(2,1)S(1)} %convert_element_type.21), channel_id=1, source_target_pairs={{0,4},{1,5},{2,6},{3,7},{16,20},{17,21},{18,22},{19,23}} | collective-permute-start | bytes 393224 | tf_op jit(solution)/shard_map/ppermute | solution.py:536
  28.0 0.0 collective-permute-done.1
  28.0 0.2 fusion
  28.2 0.7 %collective-permute-start.2 = (bf16[4,128,128]{2,1,0:T(8,128)(2,1)S(1)}, bf16[4,128,128]{2,1,0:T(8,128)(2,1)S(1)}, u32[]{:S(2)}, u32[]{:S(2)}) collective-permute-start(bf16[4,128,128]{2,1,0:T(8,128)(2,1)S(1)} %fusion), channel_id=1, source_target_pairs={{4,8},{5,9},{6,10},{7,11},{20,24},{21,25},{22,26},{23,27}} | collective-permute-start | bytes 393224 | tf_op jit(solution)/shard_map/ppermute | solution.py:536
  28.9 0.0 copy-done.2
  28.9 0.0 copy-done.8
  28.9 4.0 %rows_pass.2 = (bf16[1024,512]{1,0:T(8,128)(2,1)S(1)}, bf16[1024,512]{1,0:T(8,128)(2,1)S(1)}) custom-call(bf16[1024,512]{1,0:T(8,128)(2,1)S(1)} %copy-done.2, bf16[16,512]{1,0:T(8,128)(2,1)S(1)} %collective-permute-done.refs_2_.refs_1_, bf16[4,512]{1,0:T(4,128)(2,1)S(1)} %copy-done.8, bf16[1024,256]{1,0:T(8,128)(2,1)S(1)} %get-tuple-element.30.refs_3_, ...), custom_call_target="tpu_custom_call" | custom-call | flops 4096000000 | bytes 8388608 | tf_op jit(solution)/shard_map/rows_pass/pallas_call | solution.py:451
  32.9 0.0 collective-permute-done.3
  32.9 0.2 fusion.2
  33.1 0.7 %collective-permute-start.4 = (bf16[4,128,128]{2,1,0:T(8,128)(2,1)S(1)}, bf16[4,128,128]{2,1,0:T(8,128)(2,1)S(1)}, u32[]{:S(2)}, u32[]{:S(2)}) collective-permute-start(bf16[4,128,128]{2,1,0:T(8,128)(2,1)S(1)} %fusion.2), channel_id=1, source_target_pairs={{4,8},{5,9},{6,10},{7,11},{20,24},{21,25},{22,26},{23,27}} | collective-permute-start | bytes 393224 | tf_op jit(solution)/shard_map/ppermute | solution.py:536
  33.8 0.0 collective-permute-done.2
  33.8 0.2 fusion.1
  34.0 0.9 %collective-permute-start.6 = (bf16[4,128,128]{2,1,0:T(8,128)(2,1)S(1)}, bf16[4,128,128]{2,1,0:T(8,128)(2,1)S(1)}, u32[]{:S(2)}, u32[]{:S(2)}) collective-permute-start(bf16[4,128,128]{2,1,0:T(8,128)(2,1)S(1)} %fusion.1), channel_id=1, source_target_pairs={{8,12},{9,13},{10,14},{11,15},{24,28},{25,29},{26,30},{27,31}} | collective-permute-start | bytes 393224 | tf_op jit(solution)/shard_map/ppermute | solution.py:536
  34.9 0.0 copy-start.3
  34.9 4.0 %rows_pass.3 = (bf16[1024,512]{1,0:T(8,128)(2,1)S(1)}, bf16[1024,512]{1,0:T(8,128)(2,1)S(1)}) custom-call(bf16[1024,512]{1,0:T(8,128)(2,1)S(1)} %copy-done.2, bf16[16,512]{1,0:T(8,128)(2,1)S(1)} %collective-permute-done.refs_2_.refs_1_, bf16[4,512]{1,0:T(4,128)(2,1)S(1)} %copy-done.8, bf16[1024,256]{1,0:T(8,128)(2,1)S(1)} %get-tuple-element.24.refs_3_, ...), custom_call_target="tpu_custom_call" | custom-call | flops 4096000000 | bytes 8388608 | tf_op jit(solution)/shard_map/rows_pass/pallas_call | solution.py:451
  38.9 0.0 collective-permute-done.4
  38.9 0.2 fusion.3
  39.1 0.7 %collective-permute-start.5 = (bf16[4,128,128]{2,1,0:T(8,128)(2,1)S(1)}, bf16[4,128,128]{2,1,0:T(8,128)(2,1)S(1)}, u32[]{:S(2)}, u32[]{:S(2)}) collective-permute-start(bf16[4,128,128]{2,1,0:T(8,128)(2,1)S(1)} %fusion.3), channel_id=1, source_target_pairs={{8,12},{9,13},{10,14},{11,15},{24,28},{25,29},{26,30},{27,31}} | collective-permute-start | bytes 393224 | tf_op jit(solution)/shard_map/ppermute | solution.py:536
  39.8 0.0 collective-permute-done.6.refs_3_
  39.8 0.0 copy-done.3
  39.9 1.9 %final_pass.2.refs_5_ = bf16[1024,1024]{1,0:T(8,128)(2,1)} custom-call(bf16[1024,512]{1,0:T(8,128)(2,1)S(1)} %get-tuple-element.41.refs_0_, bf16[1024,512]{1,0:T(8,128)(2,1)S(1)} %get-tuple-element.34.refs_1_, bf16[4,128,128]{2,1,0:T(8,128)(2,1)S(1)} %add.23.refs_2_, bf16[4,128,128]{2,1,0:T(8,128)(2,1)S(1)} %collective-permute-done.6.refs_3_, ...), custom_call_target="tpu_custom_call" | custom-call | tf_op jit(solution)/shard_map/final_pass/pallas_call | solution.py:502
  41.8 0.0 collective-permute-done.5.refs_3_
  41.8 1.9 %final_pass.3 = bf16[1024,1024]{1,0:T(8,128)(2,1)} custom-call(bf16[1024,512]{1,0:T(8,128)(2,1)S(1)} %get-tuple-element.38.refs_0_, bf16[1024,512]{1,0:T(8,128)(2,1)S(1)} %get-tuple-element.39.refs_1_, bf16[4,128,128]{2,1,0:T(8,128)(2,1)S(1)} %add.21.refs_2_, ...), custom_call_target="tpu_custom_call", output_to_operand_aliasing={{}: (5, {})} | custom-call | tf_op jit(solution)/shard_map/final_pass/pallas_call | solution.py:502
  (4 shorter events, 0.1 us)
Async XLA Ops:
  0.0 8.2 %copy-start = (bf16[1024,1024]{1,0:T(8,128)(2,1)S(1)}, bf16[1024,1024]{1,0:T(8,128)(2,1)}, u32[]{:S(2)}) copy-start(bf16[1024,1024]{1,0:T(8,128)(2,1)} %refs_1_.3) | copy-start | bytes 6291460
  0.0 8.2 %copy-start.1 = (bf16[1024,512]{1,0:T(8,128)(2,1)S(1)}, bf16[1024,512]{1,0:T(8,128)(2,1)}, u32[]{:S(2)}) copy-start(bf16[1024,512]{1,0:T(8,128)(2,1)} %refs_0_.5) | copy-start | bytes 3145732
  0.0 8.2 %copy-start.6 = (bf16[4,1024]{1,0:T(4,128)(2,1)S(1)}, bf16[4,1024]{1,0:T(4,128)(2,1)}, u32[]{:S(2)}) copy-start(bf16[4,1024]{1,0:T(4,128)(2,1)} %refs_4_.3) | copy-start | bytes 24580
  0.0 8.2 %copy-start.7 = (bf16[4,512]{1,0:T(4,128)(2,1)S(1)}, bf16[4,512]{1,0:T(4,128)(2,1)}, u32[]{:S(2)}) copy-start(bf16[4,512]{1,0:T(4,128)(2,1)} %refs_3_.3) | copy-start | bytes 12292
  0.0 8.2 %copy-start.5 = (f32[1024,8]{0,1:T(8,128)S(1)}, f32[1024,8]{0,1:T(8,128)}, u32[]{:S(2)}) copy-start(f32[1024,8]{0,1:T(8,128)} %param.16) | copy-start | bytes 98308
  0.0 8.2 %copy-start.4 = (f32[1024,8]{0,1:T(8,128)S(1)}, f32[1024,8]{0,1:T(8,128)}, u32[]{:S(2)}) copy-start(f32[1024,8]{0,1:T(8,128)} %param.15) | copy-start | bytes 98308
  1.6 6.6 %collective-permute-start = (bf16[16,512]{1,0:T(8,128)(2,1)}, bf16[16,512]{1,0:T(8,128)(2,1)S(1)}, u32[]{:S(2)}, u32[]{:S(2)}) collective-permute-start(bf16[16,512]{1,0:T(8,128)(2,1)} %pack_rim.1), channel_id=1, source_target_pairs={{0,4},{4,8},{8,12},{1,5},{5,9},{9,13},{2,6},{6,10},{10,14},{3,7},{... | collective-permute-start | bytes 49160 | tf_op jit(solution)/shard_map/ppermute | solution.py:518
  15.2 13.7 %copy-start.2 = (bf16[1024,512]{1,0:T(8,128)(2,1)S(1)}, bf16[1024,512]{1,0:T(8,128)(2,1)}, u32[]{:S(2)}) copy-start(bf16[1024,512]{1,0:T(8,128)(2,1)} %refs_0_.7) | copy-start | bytes 3145732
  15.2 13.7 %copy-start.8 = (bf16[4,512]{1,0:T(4,128)(2,1)S(1)}, bf16[4,512]{1,0:T(4,128)(2,1)}, u32[]{:S(2)}) copy-start(bf16[4,512]{1,0:T(4,128)(2,1)} %refs_2_.3) | copy-start | bytes 12292
  15.2 12.8 %collective-permute-start.1 = (bf16[4,128,128]{2,1,0:T(8,128)(2,1)S(1)}, bf16[4,128,128]{2,1,0:T(8,128)(2,1)S(1)}, u32[]{:S(2)}, u32[]{:S(2)}) collective-permute-start(bf16[4,128,128]{2,1,0:T(8,128)(2,1)S(1)} %convert_element_type.18), channel_id=1, source_target_pairs={{0,4},{1,5},{2,6},{3,7},{16,20},{17,21},{18,22},{19,23}} | collective-permute-start | bytes 393224 | tf_op jit(solution)/shard_map/ppermute | solution.py:536
  26.7 6.2 %collective-permute-start.3 = (bf16[4,128,128]{2,1,0:T(8,128)(2,1)S(1)}, bf16[4,128,128]{2,1,0:T(8,128)(2,1)S(1)}, u32[]{:S(2)}, u32[]{:S(2)}) collective-permute-start(bf16[4,128,128]{2,1,0:T(8,128)(2,1)S(1)} %convert_element_type.21), channel_id=1, source_target_pairs={{0,4},{1,5},{2,6},{3,7},{16,20},{17,21},{18,22},{19,23}} | collective-permute-start | bytes 393224 | tf_op jit(solution)/shard_map/ppermute | solution.py:536
  28.2 5.6 %collective-permute-start.2 = (bf16[4,128,128]{2,1,0:T(8,128)(2,1)S(1)}, bf16[4,128,128]{2,1,0:T(8,128)(2,1)S(1)}, u32[]{:S(2)}, u32[]{:S(2)}) collective-permute-start(bf16[4,128,128]{2,1,0:T(8,128)(2,1)S(1)} %fusion), channel_id=1, source_target_pairs={{4,8},{5,9},{6,10},{7,11},{20,24},{21,25},{22,26},{23,27}} | collective-permute-start | bytes 393224 | tf_op jit(solution)/shard_map/ppermute | solution.py:536
  33.1 5.8 %collective-permute-start.4 = (bf16[4,128,128]{2,1,0:T(8,128)(2,1)S(1)}, bf16[4,128,128]{2,1,0:T(8,128)(2,1)S(1)}, u32[]{:S(2)}, u32[]{:S(2)}) collective-permute-start(bf16[4,128,128]{2,1,0:T(8,128)(2,1)S(1)} %fusion.2), channel_id=1, source_target_pairs={{4,8},{5,9},{6,10},{7,11},{20,24},{21,25},{22,26},{23,27}} | collective-permute-start | bytes 393224 | tf_op jit(solution)/shard_map/ppermute | solution.py:536
  34.0 5.9 %collective-permute-start.6 = (bf16[4,128,128]{2,1,0:T(8,128)(2,1)S(1)}, bf16[4,128,128]{2,1,0:T(8,128)(2,1)S(1)}, u32[]{:S(2)}, u32[]{:S(2)}) collective-permute-start(bf16[4,128,128]{2,1,0:T(8,128)(2,1)S(1)} %fusion.1), channel_id=1, source_target_pairs={{8,12},{9,13},{10,14},{11,15},{24,28},{25,29},{26,30},{27,31}} | collective-permute-start | bytes 393224 | tf_op jit(solution)/shard_map/ppermute | solution.py:536
  34.9 5.0 %copy-start.3 = (f32[128]{0:T(128)S(1)}, f32[128]{0:T(128)}, u32[]{:S(2)}) copy-start(f32[128]{0:T(128)} %param.17) | copy-start | bytes 1540
  39.1 2.7 %collective-permute-start.5 = (bf16[4,128,128]{2,1,0:T(8,128)(2,1)S(1)}, bf16[4,128,128]{2,1,0:T(8,128)(2,1)S(1)}, u32[]{:S(2)}, u32[]{:S(2)}) collective-permute-start(bf16[4,128,128]{2,1,0:T(8,128)(2,1)S(1)} %fusion.3), channel_id=1, source_target_pairs={{8,12},{9,13},{10,14},{11,15},{24,28},{25,29},{26,30},{27,31}} | collective-permute-start | bytes 393224 | tf_op jit(solution)/shard_map/ppermute | solution.py:536

commit v10 on v9

--- a/solution.py
+++ b/solution.py
@@ -486,7 +486,7 @@
 def final_pass(part, rows, local, early, late, gain, earlier):
     tok_count = rows.shape[0]
     vheads = early.shape[0]
-    span = min(512, tok_count)
+    span = min(1024, tok_count)
 
     def along(width, column):
         return pl.BlockSpec((span, width), lambda i: (i, column))
@@ -506,7 +506,7 @@
         out_specs=along(vheads * DV, part),
         out_shape=jax.ShapeDtypeStruct((tok_count, PARTS * vheads * DV), BF16),
         input_output_aliases={} if earlier is None else {5: 0},
-        compiler_params=pltpu.CompilerParams(vmem_limit_bytes=12 * 1024 * 1024),
+        compiler_params=pltpu.CompilerParams(vmem_limit_bytes=16 * 1024 * 1024),
         name="final_pass",
     )(*arrays)
 

time: 43.9 us -> 43.8 us (level)
  transfers between devices with their start and end apart: 7 -> 7, of which waited for: 1 -> 1; matrix products, arithmetic and copies ran while one was open for 2% -> 2% of each run, Pallas kernels for 39% -> 38%
where the time goes in v10:
time: 43.8 us; the launch traced here: 43.6 us
  Pallas kernels  27.1 us (62%)
  starting transfers between devices  13.7 us (31%)
  waiting for transfers between devices  1.65 us (4%)
  matrix products  0.71 us (2%)
    pallas_call x2, Pallas kernels, memory_pass(): pl.pallas_call(kernel, in_specs=[VMEM] * 7, out_specs=[VMEM] * 5, out_sha...  13.9 us
    ppermute x6, starting transfers between devices, send(): lax.ppermute(moved[part][source], 'ctx', [(source, source + 1)])  8.72 us
    pallas_call x2, Pallas kernels, rows_pass(): pl.pallas_call(kernel, in_specs=[VMEM] * 8, out_specs=[VMEM] * 2, out_sha...  7.96 us
    ppermute x1, starting transfers between devices, shards(): lax.ppermute(pack_rim(query_raw, key_raw, value_raw), 'ctx', [(at, at + 1...  4.93 us
    pallas_call x2, Pallas kernels, final_pass(): pl.pallas_call(kernel, grid=(tok_count // span,), in_specs=specs, out_spe...  3.7 us
    ppermute x1, waiting for transfers between devices, shards(): lax.ppermute(pack_rim(query_raw, key_raw, value_raw), 'ctx', [(at, at + 1...  1.64 us
    pallas_call x1, Pallas kernels, pack_rim(): pl.pallas_call(rim_kernel, grid=(1,), in_specs=[pl.BlockSpec((RIM, width)...  1.57 us
  transfers between devices with their start and end apart: 7, of which 1 were waited for; matrix products, arithmetic and copies ran while one was open for 2% of the time, Pallas kernels for 38%

profile of v10, /device:TPU:0, one launch (start us, length us, event | category | flops | bytes accessed | tf_op | source)
XLA Modules:
  0.0 43.6 jit_solution(17134652876566789547)
XLA Ops:
  0.0 0.0 copy-start
  0.0 0.0 copy-start.1
  0.0 0.0 copy-start.6
  0.0 0.0 copy-start.7
  0.0 0.0 copy-start.5
  0.0 0.0 copy-start.4
  0.0 1.6 %pack_rim.1 = bf16[16,512]{1,0:T(8,128)(2,1)} custom-call(bf16[1024,512]{1,0:T(8,128)(2,1)} %refs_0_.7, bf16[1024,512]{1,0:T(8,128)(2,1)} %refs_0_.5, bf16[1024,1024]{1,0:T(8,128)(2,1)} %refs_1_.3), custom_call_target="tpu_custom_call" | custom-call | tf_op jit(solution)/shard_map/pack_rim/pallas_call | solution.py:172
  1.6 4.9 %collective-permute-start = (bf16[16,512]{1,0:T(8,128)(2,1)}, bf16[16,512]{1,0:T(8,128)(2,1)S(1)}, u32[]{:S(2)}, u32[]{:S(2)}) collective-permute-start(bf16[16,512]{1,0:T(8,128)(2,1)} %pack_rim.1), channel_id=1, source_target_pairs={{0,4},{4,8},{8,12},{1,5},{5,9},{9,13},{2,6},{6,10},{10,14},{3,7},{... | collective-permute-start | bytes 49160 | tf_op jit(solution)/shard_map/ppermute | solution.py:518
  6.5 1.6 %collective-permute-done.refs_2_.refs_1_ = bf16[16,512]{1,0:T(8,128)(2,1)S(1)} collective-permute-done((bf16[16,512]{1,0:T(8,128)(2,1)}, bf16[16,512]{1,0:T(8,128)(2,1)S(1)}, u32[]{:S(2)}, u32[]{:S(2)}) %collective-permute-start) | collective-permute-done | bytes 16416 | tf_op jit(solution)/shard_map/ppermute | solution.py:518
  8.2 0.0 copy-done
  8.2 0.0 copy-done.1
  8.2 0.0 copy-done.6
  8.2 0.0 copy-done.7
  8.2 0.0 copy-done.5
  8.2 0.0 copy-done.4
  8.2 6.9 %memory_pass.3 = (bf16[1024,256]{1,0:T(8,128)(2,1)S(1)}, bf16[1024,1024]{1,0:T(8,128)(2,1)S(1)}, bf16[8,4,128,256]{3,2,1,0:T(8,128)(2,1)S(1)}, bf16[4,128,128]{2,1,0:T(8,128)(2,1)S(1)}, f32[4,128,128]{2,1,0:T(8,128)S(1)}) custom-call(bf16[1024,512]{1,0:T(8,128)(2,1)S(1)} %copy-done.1, bf16[1024,1024]{1,0:T(8,128)(2,1)S(1)} %copy-done, ...), custom_call_target="tpu_custom_call" | custom-call | flops 8192000000 | bytes 8388608 | tf_op jit(solution)/shard_map/memory_pass/pallas_call | solution.py:344
  15.2 0.0 copy-start.2
  15.2 0.0 copy-start.8
  15.2 4.5 %collective-permute-start.1 = (bf16[4,128,128]{2,1,0:T(8,128)(2,1)S(1)}, bf16[4,128,128]{2,1,0:T(8,128)(2,1)S(1)}, u32[]{:S(2)}, u32[]{:S(2)}) collective-permute-start(bf16[4,128,128]{2,1,0:T(8,128)(2,1)S(1)} %convert_element_type.18), channel_id=1, source_target_pairs={{0,4},{1,5},{2,6},{3,7},{16,20},{17,21},{18,22},{19,23}} | collective-permute-start | bytes 393224 | tf_op jit(solution)/shard_map/ppermute | solution.py:536
  19.7 6.9 %memory_pass.2 = (bf16[1024,256]{1,0:T(8,128)(2,1)S(1)}, bf16[1024,1024]{1,0:T(8,128)(2,1)S(1)}, bf16[8,4,128,256]{3,2,1,0:T(8,128)(2,1)S(1)}, bf16[4,128,128]{2,1,0:T(8,128)(2,1)S(1)}, f32[4,128,128]{2,1,0:T(8,128)S(1)}) custom-call(bf16[1024,512]{1,0:T(8,128)(2,1)S(1)} %copy-done.1, bf16[1024,1024]{1,0:T(8,128)(2,1)S(1)} %copy-done, ...), custom_call_target="tpu_custom_call" | custom-call | flops 8192000000 | bytes 8388608 | tf_op jit(solution)/shard_map/memory_pass/pallas_call | solution.py:344
  26.7 1.3 %collective-permute-start.3 = (bf16[4,128,128]{2,1,0:T(8,128)(2,1)S(1)}, bf16[4,128,128]{2,1,0:T(8,128)(2,1)S(1)}, u32[]{:S(2)}, u32[]{:S(2)}) collective-permute-start(bf16[4,128,128]{2,1,0:T(8,128)(2,1)S(1)} %convert_element_type.21), channel_id=1, source_target_pairs={{0,4},{1,5},{2,6},{3,7},{16,20},{17,21},{18,22},{19,23}} | collective-permute-start | bytes 393224 | tf_op jit(solution)/shard_map/ppermute | solution.py:536
  28.0 0.0 collective-permute-done.1
  28.0 0.2 fusion
  28.2 0.7 %collective-permute-start.2 = (bf16[4,128,128]{2,1,0:T(8,128)(2,1)S(1)}, bf16[4,128,128]{2,1,0:T(8,128)(2,1)S(1)}, u32[]{:S(2)}, u32[]{:S(2)}) collective-permute-start(bf16[4,128,128]{2,1,0:T(8,128)(2,1)S(1)} %fusion), channel_id=1, source_target_pairs={{4,8},{5,9},{6,10},{7,11},{20,24},{21,25},{22,26},{23,27}} | collective-permute-start | bytes 393224 | tf_op jit(solution)/shard_map/ppermute | solution.py:536
  28.9 0.0 copy-done.2
  28.9 0.0 copy-done.8
  28.9 4.0 %rows_pass.2 = (bf16[1024,512]{1,0:T(8,128)(2,1)S(1)}, bf16[1024,512]{1,0:T(8,128)(2,1)S(1)}) custom-call(bf16[1024,512]{1,0:T(8,128)(2,1)S(1)} %copy-done.2, bf16[16,512]{1,0:T(8,128)(2,1)S(1)} %collective-permute-done.refs_2_.refs_1_, bf16[4,512]{1,0:T(4,128)(2,1)S(1)} %copy-done.8, bf16[1024,256]{1,0:T(8,128)(2,1)S(1)} %get-tuple-element.30.refs_3_, ...), custom_call_target="tpu_custom_call" | custom-call | flops 4096000000 | bytes 8388608 | tf_op jit(solution)/shard_map/rows_pass/pallas_call | solution.py:451
  32.9 0.0 collective-permute-done.3
  32.9 0.2 fusion.2
  33.1 0.7 %collective-permute-start.4 = (bf16[4,128,128]{2,1,0:T(8,128)(2,1)S(1)}, bf16[4,128,128]{2,1,0:T(8,128)(2,1)S(1)}, u32[]{:S(2)}, u32[]{:S(2)}) collective-permute-start(bf16[4,128,128]{2,1,0:T(8,128)(2,1)S(1)} %fusion.2), channel_id=1, source_target_pairs={{4,8},{5,9},{6,10},{7,11},{20,24},{21,25},{22,26},{23,27}} | collective-permute-start | bytes 393224 | tf_op jit(solution)/shard_map/ppermute | solution.py:536
  33.8 0.0 collective-permute-done.2
  33.8 0.2 fusion.1
  34.0 0.9 %collective-permute-start.6 = (bf16[4,128,128]{2,1,0:T(8,128)(2,1)S(1)}, bf16[4,128,128]{2,1,0:T(8,128)(2,1)S(1)}, u32[]{:S(2)}, u32[]{:S(2)}) collective-permute-start(bf16[4,128,128]{2,1,0:T(8,128)(2,1)S(1)} %fusion.1), channel_id=1, source_target_pairs={{8,12},{9,13},{10,14},{11,15},{24,28},{25,29},{26,30},{27,31}} | collective-permute-start | bytes 393224 | tf_op jit(solution)/shard_map/ppermute | solution.py:536
  34.9 0.0 copy-start.3
  34.9 4.0 %rows_pass.3 = (bf16[1024,512]{1,0:T(8,128)(2,1)S(1)}, bf16[1024,512]{1,0:T(8,128)(2,1)S(1)}) custom-call(bf16[1024,512]{1,0:T(8,128)(2,1)S(1)} %copy-done.2, bf16[16,512]{1,0:T(8,128)(2,1)S(1)} %collective-permute-done.refs_2_.refs_1_, bf16[4,512]{1,0:T(4,128)(2,1)S(1)} %copy-done.8, bf16[1024,256]{1,0:T(8,128)(2,1)S(1)} %get-tuple-element.24.refs_3_, ...), custom_call_target="tpu_custom_call" | custom-call | flops 4096000000 | bytes 8388608 | tf_op jit(solution)/shard_map/rows_pass/pallas_call | solution.py:451
  38.9 0.0 collective-permute-done.4
  38.9 0.2 fusion.3
  39.1 0.7 %collective-permute-start.5 = (bf16[4,128,128]{2,1,0:T(8,128)(2,1)S(1)}, bf16[4,128,128]{2,1,0:T(8,128)(2,1)S(1)}, u32[]{:S(2)}, u32[]{:S(2)}) collective-permute-start(bf16[4,128,128]{2,1,0:T(8,128)(2,1)S(1)} %fusion.3), channel_id=1, source_target_pairs={{8,12},{9,13},{10,14},{11,15},{24,28},{25,29},{26,30},{27,31}} | collective-permute-start | bytes 393224 | tf_op jit(solution)/shard_map/ppermute | solution.py:536
  39.8 0.0 collective-permute-done.6.refs_3_
  39.8 0.0 copy-done.3
  39.9 1.9 %final_pass.2.refs_5_ = bf16[1024,1024]{1,0:T(8,128)(2,1)} custom-call(bf16[1024,512]{1,0:T(8,128)(2,1)S(1)} %get-tuple-element.41.refs_0_, bf16[1024,512]{1,0:T(8,128)(2,1)S(1)} %get-tuple-element.34.refs_1_, bf16[4,128,128]{2,1,0:T(8,128)(2,1)S(1)} %add.23.refs_2_, bf16[4,128,128]{2,1,0:T(8,128)(2,1)S(1)} %collective-permute-done.6.refs_3_, ...), custom_call_target="tpu_custom_call" | custom-call | tf_op jit(solution)/shard_map/final_pass/pallas_call | solution.py:502
  41.7 0.0 collective-permute-done.5.refs_3_
  41.7 1.9 %final_pass.3 = bf16[1024,1024]{1,0:T(8,128)(2,1)} custom-call(bf16[1024,512]{1,0:T(8,128)(2,1)S(1)} %get-tuple-element.38.refs_0_, bf16[1024,512]{1,0:T(8,128)(2,1)S(1)} %get-tuple-element.39.refs_1_, bf16[4,128,128]{2,1,0:T(8,128)(2,1)S(1)} %add.21.refs_2_, ...), custom_call_target="tpu_custom_call", output_to_operand_aliasing={{}: (5, {})} | custom-call | tf_op jit(solution)/shard_map/final_pass/pallas_call | solution.py:502
  (4 shorter events, 0.1 us)
Async XLA Ops:
  0.0 8.2 %copy-start = (bf16[1024,1024]{1,0:T(8,128)(2,1)S(1)}, bf16[1024,1024]{1,0:T(8,128)(2,1)}, u32[]{:S(2)}) copy-start(bf16[1024,1024]{1,0:T(8,128)(2,1)} %refs_1_.3) | copy-start | bytes 6291460
  0.0 8.2 %copy-start.1 = (bf16[1024,512]{1,0:T(8,128)(2,1)S(1)}, bf16[1024,512]{1,0:T(8,128)(2,1)}, u32[]{:S(2)}) copy-start(bf16[1024,512]{1,0:T(8,128)(2,1)} %refs_0_.5) | copy-start | bytes 3145732
  0.0 8.2 %copy-start.6 = (bf16[4,1024]{1,0:T(4,128)(2,1)S(1)}, bf16[4,1024]{1,0:T(4,128)(2,1)}, u32[]{:S(2)}) copy-start(bf16[4,1024]{1,0:T(4,128)(2,1)} %refs_4_.3) | copy-start | bytes 24580
  0.0 8.2 %copy-start.7 = (bf16[4,512]{1,0:T(4,128)(2,1)S(1)}, bf16[4,512]{1,0:T(4,128)(2,1)}, u32[]{:S(2)}) copy-start(bf16[4,512]{1,0:T(4,128)(2,1)} %refs_3_.3) | copy-start | bytes 12292
  0.0 8.2 %copy-start.5 = (f32[1024,8]{0,1:T(8,128)S(1)}, f32[1024,8]{0,1:T(8,128)}, u32[]{:S(2)}) copy-start(f32[1024,8]{0,1:T(8,128)} %param.16) | copy-start | bytes 98308
  0.0 8.2 %copy-start.4 = (f32[1024,8]{0,1:T(8,128)S(1)}, f32[1024,8]{0,1:T(8,128)}, u32[]{:S(2)}) copy-start(f32[1024,8]{0,1:T(8,128)} %param.15) | copy-start | bytes 98308
  1.6 6.6 %collective-permute-start = (bf16[16,512]{1,0:T(8,128)(2,1)}, bf16[16,512]{1,0:T(8,128)(2,1)S(1)}, u32[]{:S(2)}, u32[]{:S(2)}) collective-permute-start(bf16[16,512]{1,0:T(8,128)(2,1)} %pack_rim.1), channel_id=1, source_target_pairs={{0,4},{4,8},{8,12},{1,5},{5,9},{9,13},{2,6},{6,10},{10,14},{3,7},{... | collective-permute-start | bytes 49160 | tf_op jit(solution)/shard_map/ppermute | solution.py:518
  15.2 13.7 %copy-start.2 = (bf16[1024,512]{1,0:T(8,128)(2,1)S(1)}, bf16[1024,512]{1,0:T(8,128)(2,1)}, u32[]{:S(2)}) copy-start(bf16[1024,512]{1,0:T(8,128)(2,1)} %refs_0_.7) | copy-start | bytes 3145732
  15.2 13.7 %copy-start.8 = (bf16[4,512]{1,0:T(4,128)(2,1)S(1)}, bf16[4,512]{1,0:T(4,128)(2,1)}, u32[]{:S(2)}) copy-start(bf16[4,512]{1,0:T(4,128)(2,1)} %refs_2_.3) | copy-start | bytes 12292
  15.2 12.8 %collective-permute-start.1 = (bf16[4,128,128]{2,1,0:T(8,128)(2,1)S(1)}, bf16[4,128,128]{2,1,0:T(8,128)(2,1)S(1)}, u32[]{:S(2)}, u32[]{:S(2)}) collective-permute-start(bf16[4,128,128]{2,1,0:T(8,128)(2,1)S(1)} %convert_element_type.18), channel_id=1, source_target_pairs={{0,4},{1,5},{2,6},{3,7},{16,20},{17,21},{18,22},{19,23}} | collective-permute-start | bytes 393224 | tf_op jit(solution)/shard_map/ppermute | solution.py:536
  26.7 6.2 %collective-permute-start.3 = (bf16[4,128,128]{2,1,0:T(8,128)(2,1)S(1)}, bf16[4,128,128]{2,1,0:T(8,128)(2,1)S(1)}, u32[]{:S(2)}, u32[]{:S(2)}) collective-permute-start(bf16[4,128,128]{2,1,0:T(8,128)(2,1)S(1)} %convert_element_type.21), channel_id=1, source_target_pairs={{0,4},{1,5},{2,6},{3,7},{16,20},{17,21},{18,22},{19,23}} | collective-permute-start | bytes 393224 | tf_op jit(solution)/shard_map/ppermute | solution.py:536
  28.2 5.6 %collective-permute-start.2 = (bf16[4,128,128]{2,1,0:T(8,128)(2,1)S(1)}, bf16[4,128,128]{2,1,0:T(8,128)(2,1)S(1)}, u32[]{:S(2)}, u32[]{:S(2)}) collective-permute-start(bf16[4,128,128]{2,1,0:T(8,128)(2,1)S(1)} %fusion), channel_id=1, source_target_pairs={{4,8},{5,9},{6,10},{7,11},{20,24},{21,25},{22,26},{23,27}} | collective-permute-start | bytes 393224 | tf_op jit(solution)/shard_map/ppermute | solution.py:536
  33.1 5.8 %collective-permute-start.4 = (bf16[4,128,128]{2,1,0:T(8,128)(2,1)S(1)}, bf16[4,128,128]{2,1,0:T(8,128)(2,1)S(1)}, u32[]{:S(2)}, u32[]{:S(2)}) collective-permute-start(bf16[4,128,128]{2,1,0:T(8,128)(2,1)S(1)} %fusion.2), channel_id=1, source_target_pairs={{4,8},{5,9},{6,10},{7,11},{20,24},{21,25},{22,26},{23,27}} | collective-permute-start | bytes 393224 | tf_op jit(solution)/shard_map/ppermute | solution.py:536
  34.0 5.9 %collective-permute-start.6 = (bf16[4,128,128]{2,1,0:T(8,128)(2,1)S(1)}, bf16[4,128,128]{2,1,0:T(8,128)(2,1)S(1)}, u32[]{:S(2)}, u32[]{:S(2)}) collective-permute-start(bf16[4,128,128]{2,1,0:T(8,128)(2,1)S(1)} %fusion.1), channel_id=1, source_target_pairs={{8,12},{9,13},{10,14},{11,15},{24,28},{25,29},{26,30},{27,31}} | collective-permute-start | bytes 393224 | tf_op jit(solution)/shard_map/ppermute | solution.py:536
  34.9 5.0 %copy-start.3 = (f32[128]{0:T(128)S(1)}, f32[128]{0:T(128)}, u32[]{:S(2)}) copy-start(f32[128]{0:T(128)} %param.17) | copy-start | bytes 1540
  39.1 2.6 %collective-permute-start.5 = (bf16[4,128,128]{2,1,0:T(8,128)(2,1)S(1)}, bf16[4,128,128]{2,1,0:T(8,128)(2,1)S(1)}, u32[]{:S(2)}, u32[]{:S(2)}) collective-permute-start(bf16[4,128,128]{2,1,0:T(8,128)(2,1)S(1)} %fusion.3), channel_id=1, source_target_pairs={{8,12},{9,13},{10,14},{11,15},{24,28},{25,29},{26,30},{27,31}} | collective-permute-start | bytes 393224 | tf_op jit(solution)/shard_map/ppermute | solution.py:536
